TPU v7x, 512 devices: a whole 4x8x8 slice. The times are simulated.
512 devices in a mesh: depth: 32 (over z, x_hi, core), tile: 16 (over x_lo, y).
Axes of the slice: x: 4 (x_hi: 2, x_lo: 2; x = x_hi * 2 + x_lo), y: 8, z: 8, core: 2. Of those that a mesh axis runs over, the one named last changes fastest.
Arguments:
- potential: float32 [32, 4096, 384], P('depth', 'tile'), may hold values from 0 to 3
- probe: bfloat16 [2, 256, 256], replicated, may hold values from -6 to 6
- positions: int32 [16, 67, 2], P('tile'), may hold values from 0 to 128
- intensity: bfloat16 [16, 4, 256, 256], P('tile'), may hold values from 0.099609375 to 3
- fwd_wave: float32 [32, 16, 2, 256, 256], P('depth', 'tile'), may hold values from -6 to 6
- adj_wave: bfloat16 [32, 16, 2, 256, 256], P('depth', 'tile'), may hold values from -6 to 6
- saved_wave: bfloat16 [32, 16, 4, 2, 256, 256], P('depth', 'tile'), may hold values from -6 to 6
Outputs:
- fwd_next: float32 [32, 16, 2, 256, 256], P('depth', 'tile')
- adj_next: bfloat16 [32, 16, 2, 256, 256], P('depth', 'tile')
- gradient: float32 [32, 4096, 384], P('depth', 'tile')
Inputs may be any that keep to these rules, and one draw needn't show every extreme that they name: `positions`: window corners keep the whole window inside the tile's extent.
All inputs are finite; a program needn't handle non-finite values.
Results may differ from a plain program's by a relative error of at most 0.04.
Values may be sent and summed in bfloat16 or wider, within the bound.
No kernel may reach another device: no remote copies, remote signals or barrier semaphores. Data moves between devices by JAX's collectives and lax.ppermute only.
A program may use at most 64 MiB of HBM per device.

v0:
```python
import math

import jax
import jax.numpy as jnp
from jax import lax
from jax.sharding import PartitionSpec as P

TICKS = 4


SIGMA = 0.8
DEFOCUS = 6.0


def shifted(block, axis, distance):
    devices = range(lax.axis_size(axis))
    route = [(i - distance, i) for i in devices if i - distance in devices]
    return lax.ppermute(block, axis, route)


def with_halo(block, sides, width):
    for axis, dim in sides:
        count = lax.axis_size(axis)
        forward = [(i, i + 1) for i in range(count - 1)]
        backward = [(target, source) for source, target in forward]
        low = lax.ppermute(
            lax.slice_in_dim(block, block.shape[dim] - width, None, axis=dim), axis, forward
        )
        high = lax.ppermute(lax.slice_in_dim(block, 0, width, axis=dim), axis, backward)
        block = jnp.concatenate([low, block, high], axis=dim)
    return block


def tables(n):
    idx = jnp.arange(n, dtype=jnp.int32)
    prod = idx[:, None] * idx[None, :] % n
    angle = prod.astype(jnp.float32) * (2.0 * math.pi / n)
    scale = 1.0 / math.sqrt(n)
    cos_t = (jnp.cos(angle) * scale).astype(jnp.bfloat16)
    sin_t = (jnp.sin(angle) * scale).astype(jnp.bfloat16)
    return (jnp.concatenate([cos_t, sin_t], 0), jnp.concatenate([cos_t, sin_t], 1))


def propagator(n):
    idx = jnp.arange(n, dtype=jnp.int32)
    freq = jnp.where(idx < n // 2, idx, idx - n).astype(jnp.float32)
    square = freq[:, None] * freq[:, None] + freq[None, :] * freq[None, :]
    phase = -math.pi * DEFOCUS * square / (n * n)
    return (jnp.cos(phase), jnp.sin(phase))


def left_sums(real, imag, tall_cols):
    left_r = jnp.dot(tall_cols, real.astype(jnp.bfloat16), preferred_element_type=jnp.float32)
    left_i = jnp.dot(tall_cols, imag.astype(jnp.bfloat16), preferred_element_type=jnp.float32)
    return (left_r, left_i)


def finish_left(left_r, left_i, sign, n):
    first_r = (left_r[:n] + sign * left_i[n:]).astype(jnp.bfloat16)
    first_i = (left_i[:n] - sign * left_r[n:]).astype(jnp.bfloat16)
    return (first_r, first_i)


def right_rows(first_r, first_i, broad, sign, n):
    right_r = jnp.dot(first_r, broad, preferred_element_type=jnp.float32)
    right_i = jnp.dot(first_i, broad, preferred_element_type=jnp.float32)
    return (right_r[:, :n] + sign * right_i[:, n:], right_i[:, :n] - sign * right_r[:, n:])


def forward_middle(left_r, left_i, intens, is_last, tall, broad, prop_r, prop_i, n):
    first_r, first_i = finish_left(left_r, left_i, 1.0, n)
    big_r, big_i = right_rows(first_r, first_i, broad, 1.0, n)
    far_r = big_r * prop_r - big_i * prop_i
    far_i = big_r * prop_i + big_i * prop_r
    excess = far_r * far_r + far_i * far_i - intens.astype(jnp.float32)
    src_r = jnp.where(is_last, excess * far_r, far_r)
    src_i = jnp.where(is_last, excess * far_i, far_i)
    sums_r, sums_i = left_sums(src_r, src_i, tall)
    return finish_left(sums_r, sums_i, -1.0, n)


def backward_middle(left_r, left_i, tall, broad, prop_r, prop_i, n):
    first_r, first_i = finish_left(left_r, left_i, 1.0, n)
    lr, li = right_rows(first_r, first_i, broad, 1.0, n)
    mr = lr * prop_r + li * prop_i
    mi = li * prop_r - lr * prop_i
    sums_r, sums_i = left_sums(mr, mi, tall)
    return finish_left(sums_r, sums_i, -1.0, n)


def backward_rows(first_r, first_i, saved, window, broad, n):
    lur, lui = right_rows(first_r, first_i, broad, -1.0, n)
    trans_r = jnp.cos(SIGMA * window)
    trans_i = jnp.sin(SIGMA * window)
    saved_r = saved[0].astype(jnp.float32)
    saved_i = saved[1].astype(jnp.float32)
    uar = trans_r * saved_r - trans_i * saved_i
    uai = trans_r * saved_i + trans_i * saved_r
    delta = SIGMA * (lui * uar - lur * uai)
    back = jnp.stack([trans_r * lur + trans_i * lui, trans_r * lui - trans_i * lur])
    return (back, delta)


def transmitted(window, wave):
    trans_r = jnp.cos(SIGMA * window)
    trans_i = jnp.sin(SIGMA * window)
    return (trans_r * wave[0] - trans_i * wave[1], trans_r * wave[1] + trans_i * wave[0])


def place(grad, delta, corner):
    size = delta.shape[0]
    old = lax.dynamic_slice(grad, (corner[0], corner[1]), (size, size))
    return lax.dynamic_update_slice(grad, old + delta, (corner[0], corner[1]))


def fold_final(grad, core, margin):
    inner = grad[margin : margin + core]
    from_left = shifted(grad[margin + core :].astype(jnp.bfloat16), "tile", 1).astype(jnp.float32)
    from_right = shifted(grad[:margin].astype(jnp.bfloat16), "tile", -1).astype(jnp.float32)
    inner = inner + jnp.pad(from_left, ((0, core - margin), (0, 0)))
    return inner + jnp.pad(from_right, ((core - margin, 0), (0, 0)))


def on_device(potential, probe, positions, intensity, fwd_wave, adj_wave, saved_wave):
    n = probe.shape[1]
    core = potential.shape[1]
    extent_cols = potential.shape[2]
    margin = (extent_cols - core) // 2
    sections = lax.axis_size("depth")
    section = lax.axis_index("depth")
    is_last = section == sections - 1
    is_first = section == 0
    extent = with_halo(potential[0].astype(jnp.bfloat16), (("tile", 0),), margin).astype(
        jnp.float32
    )
    tall, broad = tables(n)
    prop_r, prop_i = propagator(n)
    probe_wave = probe.astype(jnp.float32)
    wave = fwd_wave[0, 0]
    adjoint = adj_wave[0, 0]
    spots = positions[0]
    total = jnp.zeros(extent.shape, jnp.float32)
    blocks = 1
    rows = n // blocks
    f_pos = lax.dynamic_slice(spots, (2 * sections - 1 - section, 0), (1, 2))[0]
    f_win = lax.dynamic_slice(extent, (f_pos[0], f_pos[1]), (n, n))
    ur, ui = transmitted(f_win, wave)
    wave_lr, wave_li = left_sums(ur, ui, tall)
    adj_lr, adj_li = left_sums(adjoint[0], adjoint[1], tall)
    for tick in range(TICKS):
        a_pos = lax.dynamic_slice(spots, (tick + section, 0), (1, 2))[0]
        a_win = lax.dynamic_slice(extent, (a_pos[0], a_pos[1]), (n, n))
        fwd_r, fwd_i = forward_middle(
            wave_lr, wave_li, intensity[0, tick], is_last, tall, broad, prop_r, prop_i, n
        )
        bwd_r, bwd_i = backward_middle(adj_lr, adj_li, tall, broad, prop_r, prop_i, n)
        more = tick + 1 < TICKS
        if more:
            n_pos = lax.dynamic_slice(spots, (tick + 1 - section + 2 * sections - 1, 0), (1, 2))[0]
            n_win = lax.dynamic_slice(extent, (n_pos[0], n_pos[1]), (n, n))
            wave_lr = jnp.zeros((2 * n, n), jnp.float32)
            wave_li = jnp.zeros((2 * n, n), jnp.float32)
            adj_lr = jnp.zeros((2 * n, n), jnp.float32)
            adj_li = jnp.zeros((2 * n, n), jnp.float32)
        sent_r, sent_i = right_rows(fwd_r, fwd_i, broad, -1.0, n)
        sent = jnp.stack([sent_r, sent_i])
        back, delta = backward_rows(
            bwd_r, bwd_i, saved_wave[0, 0, tick, :, 0:rows], a_win, broad, n
        )
        back_half = back.astype(jnp.bfloat16)
        moved = shifted(sent.astype(jnp.bfloat16), "depth", 1).astype(sent.dtype)
        returned = shifted(back_half, "depth", -1)
        wave_rows = jnp.where(is_first, probe_wave, moved)
        adj_rows = jnp.where(is_last, sent.astype(jnp.bfloat16), returned)
        if more:
            nr, ni = transmitted(n_win, wave_rows)
            part_r, part_i = left_sums(nr, ni, tall)
            wave_lr = part_r
            wave_li = part_i
            part_r, part_i = left_sums(adj_rows[0], adj_rows[1], tall)
            adj_lr = part_r
            adj_li = part_i
        delta_parts = delta
        wave = wave_rows
        adjoint = adj_rows
        delta = delta_parts
        total = place(total, delta, a_pos)
    core_sum = fold_final(total, core, margin)
    return (wave[None, None], adjoint[None, None], core_sum[None])


def solution(mesh):
    placed = (
        P("depth", "tile", None),
        P(),
        P("tile", None, None),
        P("tile", None, None, None),
        P("depth", "tile", None, None, None),
        P("depth", "tile", None, None, None),
        P("depth", "tile", None, None, None, None),
    )
    return jax.shard_map(
        on_device,
        mesh=mesh,
        in_specs=placed,
        out_specs=(
            P("depth", "tile", None, None, None),
            P("depth", "tile", None, None, None),
            P("depth", "tile", None),
        ),
        check_vma=False,
    )
```

profile of v0, /device:TPU:312, one launch (start us, length us, event | category | flops | bytes accessed | tf_op | source)
XLA Modules:
  0.0 159.9 jit_solution(6604545847892870524)
XLA Ops:
  1.7 3.3 %collective-permute-start.1 = (bf16[64,384]{1,0:T(8,128)(2,1)S(1)}, bf16[64,384]{1,0:T(8,128)(2,1)S(1)}, u32[]{:S(2)}, u32[]{:S(2)}) collective-permute-start(bf16[64,384]{1,0:T(8,128)(2,1)S(1)} %get-tuple-element.42), channel_id=1, source_target_pairs={{1,0},{2,1},{3,2},{4,3},{5,4},{6,5},{7,6},{8,7},{9,8},{10,9},{11,1... | collective-permute-start | bytes 147464 | tf_op jit(solution)/shard_map/ppermute | solution.py:29
  5.0 4.7 %collective-permute-start = (bf16[64,384]{1,0:T(8,128)(2,1)S(1)}, bf16[64,384]{1,0:T(8,128)(2,1)S(1)}, u32[]{:S(2)}, u32[]{:S(2)}) collective-permute-start(bf16[64,384]{1,0:T(8,128)(2,1)S(1)} %get-tuple-element.41), channel_id=1, source_target_pairs={{0,1},{1,2},{2,3},{3,4},{4,5},{5,6},{6,7},{7,8},{8,9},{9,10},{10,1... | collective-permute-start | bytes 147464 | tf_op jit(solution)/shard_map/ppermute | solution.py:26
  52.4 2.2 %fusion.6 = (f32[256,256]{1,0:T(8,128)S(1)}, bf16[1,256,256]{2,1,0:T(8,128)(2,1)S(1)}, bf16[1,256,256]{2,1,0:T(8,128)(2,1)S(1)}) fusion(f32[384,384]{1,0:T(8,128)S(1)} %maximum_convert_fusion, s32[]{:T(128)S(6)} %select_n.288, s32[]{:T(128)S(6)} %select_n.289, bf16[1,1,4,2,256,256]{5,4,3,2,1,0:T(8,128)(2,1)} %param.13, f32[256,512]{1,0:T(8,128)S(1)} %fusion.202, ...), kind=kLoop, calls=%fused_computation.39 | loop fusion | flops 1638400 | bytes 2097160 | tf_op jit(solution)/shard_map/mul | solution.py:99
  54.6 3.1 %collective-permute-start.6 = (bf16[2,256,256]{2,1,0:T(8,128)(2,1)S(1)}, bf16[2,256,256]{2,1,0:T(8,128)(2,1)}, u32[]{:S(2)}, u32[]{:S(2)}) collective-permute-start(bf16[2,256,256]{2,1,0:T(8,128)(2,1)S(1)} %pad_maximum_fusion.6), channel_id=1, source_target_pairs={{16,0},{32,16},{48,32},{64,48},{80,64},{96,80},{112,96},{128,112},... | collective-permute-start | bytes 786440 | tf_op jit(solution)/shard_map/ppermute | solution.py:18
  58.2 4.0 %dynamic_update_slice.12 = f32[384,384]{1,0:T(8,128)S(1)} dynamic-update-slice(f32[384,384]{1,0:T(8,128)S(1)} %broadcast_in_dim.20, f32[256,256]{1,0:T(8,128)S(1)} %get-tuple-element.12, s32[]{:T(128)S(6)} %select_n.288, s32[]{:T(128)S(6)} %select_n.289) | dynamic-update-slice | bytes 524292 | tf_op jit(solution)/shard_map/dynamic_update_slice | solution.py:113
  64.2 1.3 fusion.146
  67.3 3.4 %collective-permute-start.2 = (bf16[2,256,256]{2,1,0:T(8,128)(2,1)S(1)}, bf16[2,256,256]{2,1,0:T(8,128)(2,1)S(1)}, u32[]{:S(2)}, u32[]{:S(2)}) collective-permute-start(bf16[2,256,256]{2,1,0:T(8,128)(2,1)S(1)} %get-tuple-element.40), channel_id=1, source_target_pairs={{0,16},{16,32},{32,48},{48,64},{64,80},{80,96},{96,112},{112,128},... | collective-permute-start | bytes 786440 | tf_op jit(solution)/shard_map/ppermute | solution.py:18
  70.7 2.2 %fusion.13 = (f32[256,256]{1,0:T(8,128)S(1)}, bf16[1,256,256]{2,1,0:T(8,128)(2,1)S(1)}, bf16[1,256,256]{2,1,0:T(8,128)(2,1)S(1)}) fusion(f32[384,384]{1,0:T(8,128)S(1)} %dynamic_update_slice.12, s32[]{:T(128)S(6)} %select_n.285, s32[]{:T(128)S(6)} %select_n.286, f32[384,384]{1,0:T(8,128)S(1)} %maximum_convert_fusion, ...), kind=kLoop, calls=%fused_computation.46 | loop fusion | flops 1703936 | bytes 2359304 | tf_op jit(solution)/shard_map/add | solution.py:113
  73.0 3.8 %dynamic_update_slice.13 = f32[384,384]{1,0:T(8,128)S(1)} dynamic-update-slice(f32[384,384]{1,0:T(8,128)S(1)} %dynamic_update_slice.12, f32[256,256]{1,0:T(8,128)S(1)} %get-tuple-element.9, s32[]{:T(128)S(6)} %select_n.285, s32[]{:T(128)S(6)} %select_n.286) | dynamic-update-slice | bytes 524292 | tf_op jit(solution)/shard_map/dynamic_update_slice | solution.py:113
  76.8 6.3 %collective-permute-start.7 = (bf16[2,256,256]{2,1,0:T(8,128)(2,1)S(1)}, bf16[2,256,256]{2,1,0:T(8,128)(2,1)S(1)}, u32[]{:S(2)}, u32[]{:S(2)}) collective-permute-start(bf16[2,256,256]{2,1,0:T(8,128)(2,1)S(1)} %pad_maximum_fusion.7), channel_id=1, source_target_pairs={{16,0},{32,16},{48,32},{64,48},{80,64},{96,80},{112,96},{128,112},... | collective-permute-start | bytes 786440 | tf_op jit(solution)/shard_map/ppermute | solution.py:18
  89.4 1.3 fusion.148
  90.7 1.3 fusion.149
  92.5 1.9 %collective-permute-start.3 = (bf16[2,256,256]{2,1,0:T(8,128)(2,1)S(1)}, bf16[2,256,256]{2,1,0:T(8,128)(2,1)S(1)}, u32[]{:S(2)}, u32[]{:S(2)}) collective-permute-start(bf16[2,256,256]{2,1,0:T(8,128)(2,1)S(1)} %get-tuple-element.38), channel_id=1, source_target_pairs={{0,16},{16,32},{32,48},{48,64},{64,80},{80,96},{96,112},{112,128},... | collective-permute-start | bytes 786440 | tf_op jit(solution)/shard_map/ppermute | solution.py:18
  94.4 2.2 %fusion.20 = (f32[256,256]{1,0:T(8,128)S(1)}, bf16[1,256,256]{2,1,0:T(8,128)(2,1)S(1)}, bf16[1,256,256]{2,1,0:T(8,128)(2,1)S(1)}) fusion(f32[384,384]{1,0:T(8,128)S(1)} %dynamic_update_slice.13, s32[]{:T(128)S(6)} %select_n.282, s32[]{:T(128)S(6)} %select_n.283, f32[384,384]{1,0:T(8,128)S(1)} %maximum_convert_fusion, ...), kind=kLoop, calls=%fused_computation.53 | loop fusion | flops 1703936 | bytes 2359304 | tf_op jit(solution)/shard_map/add | solution.py:113
  96.7 3.8 %dynamic_update_slice.14 = f32[384,384]{1,0:T(8,128)S(1)} dynamic-update-slice(f32[384,384]{1,0:T(8,128)S(1)} %dynamic_update_slice.13, f32[256,256]{1,0:T(8,128)S(1)} %get-tuple-element.6, s32[]{:T(128)S(6)} %select_n.282, s32[]{:T(128)S(6)} %select_n.283) | dynamic-update-slice | bytes 524292 | tf_op jit(solution)/shard_map/dynamic_update_slice | solution.py:113
  100.6 7.5 %collective-permute-start.8 = (bf16[2,256,256]{2,1,0:T(8,128)(2,1)S(1)}, bf16[2,256,256]{2,1,0:T(8,128)(2,1)S(1)}, u32[]{:S(2)}, u32[]{:S(2)}) collective-permute-start(bf16[2,256,256]{2,1,0:T(8,128)(2,1)S(1)} %pad_maximum_fusion.8), channel_id=1, source_target_pairs={{16,0},{32,16},{48,32},{64,48},{80,64},{96,80},{112,96},{128,112},... | collective-permute-start | bytes 786440 | tf_op jit(solution)/shard_map/ppermute | solution.py:18
  117.4 1.9 %collective-permute-start.4 = (bf16[2,256,256]{2,1,0:T(8,128)(2,1)S(1)}, bf16[2,256,256]{2,1,0:T(8,128)(2,1)}, u32[]{:S(2)}, u32[]{:S(2)}) collective-permute-start(bf16[2,256,256]{2,1,0:T(8,128)(2,1)S(1)} %get-tuple-element.36), channel_id=1, source_target_pairs={{0,16},{16,32},{32,48},{48,64},{64,80},{80,96},{96,112},{112,128},... | collective-permute-start | bytes 786440 | tf_op jit(solution)/shard_map/ppermute | solution.py:18
  119.4 2.2 %fusion.27 = (f32[256,256]{1,0:T(8,128)S(1)}, bf16[1,256,256]{2,1,0:T(8,128)(2,1)S(1)}, bf16[1,256,256]{2,1,0:T(8,128)(2,1)S(1)}) fusion(f32[384,384]{1,0:T(8,128)S(1)} %dynamic_update_slice.14, s32[]{:T(128)S(6)} %select_n.279, s32[]{:T(128)S(6)} %select_n.280, f32[384,384]{1,0:T(8,128)S(1)} %maximum_convert_fusion, ...), kind=kLoop, calls=%fused_computation.60 | loop fusion | flops 1703936 | bytes 2359304 | tf_op jit(solution)/shard_map/add | solution.py:113
  121.6 7.3 %collective-permute-start.9 = (bf16[2,256,256]{2,1,0:T(8,128)(2,1)S(1)}, bf16[2,256,256]{2,1,0:T(8,128)(2,1)S(1)}, u32[]{:S(2)}, u32[]{:S(2)}) collective-permute-start(bf16[2,256,256]{2,1,0:T(8,128)(2,1)S(1)} %pad_maximum_fusion.9), channel_id=1, source_target_pairs={{16,0},{32,16},{48,32},{64,48},{80,64},{96,80},{112,96},{128,112},... | collective-permute-start | bytes 786440 | tf_op jit(solution)/shard_map/ppermute | solution.py:18
  128.9 3.5 %dynamic_update_slice.15 = f32[384,384]{1,0:T(8,128)S(1)} dynamic-update-slice(f32[384,384]{1,0:T(8,128)S(1)} %dynamic_update_slice.14, f32[256,256]{1,0:T(8,128)S(1)} %get-tuple-element.3, s32[]{:T(128)S(6)} %select_n.279, s32[]{:T(128)S(6)} %select_n.280) | dynamic-update-slice | bytes 524292 | tf_op jit(solution)/shard_map/dynamic_update_slice | solution.py:113
  132.5 1.9 %collective-permute-start.11 = (bf16[64,384]{1,0:T(8,128)(2,1)S(1)}, bf16[64,384]{1,0:T(8,128)(2,1)S(1)}, u32[]{:S(2)}, u32[]{:S(2)}) collective-permute-start(bf16[64,384]{1,0:T(8,128)(2,1)S(1)} %get-tuple-element.32), channel_id=1, source_target_pairs={{1,0},{2,1},{3,2},{4,3},{5,4},{6,5},{7,6},{8,7},{9,8},{10,9},{11,1... | collective-permute-start | bytes 147464 | tf_op jit(solution)/shard_map/ppermute | solution.py:18
  134.4 6.3 %collective-permute-start.10 = (bf16[64,384]{1,0:T(8,128)(2,1)S(1)}, bf16[64,384]{1,0:T(8,128)(2,1)S(1)}, u32[]{:S(2)}, u32[]{:S(2)}) collective-permute-start(bf16[64,384]{1,0:T(8,128)(2,1)S(1)} %get-tuple-element.31), channel_id=1, source_target_pairs={{0,1},{1,2},{2,3},{3,4},{4,5},{5,6},{6,7},{7,8},{8,9},{9,10},{10,1... | collective-permute-start | bytes 147464 | tf_op jit(solution)/shard_map/ppermute | solution.py:18
  147.8 1.9 %collective-permute-start.5 = (bf16[2,256,256]{2,1,0:T(8,128)(2,1)S(1)}, bf16[2,256,256]{2,1,0:T(8,128)(2,1)S(1)}, u32[]{:S(2)}, u32[]{:S(2)}) collective-permute-start(bf16[2,256,256]{2,1,0:T(8,128)(2,1)S(1)} %get-tuple-element.34), channel_id=1, source_target_pairs={{0,16},{16,32},{32,48},{48,64},{64,80},{80,96},{96,112},{112,128},... | collective-permute-start | bytes 786440 | tf_op jit(solution)/shard_map/ppermute | solution.py:18
  150.5 8.6 %collective-permute-done.5 = bf16[2,256,256]{2,1,0:T(8,128)(2,1)S(1)} collective-permute-done((bf16[2,256,256]{2,1,0:T(8,128)(2,1)S(1)}, bf16[2,256,256]{2,1,0:T(8,128)(2,1)S(1)}, u32[]{:S(2)}, u32[]{:S(2)}) %collective-permute-start.5) | collective-permute-done | bytes 262176 | tf_op jit(solution)/shard_map/ppermute | solution.py:18
  (119 shorter events, 42.7 us)
Async XLA Ops:
  0.6 9.1 %copy-start.2 = (f32[1,256,384]{2,1,0:T(8,128)S(1)}, f32[1,256,384]{2,1,0:T(8,128)}, u32[]{:S(2)}) copy-start(f32[1,256,384]{2,1,0:T(8,128)} %param.7) | copy-start | bytes 1179652
  1.7 45.8 %collective-permute-start.1 = (bf16[64,384]{1,0:T(8,128)(2,1)S(1)}, bf16[64,384]{1,0:T(8,128)(2,1)S(1)}, u32[]{:S(2)}, u32[]{:S(2)}) collective-permute-start(bf16[64,384]{1,0:T(8,128)(2,1)S(1)} %get-tuple-element.42), channel_id=1, source_target_pairs={{1,0},{2,1},{3,2},{4,3},{5,4},{6,5},{7,6},{8,7},{9,8},{10,9},{11,1... | collective-permute-start | bytes 147464 | tf_op jit(solution)/shard_map/ppermute | solution.py:29
  5.0 42.6 %collective-permute-start = (bf16[64,384]{1,0:T(8,128)(2,1)S(1)}, bf16[64,384]{1,0:T(8,128)(2,1)S(1)}, u32[]{:S(2)}, u32[]{:S(2)}) collective-permute-start(bf16[64,384]{1,0:T(8,128)(2,1)S(1)} %get-tuple-element.41), channel_id=1, source_target_pairs={{0,1},{1,2},{2,3},{3,4},{4,5},{5,6},{6,7},{7,8},{8,9},{9,10},{10,1... | collective-permute-start | bytes 147464 | tf_op jit(solution)/shard_map/ppermute | solution.py:26
  9.8 1.1 copy-start.4
  14.9 0.7 copy-start.5
  17.4 30.3 %copy-start.3 = (f32[1,1,2,256,256]{4,3,2,1,0:T(8,128)S(1)}, f32[1,1,2,256,256]{4,3,2,1,0:T(8,128)}, u32[]{:S(2)}) copy-start(f32[1,1,2,256,256]{4,3,2,1,0:T(8,128)} %param.11) | copy-start | bytes 1572868
  50.6 1.2 copy-start.1
  54.6 7.7 %collective-permute-start.6 = (bf16[2,256,256]{2,1,0:T(8,128)(2,1)S(1)}, bf16[2,256,256]{2,1,0:T(8,128)(2,1)}, u32[]{:S(2)}, u32[]{:S(2)}) collective-permute-start(bf16[2,256,256]{2,1,0:T(8,128)(2,1)S(1)} %pad_maximum_fusion.6), channel_id=1, source_target_pairs={{16,0},{32,16},{48,32},{64,48},{80,64},{96,80},{112,96},{128,112},... | collective-permute-start | bytes 786440 | tf_op jit(solution)/shard_map/ppermute | solution.py:18
  67.3 15.8 %collective-permute-start.2 = (bf16[2,256,256]{2,1,0:T(8,128)(2,1)S(1)}, bf16[2,256,256]{2,1,0:T(8,128)(2,1)S(1)}, u32[]{:S(2)}, u32[]{:S(2)}) collective-permute-start(bf16[2,256,256]{2,1,0:T(8,128)(2,1)S(1)} %get-tuple-element.40), channel_id=1, source_target_pairs={{0,16},{16,32},{32,48},{48,64},{64,80},{80,96},{96,112},{112,128},... | collective-permute-start | bytes 786440 | tf_op jit(solution)/shard_map/ppermute | solution.py:18
  76.8 6.3 %copy-start = (bf16[2,256,256]{2,1,0:T(8,128)(2,1)S(1)}, bf16[2,256,256]{2,1,0:T(8,128)(2,1)}, u32[]{:S(2)}) copy-start(bf16[2,256,256]{2,1,0:T(8,128)(2,1)} %param.8) | copy-start | bytes 786436
  76.8 11.6 %collective-permute-start.7 = (bf16[2,256,256]{2,1,0:T(8,128)(2,1)S(1)}, bf16[2,256,256]{2,1,0:T(8,128)(2,1)S(1)}, u32[]{:S(2)}, u32[]{:S(2)}) collective-permute-start(bf16[2,256,256]{2,1,0:T(8,128)(2,1)S(1)} %pad_maximum_fusion.7), channel_id=1, source_target_pairs={{16,0},{32,16},{48,32},{64,48},{80,64},{96,80},{112,96},{128,112},... | collective-permute-start | bytes 786440 | tf_op jit(solution)/shard_map/ppermute | solution.py:18
  92.5 15.6 %collective-permute-start.3 = (bf16[2,256,256]{2,1,0:T(8,128)(2,1)S(1)}, bf16[2,256,256]{2,1,0:T(8,128)(2,1)S(1)}, u32[]{:S(2)}, u32[]{:S(2)}) collective-permute-start(bf16[2,256,256]{2,1,0:T(8,128)(2,1)S(1)} %get-tuple-element.38), channel_id=1, source_target_pairs={{0,16},{16,32},{32,48},{48,64},{64,80},{80,96},{96,112},{112,128},... | collective-permute-start | bytes 786440 | tf_op jit(solution)/shard_map/ppermute | solution.py:18
  100.6 12.8 %collective-permute-start.8 = (bf16[2,256,256]{2,1,0:T(8,128)(2,1)S(1)}, bf16[2,256,256]{2,1,0:T(8,128)(2,1)S(1)}, u32[]{:S(2)}, u32[]{:S(2)}) collective-permute-start(bf16[2,256,256]{2,1,0:T(8,128)(2,1)S(1)} %pad_maximum_fusion.8), channel_id=1, source_target_pairs={{16,0},{32,16},{48,32},{64,48},{80,64},{96,80},{112,96},{128,112},... | collective-permute-start | bytes 786440 | tf_op jit(solution)/shard_map/ppermute | solution.py:18
  117.4 23.3 %collective-permute-start.4 = (bf16[2,256,256]{2,1,0:T(8,128)(2,1)S(1)}, bf16[2,256,256]{2,1,0:T(8,128)(2,1)}, u32[]{:S(2)}, u32[]{:S(2)}) collective-permute-start(bf16[2,256,256]{2,1,0:T(8,128)(2,1)S(1)} %get-tuple-element.36), channel_id=1, source_target_pairs={{0,16},{16,32},{32,48},{48,64},{64,80},{80,96},{96,112},{112,128},... | collective-permute-start | bytes 786440 | tf_op jit(solution)/shard_map/ppermute | solution.py:18
  121.6 25.4 %collective-permute-start.9 = (bf16[2,256,256]{2,1,0:T(8,128)(2,1)S(1)}, bf16[2,256,256]{2,1,0:T(8,128)(2,1)S(1)}, u32[]{:S(2)}, u32[]{:S(2)}) collective-permute-start(bf16[2,256,256]{2,1,0:T(8,128)(2,1)S(1)} %pad_maximum_fusion.9), channel_id=1, source_target_pairs={{16,0},{32,16},{48,32},{64,48},{80,64},{96,80},{112,96},{128,112},... | collective-permute-start | bytes 786440 | tf_op jit(solution)/shard_map/ppermute | solution.py:18
  132.5 17.2 %collective-permute-start.11 = (bf16[64,384]{1,0:T(8,128)(2,1)S(1)}, bf16[64,384]{1,0:T(8,128)(2,1)S(1)}, u32[]{:S(2)}, u32[]{:S(2)}) collective-permute-start(bf16[64,384]{1,0:T(8,128)(2,1)S(1)} %get-tuple-element.32), channel_id=1, source_target_pairs={{1,0},{2,1},{3,2},{4,3},{5,4},{6,5},{7,6},{8,7},{9,8},{10,9},{11,1... | collective-permute-start | bytes 147464 | tf_op jit(solution)/shard_map/ppermute | solution.py:18
  134.4 15.3 %collective-permute-start.10 = (bf16[64,384]{1,0:T(8,128)(2,1)S(1)}, bf16[64,384]{1,0:T(8,128)(2,1)S(1)}, u32[]{:S(2)}, u32[]{:S(2)}) collective-permute-start(bf16[64,384]{1,0:T(8,128)(2,1)S(1)} %get-tuple-element.31), channel_id=1, source_target_pairs={{0,1},{1,2},{2,3},{3,4},{4,5},{5,6},{6,7},{7,8},{8,9},{9,10},{10,1... | collective-permute-start | bytes 147464 | tf_op jit(solution)/shard_map/ppermute | solution.py:18
  147.8 11.3 %collective-permute-start.5 = (bf16[2,256,256]{2,1,0:T(8,128)(2,1)S(1)}, bf16[2,256,256]{2,1,0:T(8,128)(2,1)S(1)}, u32[]{:S(2)}, u32[]{:S(2)}) collective-permute-start(bf16[2,256,256]{2,1,0:T(8,128)(2,1)S(1)} %get-tuple-element.34), channel_id=1, source_target_pairs={{0,16},{16,32},{32,48},{48,64},{64,80},{80,96},{96,112},{112,128},... | collective-permute-start | bytes 786440 | tf_op jit(solution)/shard_map/ppermute | solution.py:18
where the time goes:
time: 161 us; the launch traced here: 160 us
  starting transfers between devices  49.5 us (31%)
  matrix products  31.3 us (19%)
  between operations  31.2 us (19%)
  other arithmetic  21 us (13%)
  local copies, waits for them, and re-layouts  18.3 us (11%)
  waiting for transfers between devices  8.61 us (5%)
    ppermute x10, starting transfers between devices, shifted(): return lax.ppermute(block, axis, route)  41.5 us
    dynamic_update_slice x4, local copies, waits for them, and re-layouts, place(): return lax.dynamic_update_slice(grad, old + delta, (corner[0], corner[1]))  15.1 us
    dot_general x16, matrix products, left_sums(): jnp.dot(tall_cols, real.astype(jnp.bfloat16), preferred_element_type=jnp....  12 us
    dot_general x16, matrix products, left_sums(): jnp.dot(tall_cols, imag.astype(jnp.bfloat16), preferred_element_type=jnp....  12 us
    ppermute x10, waiting for transfers between devices, shifted(): return lax.ppermute(block, axis, route)  8.6 us
    add x3, other arithmetic, place(): return lax.dynamic_update_slice(grad, old + delta, (corner[0], corner[1]))  6.73 us
    sub x4, other arithmetic, forward_middle(): far_r = big_r * prop_r - big_i * prop_i  4.76 us
    ppermute x1, starting transfers between devices, with_halo(): lax.ppermute(lax.slice_in_dim(block, block.shape[dim] - width, None, axis...  4.7 us
  transfers between devices with their start and end apart: 12, of which 1 were waited for; matrix products, arithmetic and copies ran while one was open for 30% of the time, Pallas kernels for 0%

commit v1 on v0

v1 whole, which is shorter than its diff:
```python
import functools
import math

import jax
import jax.numpy as jnp
import numpy as np
from jax import lax
from jax.experimental import pallas as pl
from jax.experimental.pallas import tpu as pltpu
from jax.sharding import PartitionSpec as P

TICKS = 4
SIGMA = 0.8
DEFOCUS = 6.0
LANES = 128
SUB = 8
F32 = jnp.float32
BF16 = jnp.bfloat16


def dft_matrices(n):
    idx = np.arange(n)
    angle = ((idx[:, None] * idx[None, :]) % n).astype(np.float32) * np.float32(2.0 * math.pi / n)
    scale = np.float32(1.0 / math.sqrt(n))
    cos_t = np.cos(angle) * scale
    sin_t = np.sin(angle) * scale
    both = np.block([[cos_t, sin_t], [-sin_t, cos_t]])
    return both.astype(BF16), np.ascontiguousarray(both.T).astype(BF16)


def propagator(n):
    idx = np.arange(n)
    freq = np.where(idx < n // 2, idx, idx - n).astype(np.float32)
    square = freq[:, None] * freq[:, None] + freq[None, :] * freq[None, :]
    phase = np.float32(-math.pi * DEFOCUS) * square / np.float32(n * n)
    return np.cos(phase).astype(np.float32), np.sin(phase).astype(np.float32)


def sin_cos(x):
    mid = 1.2
    y = x - mid
    z = y * y
    s = y * (1.0 + z * (-1.0 / 6 + z * (1.0 / 120 + z * (-1.0 / 5040 + z * (1.0 / 362880)))))
    c = 1.0 + z * (-0.5 + z * (1.0 / 24 + z * (-1.0 / 720 + z * (1.0 / 40320 + z * (-1.0 / 3628800)))))
    cm, sm = math.cos(mid), math.sin(mid)
    return s * cm + c * sm, c * cm - s * sm


def turned(x, back, size, axis):
    own = lax.broadcasted_iota(jnp.int32, x.shape, axis)
    return pltpu.roll(x, lax.rem(size - back, size), axis), own < size - back


def cut(ref, row, col, n):
    base = pl.multiple_of(row // SUB * SUB, SUB)
    groups = n // SUB + 1
    pieces = []
    for j in range(n // LANES + 1):
        x = ref[pl.ds(base, n + SUB), j * LANES : (j + 1) * LANES].reshape(groups, SUB, LANES)
        x, near = turned(x, row - base, SUB, 1)
        x = jnp.where(near[1:], x[:-1], x[1:]).reshape(n, LANES)
        pieces.append(turned(x, col, LANES, 1))
    return jnp.concatenate(
        [jnp.where(here[1], here[0], after[0]) for here, after in zip(pieces[:-1], pieces[1:])], axis=1
    )


def place(ref, row, col, block):
    n = block.shape[0]
    base = pl.multiple_of(row // SUB * SUB, SUB)
    groups = n // SUB
    zero = jnp.zeros((n, LANES), F32)
    pieces = [
        pltpu.roll(block[:, j * LANES : (j + 1) * LANES], lax.rem(col, LANES), 1) for j in range(n // LANES)
    ]
    far = lax.broadcasted_iota(jnp.int32, (n, LANES), 1) >= col
    gap = jnp.zeros((1, SUB, LANES), F32)
    low = lax.broadcasted_iota(jnp.int32, (groups + 1, SUB, LANES), 1) >= row - base
    for j, (before, here) in enumerate(zip([zero] + pieces, pieces + [zero])):
        x = jnp.where(far, here, before).reshape(groups, SUB, LANES)
        x = pltpu.roll(x, row - base, 1)
        x = jnp.where(low, jnp.concatenate([x, gap], 0), jnp.concatenate([gap, x], 0))
        spot = (pl.ds(base, n + SUB), slice(j * LANES, (j + 1) * LANES))
        ref[spot] = ref[spot] + x.reshape(n + SUB, LANES)


def right(real, imag, table):
    n = real.shape[1]
    both = jnp.concatenate([real.astype(BF16), imag.astype(BF16)], axis=1)
    out = jnp.dot(both, table[...], preferred_element_type=F32)
    return out[:, :n], out[:, n:]


def left(real, imag, table):
    n = real.shape[0]
    both = jnp.concatenate([real.astype(BF16), imag.astype(BF16)], axis=0)
    out = jnp.dot(table[...], both, preferred_element_type=F32)
    return out[:n], out[n:]


def forward(ur, ui, m, mt, pr, pi):
    ar, ai = right(ur, ui, mt)
    br, bi = left(ar, ai, m)
    return br * pr - bi * pi, br * pi + bi * pr


def inverse(fr, fi, m, mt):
    ar, ai = right(fr, fi, m)
    return left(ar, ai, mt)


def adjoint(lr, li, m, mt, pr, pi):
    ar, ai = right(lr, li, mt)
    br, bi = left(ar, ai, m)
    return inverse(br * pr + bi * pi, bi * pr - br * pi, m, mt)


def extent_kernel(pot, low, high, tr, ti):
    margin = low.shape[0]
    core = pot.shape[1]
    for rows, v in (
        (slice(0, margin), low[...].astype(F32)),
        (slice(margin, margin + core), pot[0]),
        (slice(margin + core, margin + core + margin), high[...].astype(F32)),
    ):
        s, c = sin_cos(SIGMA * v)
        tr[rows] = c
        ti[rows] = s


def first_adjoint_kernel(adj, m, mt, pr, pi, lr, li):
    lr[...], li[...] = adjoint(adj[0, 0, 0], adj[0, 0, 1], m, mt, pr[...], pi[...])


def step_kernel(tick, turn, gathered, *refs):
    first = tick == 0
    refs = list(refs)
    pos, tr, ti, saved, intens, m, mt, pr, pi = refs[:9]
    rest = refs[9:]
    fresh = first and turn == 1
    if first:
        fwd, lr0, li0 = rest[:3]
        rest = rest[3:]
    else:
        recv, probe = rest[:2]
        rest = rest[2:]
    if not fresh:
        rest = rest[1:]
    out, acc = rest
    n = out.shape[1]
    sections = lax.axis_size("depth")
    section = lax.axis_index("depth")
    parity = lax.rem(section, 2)
    is_forward = lax.rem(parity + tick, 2) == turn
    if fresh:
        acc[...] = jnp.zeros(acc.shape, F32)

    def received(part):
        return recv[1 - parity, part] if gathered else recv[part]

    @pl.when(is_forward)
    def _():
        mb = tick - section + 2 * sections - 1
        row, col = pos[mb, 0], pos[mb, 1]
        wr = cut(tr, row, col, n)
        wi = cut(ti, row, col, n)
        if first:
            xr, xi = fwd[0, 0, 0], fwd[0, 0, 1]
        else:
            xr, xi = received(0), received(1)
            if not gathered:
                at_start = section == 0
                xr = jnp.where(at_start, probe[0], xr)
                xi = jnp.where(at_start, probe[1], xi)
            xr, xi = xr.astype(F32), xi.astype(F32)
        fr, fi = forward(wr * xr - wi * xi, wr * xi + wi * xr, m, mt, pr[...], pi[...])
        excess = fr * fr + fi * fi - intens[0, tick].astype(F32)
        weight = jnp.where(section == sections - 1, excess, 1.0)
        sr, si = inverse(fr * weight, fi * weight, m, mt)
        out[0] = sr.astype(BF16)
        out[1] = si.astype(BF16)

    @pl.when(jnp.logical_not(is_forward))
    def _():
        mb = tick + section
        row, col = pos[mb, 0], pos[mb, 1]
        if first:
            lr, li = lr0[...], li0[...]
        else:
            lr, li = adjoint(received(0), received(1), m, mt, pr[...], pi[...])
        wr = cut(tr, row, col, n)
        wi = cut(ti, row, col, n)
        br = wr * lr + wi * li
        bi = wr * li - wi * lr
        out[0] = br.astype(BF16)
        out[1] = bi.astype(BF16)
        delta = SIGMA * (bi * saved[0, 0, tick, 0].astype(F32) - br * saved[0, 0, tick, 1].astype(F32))
        place(acc, row, col, delta)


def waves_kernel(swapped, gathered, probe, wave, adj):
    section = lax.axis_index("depth")
    parity = lax.rem(section, 2)

    @pl.when(parity == 0)
    def _():
        wave[0, 0] = jnp.where(section == 0, probe[...], swapped[...]).astype(F32)
        adj[0, 0] = gathered[1]

    @pl.when(parity == 1)
    def _():
        wave[0, 0] = gathered[0].astype(F32)
        adj[0, 0] = swapped[...]


def fold_kernel(acc, from_low, from_high, grad):
    margin = from_low.shape[0]
    core = grad.shape[1]
    grad[0, :margin] = acc[margin : 2 * margin] + from_low[...].astype(F32)
    grad[0, margin : core - margin] = acc[2 * margin : core]
    grad[0, core - margin :] = acc[core : core + margin] + from_high[...].astype(F32)


VM = pl.BlockSpec(memory_space=pltpu.VMEM)
SM = pl.BlockSpec(memory_space=pltpu.SMEM)


def call(kernel, name, in_specs, outs, args, aliases=None, cost=None, limit=24):
    return pl.pallas_call(
        kernel,
        name=name,
        in_specs=in_specs,
        out_specs=[VM] * len(outs),
        out_shape=outs,
        input_output_aliases=aliases or {},
        compiler_params=pltpu.CompilerParams(vmem_limit_bytes=limit << 20),
        cost_estimate=cost,
    )(*args)


def shape(*dims, dtype=F32):
    return jax.ShapeDtypeStruct(dims, dtype)


def swap_chips(x):
    last = lax.axis_size("depth") - 1
    route = [(0, 0), (last, last)]
    for i in range(1, last, 2):
        route += [(i, i + 1), (i + 1, i)]
    return lax.ppermute(x, "depth", route)


def gather_chip(x):
    count = lax.axis_size("depth")
    groups = [[i, i + 1] for i in range(0, count, 2)]
    return lax.all_gather(x, "depth", axis_index_groups=groups)


def tile_shift(x, distance):
    devices = range(lax.axis_size("tile"))
    route = [(i - distance, i) for i in devices if i - distance in devices]
    return lax.ppermute(x, "tile", route)


def on_device(potential, probe, positions, intensity, fwd_wave, adj_wave, saved_wave):
    n = probe.shape[1]
    core, cols = potential.shape[1:]
    margin = (cols - core) // 2
    tall = core + 2 * margin + SUB
    spots = positions[0]
    m, mt = (jnp.asarray(t) for t in dft_matrices(n))
    pr, pi = (jnp.asarray(t) for t in propagator(n))
    step_cost = pl.CostEstimate(flops=8 * 2 * n * n * n * 2, bytes_accessed=1 << 20, transcendentals=0)

    low = tile_shift(potential[0, core - margin :].astype(BF16), 1)
    high = tile_shift(potential[0, :margin].astype(BF16), -1)
    lr0, li0 = call(
        first_adjoint_kernel, "first_adjoint", [VM] * 5, [shape(n, n)] * 2, (adj_wave, m, mt, pr, pi), cost=step_cost
    )
    tr, ti = call(extent_kernel, "extent", [VM] * 3, [shape(tall, cols)] * 2, (potential, low, high))

    common = (spots, tr, ti, saved_wave, intensity, m, mt, pr, pi)
    outs = [shape(2, n, n, dtype=BF16), shape(tall, cols)]

    def start(turn, acc):
        args = common + (fwd_wave, lr0, li0) + (() if acc is None else (acc,))
        aliases = {} if acc is None else {len(args) - 1: 1}
        return call(
            functools.partial(step_kernel, 0, turn, False), f"step0_{turn}",
            [SM] + [VM] * (len(args) - 1), outs, args, aliases, step_cost,
        )

    def step(tick, turn, gathered, recv, acc):
        args = common + (recv, probe, acc)
        return call(
            functools.partial(step_kernel, tick, turn, gathered), f"step{tick}_{turn}",
            [SM] + [VM] * (len(args) - 1), outs, args, {len(args) - 1: 1}, step_cost,
        )

    b, acc = start(1, None)
    b = swap_chips(b)
    a, acc = start(0, acc)
    a = gather_chip(a)
    a, acc = step(1, 0, True, a, acc)
    a = swap_chips(a)
    b, acc = step(1, 1, False, b, acc)
    b = gather_chip(b)
    b, acc = step(2, 1, True, b, acc)
    b = swap_chips(b)
    a, acc = step(2, 0, False, a, acc)
    a = gather_chip(a)
    a, acc = step(3, 0, True, a, acc)
    a = swap_chips(a)
    b, acc = step(3, 1, False, b, acc)
    from_low = tile_shift(acc[margin + core : core + 2 * margin].astype(BF16), 1)
    from_high = tile_shift(acc[:margin].astype(BF16), -1)
    b = gather_chip(b)
    wave, adj = call(
        waves_kernel, "waves", [VM] * 3,
        [shape(1, 1, 2, n, n), shape(1, 1, 2, n, n, dtype=BF16)], (a, b, probe),
    )
    (grad,) = call(fold_kernel, "fold", [VM] * 3, [shape(1, core, cols)], (acc, from_low, from_high))
    return wave, adj, grad


def solution(mesh):
    placed = (
        P("depth", "tile", None),
        P(),
        P("tile", None, None),
        P("tile", None, None, None),
        P("depth", "tile", None, None, None),
        P("depth", "tile", None, None, None),
        P("depth", "tile", None, None, None, None),
    )
    return jax.shard_map(
        on_device,
        mesh=mesh,
        in_specs=placed,
        out_specs=(
            P("depth", "tile", None, None, None),
            P("depth", "tile", None, None, None),
            P("depth", "tile", None),
        ),
        check_vma=False,
    )
```

time: 161 us -> 75.4 us (0.47)
  the two profiles are of different devices: /device:TPU:312 before, /device:TPU:199 now
where the time goes in v1:
time: 75.4 us; the launch traced here: 74.8 us
  starting transfers between devices  33.2 us (44%)
  Pallas kernels  22.9 us (30%)
  blocking collectives  8.86 us (12%)
  local copies, waits for them, and re-layouts  5.15 us (7%)
  waiting for transfers between devices  2.68 us (4%)
  other arithmetic  1.13 us (1%)
  between operations  0.94 us (1%)
    pallas_call x12, Pallas kernels, call(): pl.pallas_call(kernel, name=name, in_specs=in_specs, out_specs=[VM] * len...  22.9 us
    ppermute x4, starting transfers between devices, swap_chips(): return lax.ppermute(x, 'depth', route)  19.9 us
    ppermute x4, starting transfers between devices, tile_shift(): return lax.ppermute(x, 'tile', route)  13.2 us
    all_gather x4, blocking collectives, gather_chip(): return lax.all_gather(x, 'depth', axis_index_groups=groups)  8.86 us
    unnamed x29, local copies, waits for them, and re-layouts  5.13 us
    ppermute x4, waiting for transfers between devices, tile_shift(): return lax.ppermute(x, 'tile', route)  2.67 us
  transfers between devices with their start and end apart: 8, of which 2 were waited for; matrix products, arithmetic and copies ran while one was open for 0% of the time, Pallas kernels for 25%

profile of v1, /device:TPU:199, one launch (start us, length us, event | category | flops | bytes accessed | tf_op | source)
XLA Modules:
  0.0 74.8 jit_solution(6862765124332617997)
XLA Ops:
  0.7 1.1 %convert.8 = bf16[1,256,384]{2,1,0:T(8,128)(2,1)S(1)} convert(f32[1,256,384]{2,1,0:T(8,128)} %pot.1) | non-fusion elementwise | flops 98304 | bytes 589824 | tf_op jit(solution)/shard_map/convert.3
  1.8 5.4 %collective-permute-start.1 = (bf16[64,384]{1,0:T(8,128)(2,1)S(1)}, bf16[64,384]{1,0:T(8,128)(2,1)S(1)}, u32[]{:S(2)}, u32[]{:S(2)}) collective-permute-start(bf16[64,384]{1,0:T(8,128)(2,1)S(1)} %get-tuple-element.49), channel_id=1, source_target_pairs={{1,0},{2,1},{3,2},{4,3},{5,4},{6,5},{7,6},{8,7},{9,8},{10,9},{11,1... | collective-permute-start | bytes 147464 | tf_op jit(solution)/shard_map/ppermute | solution.py:262
  7.2 1.9 %collective-permute-start = (bf16[64,384]{1,0:T(8,128)(2,1)S(1)}, bf16[64,384]{1,0:T(8,128)(2,1)S(1)}, u32[]{:S(2)}, u32[]{:S(2)}) collective-permute-start(bf16[64,384]{1,0:T(8,128)(2,1)S(1)} %get-tuple-element.50), channel_id=1, source_target_pairs={{0,1},{1,2},{2,3},{3,4},{4,5},{5,6},{6,7},{7,8},{8,9},{9,10},{10,1... | collective-permute-start | bytes 147464 | tf_op jit(solution)/shard_map/ppermute | solution.py:262
  9.2 1.0 %copy-done.3 = bf16[512,512]{1,0:T(8,128)(2,1)S(1)} copy-done((bf16[512,512]{1,0:T(8,128)(2,1)S(1)}, bf16[512,512]{1,0:T(8,128)(2,1)}, u32[]{:S(2)}) %copy-start.3) | copy-done | bytes 524312
  12.2 1.1 %first_adjoint.1 = (f32[256,256]{1,0:T(8,128)S(1)}, f32[256,256]{1,0:T(8,128)S(1)}) custom-call(bf16[1,1,2,256,256]{4,3,2,1,0:T(8,128)(2,1)S(1)} %copy-done.12, bf16[512,512]{1,0:T(8,128)(2,1)S(1)} %copy-done.3, bf16[512,512]{1,0:T(8,128)(2,1)S(1)} %copy-done.2, f32[256,256]{1,0:T(8,128)S(1)} %copy-done.6, f32[256,256]{1,0:T(8,128)S(1)} %copy-done.5), custom_call_target="tpu_custom_call" | custom-call | flops 536870912 | bytes 1048576 | tf_op jit(solution)/shard_map/first_adjoint/pallas_call | solution.py:229
  16.8 2.6 %step0_1.1 = (bf16[2,256,256]{2,1,0:T(8,128)(2,1)S(1)}, f32[392,384]{1,0:T(8,128)S(1)}) custom-call(s32[67,2]{1,0:T(8,128)S(1)} %bitcast.9, f32[392,384]{1,0:T(8,128)S(1)} %get-tuple-element.25.refs_1_, f32[392,384]{1,0:T(8,128)S(1)} %get-tuple-element.26.refs_2_, bf16[1,1,4,2,256,256]{5,4,3,2,1,0:T(8,128)(2,1)S(1)} %copy-done, ...), custom_call_target="tpu_custom_call" | custom-call | flops 536870912 | bytes 1048576 | tf_op jit(solution)/shard_map/step0_1/pallas_call | solution.py:229
  19.4 6.8 %collective-permute-start.3 = (bf16[2,256,256]{2,1,0:T(8,128)(2,1)S(1)}, bf16[2,256,256]{2,1,0:T(8,128)(2,1)S(1)}, u32[]{:S(2)}, u32[]{:S(2)}) collective-permute-start(bf16[2,256,256]{2,1,0:T(8,128)(2,1)S(1)} %get-tuple-element.33), channel_id=1, source_target_pairs={{0,0},{496,496},{16,32},{32,16},{48,64},{64,48},{80,96},{96,80},{1... | collective-permute-start | bytes 786440 | tf_op jit(solution)/shard_map/ppermute | solution.py:250
  26.2 1.6 %step0_0.1 = (bf16[2,256,256]{2,1,0:T(8,128)(2,1)S(1)}, f32[392,384]{1,0:T(8,128)S(1)}) custom-call(s32[67,2]{1,0:T(8,128)S(1)} %bitcast.10, f32[392,384]{1,0:T(8,128)S(1)} %get-tuple-element.25.refs_1_, f32[392,384]{1,0:T(8,128)S(1)} %get-tuple-element.26.refs_2_, bf16[1,1,4,2,256,256]{5,4,3,2,1,0:T(8,128)(2,1)S(1)} %copy-done, ...), custom_call_target="tpu_custom_call", output_to_operand_aliasing={{1}: (12, {})} | custom-call | flops 536870912 | bytes 1048576 | tf_op jit(solution)/shard_map/step0_0/pallas_call | solution.py:229
  27.8 2.3 %all-gather = bf16[4,256,256]{2,1,0:T(8,128)(2,1)S(1)} all-gather(bf16[2,256,256]{2,1,0:T(8,128)(2,1)S(1)} %get-tuple-element.30), channel_id=2, replica_groups={{0,16},{32,48},{64,80},{96,112},{128,144},{160,176},{192,208},{224,240}..., dimensions={0}, use_global_device_ids=true | all-gather | bytes 786432 | tf_op jit(solution)/shard_map/all_gather | solution.py:256
  30.1 2.6 %step1_0.1 = (bf16[2,256,256]{2,1,0:T(8,128)(2,1)S(1)}, f32[392,384]{1,0:T(8,128)S(1)}) custom-call(s32[67,2]{1,0:T(8,128)S(1)} %bitcast.11, f32[392,384]{1,0:T(8,128)S(1)} %get-tuple-element.25.refs_1_, f32[392,384]{1,0:T(8,128)S(1)} %get-tuple-element.26.refs_2_, bf16[1,1,4,2,256,256]{5,4,3,2,1,0:T(8,128)(2,1)S(1)} %copy-done, ...), custom_call_target="tpu_custom_call", output_to_operand_aliasing={{1}: (11, {})} | custom-call | flops 536870912 | bytes 1048576 | tf_op jit(solution)/shard_map/step1_0/pallas_call | solution.py:229
  32.7 4.0 %collective-permute-start.2 = (bf16[2,256,256]{2,1,0:T(8,128)(2,1)S(1)}, bf16[2,256,256]{2,1,0:T(8,128)(2,1)S(1)}, u32[]{:S(2)}, u32[]{:S(2)}) collective-permute-start(bf16[2,256,256]{2,1,0:T(8,128)(2,1)S(1)} %get-tuple-element.32), channel_id=1, source_target_pairs={{0,0},{496,496},{16,32},{32,16},{48,64},{64,48},{80,96},{96,80},{1... | collective-permute-start | bytes 786440 | tf_op jit(solution)/shard_map/ppermute | solution.py:250
  36.7 2.5 %step1_1.1 = (bf16[2,256,256]{2,1,0:T(8,128)(2,1)S(1)}, f32[392,384]{1,0:T(8,128)S(1)}) custom-call(s32[67,2]{1,0:T(8,128)S(1)} %bitcast.12, f32[392,384]{1,0:T(8,128)S(1)} %get-tuple-element.25.refs_1_, f32[392,384]{1,0:T(8,128)S(1)} %get-tuple-element.26.refs_2_, bf16[1,1,4,2,256,256]{5,4,3,2,1,0:T(8,128)(2,1)S(1)} %copy-done, ...), custom_call_target="tpu_custom_call", output_to_operand_aliasing={{1}: (11, {})} | custom-call | flops 536870912 | bytes 1048576 | tf_op jit(solution)/shard_map/step1_1/pallas_call | solution.py:229
  39.1 2.2 %all-gather.1 = bf16[4,256,256]{2,1,0:T(8,128)(2,1)S(1)} all-gather(bf16[2,256,256]{2,1,0:T(8,128)(2,1)S(1)} %get-tuple-element.35), channel_id=3, replica_groups={{0,16},{32,48},{64,80},{96,112},{128,144},{160,176},{192,208},{224,240}..., dimensions={0}, use_global_device_ids=true | all-gather | bytes 786432 | tf_op jit(solution)/shard_map/all_gather | solution.py:256
  41.3 2.6 %step2_1.1 = (bf16[2,256,256]{2,1,0:T(8,128)(2,1)S(1)}, f32[392,384]{1,0:T(8,128)S(1)}) custom-call(s32[67,2]{1,0:T(8,128)S(1)} %bitcast.13, f32[392,384]{1,0:T(8,128)S(1)} %get-tuple-element.25.refs_1_, f32[392,384]{1,0:T(8,128)S(1)} %get-tuple-element.26.refs_2_, bf16[1,1,4,2,256,256]{5,4,3,2,1,0:T(8,128)(2,1)S(1)} %copy-done, ...), custom_call_target="tpu_custom_call", output_to_operand_aliasing={{1}: (11, {})} | custom-call | flops 536870912 | bytes 1048576 | tf_op jit(solution)/shard_map/step2_1/pallas_call | solution.py:229
  43.9 5.2 %collective-permute-start.5 = (bf16[2,256,256]{2,1,0:T(8,128)(2,1)S(1)}, bf16[2,256,256]{2,1,0:T(8,128)(2,1)S(1)}, u32[]{:S(2)}, u32[]{:S(2)}) collective-permute-start(bf16[2,256,256]{2,1,0:T(8,128)(2,1)S(1)} %get-tuple-element.41), channel_id=1, source_target_pairs={{0,0},{496,496},{16,32},{32,16},{48,64},{64,48},{80,96},{96,80},{1... | collective-permute-start | bytes 786440 | tf_op jit(solution)/shard_map/ppermute | solution.py:250
  49.1 2.6 %step2_0.1 = (bf16[2,256,256]{2,1,0:T(8,128)(2,1)S(1)}, f32[392,384]{1,0:T(8,128)S(1)}) custom-call(s32[67,2]{1,0:T(8,128)S(1)} %bitcast.14, f32[392,384]{1,0:T(8,128)S(1)} %get-tuple-element.25.refs_1_, f32[392,384]{1,0:T(8,128)S(1)} %get-tuple-element.26.refs_2_, bf16[1,1,4,2,256,256]{5,4,3,2,1,0:T(8,128)(2,1)S(1)} %copy-done, ...), custom_call_target="tpu_custom_call", output_to_operand_aliasing={{1}: (11, {})} | custom-call | flops 536870912 | bytes 1048576 | tf_op jit(solution)/shard_map/step2_0/pallas_call | solution.py:229
  51.8 2.2 %all-gather.2 = bf16[4,256,256]{2,1,0:T(8,128)(2,1)S(1)} all-gather(bf16[2,256,256]{2,1,0:T(8,128)(2,1)S(1)} %get-tuple-element.38), channel_id=4, replica_groups={{0,16},{32,48},{64,80},{96,112},{128,144},{160,176},{192,208},{224,240}..., dimensions={0}, use_global_device_ids=true | all-gather | bytes 786432 | tf_op jit(solution)/shard_map/all_gather | solution.py:256
  53.9 2.6 %step3_0.1 = (bf16[2,256,256]{2,1,0:T(8,128)(2,1)S(1)}, f32[392,384]{1,0:T(8,128)S(1)}) custom-call(s32[67,2]{1,0:T(8,128)S(1)} %bitcast.15, f32[392,384]{1,0:T(8,128)S(1)} %get-tuple-element.25.refs_1_, f32[392,384]{1,0:T(8,128)S(1)} %get-tuple-element.26.refs_2_, bf16[1,1,4,2,256,256]{5,4,3,2,1,0:T(8,128)(2,1)S(1)} %copy-done, ...), custom_call_target="tpu_custom_call", output_to_operand_aliasing={{1}: (11, {})} | custom-call | flops 536870912 | bytes 1048576 | tf_op jit(solution)/shard_map/step3_0/pallas_call | solution.py:229
  56.5 4.0 %collective-permute-start.4 = (bf16[2,256,256]{2,1,0:T(8,128)(2,1)S(1)}, bf16[2,256,256]{2,1,0:T(8,128)(2,1)S(1)}, u32[]{:S(2)}, u32[]{:S(2)}) collective-permute-start(bf16[2,256,256]{2,1,0:T(8,128)(2,1)S(1)} %get-tuple-element.40), channel_id=1, source_target_pairs={{0,0},{496,496},{16,32},{32,16},{48,64},{64,48},{80,96},{96,80},{1... | collective-permute-start | bytes 786440 | tf_op jit(solution)/shard_map/ppermute | solution.py:250
  60.5 2.5 %step3_1.1 = (bf16[2,256,256]{2,1,0:T(8,128)(2,1)S(1)}, f32[392,384]{1,0:T(8,128)S(1)}) custom-call(s32[67,2]{1,0:T(8,128)S(1)} %bitcast.16, f32[392,384]{1,0:T(8,128)S(1)} %get-tuple-element.25.refs_1_, f32[392,384]{1,0:T(8,128)S(1)} %get-tuple-element.26.refs_2_, bf16[1,1,4,2,256,256]{5,4,3,2,1,0:T(8,128)(2,1)S(1)} %copy-done, ...), custom_call_target="tpu_custom_call", output_to_operand_aliasing={{1}: (11, {})} | custom-call | flops 536870912 | bytes 1048576 | tf_op jit(solution)/shard_map/step3_1/pallas_call | solution.py:229
  63.0 4.0 %collective-permute-start.7 = (bf16[64,384]{1,0:T(8,128)(2,1)S(1)}, bf16[64,384]{1,0:T(8,128)(2,1)S(1)}, u32[]{:S(2)}, u32[]{:S(2)}) collective-permute-start(bf16[64,384]{1,0:T(8,128)(2,1)S(1)} %get-tuple-element.47), channel_id=1, source_target_pairs={{1,0},{2,1},{3,2},{4,3},{5,4},{6,5},{7,6},{8,7},{9,8},{10,9},{11,1... | collective-permute-start | bytes 147464 | tf_op jit(solution)/shard_map/ppermute | solution.py:262
  67.1 1.9 %collective-permute-start.6 = (bf16[64,384]{1,0:T(8,128)(2,1)S(1)}, bf16[64,384]{1,0:T(8,128)(2,1)S(1)}, u32[]{:S(2)}, u32[]{:S(2)}) collective-permute-start(bf16[64,384]{1,0:T(8,128)(2,1)S(1)} %get-tuple-element.48), channel_id=1, source_target_pairs={{0,1},{1,2},{2,3},{3,4},{4,5},{5,6},{6,7},{7,8},{8,9},{9,10},{10,1... | collective-permute-start | bytes 147464 | tf_op jit(solution)/shard_map/ppermute | solution.py:262
  69.0 2.2 %all-gather.3 = bf16[4,256,256]{2,1,0:T(8,128)(2,1)S(1)} all-gather(bf16[2,256,256]{2,1,0:T(8,128)(2,1)S(1)} %get-tuple-element.43), channel_id=5, replica_groups={{0,16},{32,48},{64,80},{96,112},{128,144},{160,176},{192,208},{224,240}..., dimensions={0}, use_global_device_ids=true | all-gather | bytes 786432 | tf_op jit(solution)/shard_map/all_gather | solution.py:256
  72.1 1.9 %collective-permute-done.6.from_low = bf16[64,384]{1,0:T(8,128)(2,1)S(1)} collective-permute-done((bf16[64,384]{1,0:T(8,128)(2,1)S(1)}, bf16[64,384]{1,0:T(8,128)(2,1)S(1)}, u32[]{:S(2)}, u32[]{:S(2)}) %collective-permute-start.6) | collective-permute-done | bytes 49184 | tf_op jit(solution)/shard_map/ppermute | solution.py:262
  (41 shorter events, 7.2 us)
Async XLA Ops:
  0.6 8.6 %copy-start.2 = (bf16[512,512]{1,0:T(8,128)(2,1)S(1)}, bf16[512,512]{1,0:T(8,128)(2,1)}, u32[]{:S(2)}) copy-start(bf16[512,512]{1,0:T(8,128)(2,1)} %constant.9.clone.mt.refs_6_) | copy-start | bytes 1572868
  0.6 8.6 %copy-start.5 = (f32[256,256]{1,0:T(8,128)S(1)}, f32[256,256]{1,0:T(8,128)}, u32[]{:S(2)}) copy-start(f32[256,256]{1,0:T(8,128)} %constant.11.clone.pi.refs_8_) | copy-start | bytes 786436
  1.8 7.3 %copy-start.13 = (s32[1,67,2]{1,2,0:T(2,128)S(1)}, s32[1,67,2]{1,2,0:T(2,128)}, u32[]{:S(2)}) copy-start(s32[1,67,2]{1,2,0:T(2,128)} %param.13) | copy-start | bytes 1612
  1.8 11.5 %collective-permute-start.1 = (bf16[64,384]{1,0:T(8,128)(2,1)S(1)}, bf16[64,384]{1,0:T(8,128)(2,1)S(1)}, u32[]{:S(2)}, u32[]{:S(2)}) collective-permute-start(bf16[64,384]{1,0:T(8,128)(2,1)S(1)} %get-tuple-element.49), channel_id=1, source_target_pairs={{1,0},{2,1},{3,2},{4,3},{5,4},{6,5},{7,6},{8,7},{9,8},{10,9},{11,1... | collective-permute-start | bytes 147464 | tf_op jit(solution)/shard_map/ppermute | solution.py:262
  7.2 6.9 %collective-permute-start = (bf16[64,384]{1,0:T(8,128)(2,1)S(1)}, bf16[64,384]{1,0:T(8,128)(2,1)S(1)}, u32[]{:S(2)}, u32[]{:S(2)}) collective-permute-start(bf16[64,384]{1,0:T(8,128)(2,1)S(1)} %get-tuple-element.50), channel_id=1, source_target_pairs={{0,1},{1,2},{2,3},{3,4},{4,5},{5,6},{6,7},{7,8},{8,9},{9,10},{10,1... | collective-permute-start | bytes 147464 | tf_op jit(solution)/shard_map/ppermute | solution.py:262
  9.2 1.0 %copy-start.3 = (bf16[512,512]{1,0:T(8,128)(2,1)S(1)}, bf16[512,512]{1,0:T(8,128)(2,1)}, u32[]{:S(2)}) copy-start(bf16[512,512]{1,0:T(8,128)(2,1)} %constant.8.clone.m.refs_5_) | copy-start | bytes 1572868
  10.3 0.9 %copy-start.6 = (f32[256,256]{1,0:T(8,128)S(1)}, f32[256,256]{1,0:T(8,128)}, u32[]{:S(2)}) copy-start(f32[256,256]{1,0:T(8,128)} %constant.10.clone.pr.refs_7_) | copy-start | bytes 786436
  11.2 0.9 %copy-start.12 = (bf16[1,1,2,256,256]{4,3,2,1,0:T(8,128)(2,1)S(1)}, bf16[1,1,2,256,256]{4,3,2,1,0:T(8,128)(2,1)}, u32[]{:S(2)}) copy-start(bf16[1,1,2,256,256]{4,3,2,1,0:T(8,128)(2,1)} %adj.1) | copy-start | bytes 786436
  12.2 3.5 %copy-start = (bf16[1,1,4,2,256,256]{5,4,3,2,1,0:T(8,128)(2,1)S(1)}, bf16[1,1,4,2,256,256]{5,4,3,2,1,0:T(8,128)(2,1)}, u32[]{:S(2)}) copy-start(bf16[1,1,4,2,256,256]{5,4,3,2,1,0:T(8,128)(2,1)} %refs_3_.15) | copy-start | bytes 3145732
  12.2 3.6 %copy-start.1 = (bf16[1,4,256,256]{3,2,1,0:T(8,128)(2,1)S(1)}, bf16[1,4,256,256]{3,2,1,0:T(8,128)(2,1)}, u32[]{:S(2)}) copy-start(bf16[1,4,256,256]{3,2,1,0:T(8,128)(2,1)} %refs_4_.15) | copy-start | bytes 1572868
  12.2 3.6 %copy-start.4 = (bf16[512,512]{1,0:T(8,128)(2,1)S(1)}, bf16[512,512]{1,0:T(8,128)(2,1)}, u32[]{:S(2)}) copy-start(bf16[512,512]{1,0:T(8,128)(2,1)} %constant.8.clone.m.refs_5_) | copy-start | bytes 1572868
  13.3 2.4 %copy-start.7 = (f32[256,256]{1,0:T(8,128)S(1)}, f32[256,256]{1,0:T(8,128)}, u32[]{:S(2)}) copy-start(f32[256,256]{1,0:T(8,128)} %constant.10.clone.pr.refs_7_) | copy-start | bytes 786436
  14.1 1.0 %copy-start.11 = (f32[1,256,384]{2,1,0:T(8,128)S(1)}, f32[1,256,384]{2,1,0:T(8,128)}, u32[]{:S(2)}) copy-start(f32[1,256,384]{2,1,0:T(8,128)} %pot.1) | copy-start | bytes 1179652
  15.7 1.0 %copy-start.9 = (f32[1,1,2,256,256]{4,3,2,1,0:T(8,128)S(1)}, f32[1,1,2,256,256]{4,3,2,1,0:T(8,128)}, u32[]{:S(2)}) copy-start(f32[1,1,2,256,256]{4,3,2,1,0:T(8,128)} %refs_9_.3) | copy-start | bytes 1572868
  16.8 9.4 %copy-start.10 = (f32[1,1,2,256,256]{4,3,2,1,0:T(8,128)S(1)}, f32[1,1,2,256,256]{4,3,2,1,0:T(8,128)}, u32[]{:S(2)}) copy-start(f32[1,1,2,256,256]{4,3,2,1,0:T(8,128)} %refs_9_.3) | copy-start | bytes 1572868
  19.4 17.3 %collective-permute-start.3 = (bf16[2,256,256]{2,1,0:T(8,128)(2,1)S(1)}, bf16[2,256,256]{2,1,0:T(8,128)(2,1)S(1)}, u32[]{:S(2)}, u32[]{:S(2)}) collective-permute-start(bf16[2,256,256]{2,1,0:T(8,128)(2,1)S(1)} %get-tuple-element.33), channel_id=1, source_target_pairs={{0,0},{496,496},{16,32},{32,16},{48,64},{64,48},{80,96},{96,80},{1... | collective-permute-start | bytes 786440 | tf_op jit(solution)/shard_map/ppermute | solution.py:250
  27.8 2.3 %copy-start.8 = (bf16[2,256,256]{2,1,0:T(8,128)(2,1)S(1)}, bf16[2,256,256]{2,1,0:T(8,128)(2,1)}, u32[]{:S(2)}) copy-start(bf16[2,256,256]{2,1,0:T(8,128)(2,1)} %probe.1) | copy-start | bytes 786436
  32.7 16.4 %collective-permute-start.2 = (bf16[2,256,256]{2,1,0:T(8,128)(2,1)S(1)}, bf16[2,256,256]{2,1,0:T(8,128)(2,1)S(1)}, u32[]{:S(2)}, u32[]{:S(2)}) collective-permute-start(bf16[2,256,256]{2,1,0:T(8,128)(2,1)S(1)} %get-tuple-element.32), channel_id=1, source_target_pairs={{0,0},{496,496},{16,32},{32,16},{48,64},{64,48},{80,96},{96,80},{1... | collective-permute-start | bytes 786440 | tf_op jit(solution)/shard_map/ppermute | solution.py:250
  43.9 16.6 %collective-permute-start.5 = (bf16[2,256,256]{2,1,0:T(8,128)(2,1)S(1)}, bf16[2,256,256]{2,1,0:T(8,128)(2,1)S(1)}, u32[]{:S(2)}, u32[]{:S(2)}) collective-permute-start(bf16[2,256,256]{2,1,0:T(8,128)(2,1)S(1)} %get-tuple-element.41), channel_id=1, source_target_pairs={{0,0},{496,496},{16,32},{32,16},{48,64},{64,48},{80,96},{96,80},{1... | collective-permute-start | bytes 786440 | tf_op jit(solution)/shard_map/ppermute | solution.py:250
  56.5 14.7 %collective-permute-start.4 = (bf16[2,256,256]{2,1,0:T(8,128)(2,1)S(1)}, bf16[2,256,256]{2,1,0:T(8,128)(2,1)S(1)}, u32[]{:S(2)}, u32[]{:S(2)}) collective-permute-start(bf16[2,256,256]{2,1,0:T(8,128)(2,1)S(1)} %get-tuple-element.40), channel_id=1, source_target_pairs={{0,0},{496,496},{16,32},{32,16},{48,64},{64,48},{80,96},{96,80},{1... | collective-permute-start | bytes 786440 | tf_op jit(solution)/shard_map/ppermute | solution.py:250
  63.0 9.1 %collective-permute-start.7 = (bf16[64,384]{1,0:T(8,128)(2,1)S(1)}, bf16[64,384]{1,0:T(8,128)(2,1)S(1)}, u32[]{:S(2)}, u32[]{:S(2)}) collective-permute-start(bf16[64,384]{1,0:T(8,128)(2,1)S(1)} %get-tuple-element.47), channel_id=1, source_target_pairs={{1,0},{2,1},{3,2},{4,3},{5,4},{6,5},{7,6},{8,7},{9,8},{10,9},{11,1... | collective-permute-start | bytes 147464 | tf_op jit(solution)/shard_map/ppermute | solution.py:262
  67.1 6.9 %collective-permute-start.6 = (bf16[64,384]{1,0:T(8,128)(2,1)S(1)}, bf16[64,384]{1,0:T(8,128)(2,1)S(1)}, u32[]{:S(2)}, u32[]{:S(2)}) collective-permute-start(bf16[64,384]{1,0:T(8,128)(2,1)S(1)} %get-tuple-element.48), channel_id=1, source_target_pairs={{0,1},{1,2},{2,3},{3,4},{4,5},{5,6},{6,7},{7,8},{8,9},{9,10},{10,1... | collective-permute-start | bytes 147464 | tf_op jit(solution)/shard_map/ppermute | solution.py:262

commit v2 on v1

--- a/solution.py
+++ b/solution.py
@@ -115,44 +115,64 @@
     return inverse(br * pr + bi * pi, bi * pr - br * pi, m, mt)
 
 
-def extent_kernel(pot, low, high, tr, ti):
+def edges_kernel(pot, low, high):
     margin = low.shape[0]
     core = pot.shape[1]
-    for rows, v in (
-        (slice(0, margin), low[...].astype(F32)),
-        (slice(margin, margin + core), pot[0]),
-        (slice(margin + core, margin + core + margin), high[...].astype(F32)),
-    ):
-        s, c = sin_cos(SIGMA * v)
-        tr[rows] = c
-        ti[rows] = s
-
-
-def first_adjoint_kernel(adj, m, mt, pr, pi, lr, li):
+    low[...] = pot[0, core - margin :].astype(BF16)
+    high[...] = pot[0, :margin].astype(BF16)
+
+
+def transmit(v, tr, ti, rows):
+    s, c = sin_cos(SIGMA * v)
+    tr[rows] = c
+    ti[rows] = s
+
+
+def first_kernel(spots, pot, adj, m, mt, pr, pi, corners, lr, li, tr, ti):
+    core = pot.shape[1]
+    margin = (tr.shape[0] - SUB - core) // 2
+    sections = lax.axis_size("depth")
+    section = lax.axis_index("depth")
+    which = lax.broadcasted_iota(jnp.int32, spots.shape, 1)
+    for tick in range(TICKS):
+        for backward, mb in enumerate((tick - section + 2 * sections - 1, tick + section)):
+            at = 4 * tick + 2 * backward
+            chosen = jnp.sum(jnp.where(which == mb, spots[...].astype(F32), 0.0), axis=1, keepdims=True)
+            corners[at : at + 2] = jnp.broadcast_to(chosen.astype(jnp.int32), (2, LANES))
     lr[...], li[...] = adjoint(adj[0, 0, 0], adj[0, 0, 1], m, mt, pr[...], pi[...])
-
-
-def step_kernel(tick, turn, gathered, *refs):
-    first = tick == 0
-    refs = list(refs)
-    pos, tr, ti, saved, intens, m, mt, pr, pi = refs[:9]
-    rest = refs[9:]
-    fresh = first and turn == 1
+    transmit(pot[0], tr, ti, slice(margin, margin + core))
+
+
+def corner(corners, tick, backward):
+    at = 4 * tick + 2 * backward
+    numbers = corners[...]
+    return numbers[at, 0], numbers[at + 1, 0]
+
+
+def step_kernel(tick, turn, *refs):
+    first, fresh, last = tick == 0, tick == 0 and turn == 1, tick == TICKS - 1 and turn == 1
+    gathered = tick > 0 and (tick + turn) % 2 == 1
+    corners, saved, intens, m, mt, pr, pi, tr, ti, *rest = refs
     if first:
-        fwd, lr0, li0 = rest[:3]
-        rest = rest[3:]
+        fwd, lr0, li0, *rest = rest
     else:
-        recv, probe = rest[:2]
-        rest = rest[2:]
-    if not fresh:
-        rest = rest[1:]
-    out, acc = rest
+        recv, probe, *rest = rest
+    if fresh:
+        low, high, out, acc, tr, ti = rest
+    elif last:
+        _, out, acc, to_low, to_high = rest
+    else:
+        _, out, acc = rest
     n = out.shape[1]
     sections = lax.axis_size("depth")
     section = lax.axis_index("depth")
     parity = lax.rem(section, 2)
     is_forward = lax.rem(parity + tick, 2) == turn
     if fresh:
+        margin = low.shape[0]
+        core = tr.shape[0] - SUB - 2 * margin
+        transmit(low[...].astype(F32), tr, ti, slice(0, margin))
+        transmit(high[...].astype(F32), tr, ti, slice(margin + core, 2 * margin + core))
         acc[...] = jnp.zeros(acc.shape, F32)
 
     def received(part):
@@ -160,8 +180,7 @@
 
     @pl.when(is_forward)
     def _():
-        mb = tick - section + 2 * sections - 1
-        row, col = pos[mb, 0], pos[mb, 1]
+        row, col = corner(corners, tick, 0)
         wr = cut(tr, row, col, n)
         wi = cut(ti, row, col, n)
         if first:
@@ -182,8 +201,7 @@
 
     @pl.when(jnp.logical_not(is_forward))
     def _():
-        mb = tick + section
-        row, col = pos[mb, 0], pos[mb, 1]
+        row, col = corner(corners, tick, 1)
         if first:
             lr, li = lr0[...], li0[...]
         else:
@@ -197,8 +215,13 @@
         delta = SIGMA * (bi * saved[0, 0, tick, 0].astype(F32) - br * saved[0, 0, tick, 1].astype(F32))
         place(acc, row, col, delta)
 
-
-def waves_kernel(swapped, gathered, probe, wave, adj):
+    if last:
+        margin = to_low.shape[0]
+        to_low[...] = acc[:margin].astype(BF16)
+        to_high[...] = acc[acc.shape[0] - SUB - margin : acc.shape[0] - SUB].astype(BF16)
+
+
+def finish_kernel(swapped, gathered, probe, acc, from_low, from_high, wave, adj, grad):
     section = lax.axis_index("depth")
     parity = lax.rem(section, 2)
 
@@ -212,8 +235,6 @@
         wave[0, 0] = gathered[0].astype(F32)
         adj[0, 0] = swapped[...]
 
-
-def fold_kernel(acc, from_low, from_high, grad):
     margin = from_low.shape[0]
     core = grad.shape[1]
     grad[0, :margin] = acc[margin : 2 * margin] + from_low[...].astype(F32)
@@ -222,18 +243,17 @@
 
 
 VM = pl.BlockSpec(memory_space=pltpu.VMEM)
-SM = pl.BlockSpec(memory_space=pltpu.SMEM)
-
-
-def call(kernel, name, in_specs, outs, args, aliases=None, cost=None, limit=24):
+
+
+def call(kernel, name, outs, args, aliases=None, cost=None):
     return pl.pallas_call(
         kernel,
         name=name,
-        in_specs=in_specs,
+        in_specs=[VM] * len(args),
         out_specs=[VM] * len(outs),
         out_shape=outs,
         input_output_aliases=aliases or {},
-        compiler_params=pltpu.CompilerParams(vmem_limit_bytes=limit << 20),
+        compiler_params=pltpu.CompilerParams(vmem_limit_bytes=24 << 20),
         cost_estimate=cost,
     )(*args)
 
@@ -267,60 +287,60 @@
     core, cols = potential.shape[1:]
     margin = (cols - core) // 2
     tall = core + 2 * margin + SUB
-    spots = positions[0]
-    m, mt = (jnp.asarray(t) for t in dft_matrices(n))
-    pr, pi = (jnp.asarray(t) for t in propagator(n))
+    spots = positions[0].T
     step_cost = pl.CostEstimate(flops=8 * 2 * n * n * n * 2, bytes_accessed=1 << 20, transcendentals=0)
-
-    low = tile_shift(potential[0, core - margin :].astype(BF16), 1)
-    high = tile_shift(potential[0, :margin].astype(BF16), -1)
-    lr0, li0 = call(
-        first_adjoint_kernel, "first_adjoint", [VM] * 5, [shape(n, n)] * 2, (adj_wave, m, mt, pr, pi), cost=step_cost
-    )
-    tr, ti = call(extent_kernel, "extent", [VM] * 3, [shape(tall, cols)] * 2, (potential, low, high))
-
-    common = (spots, tr, ti, saved_wave, intensity, m, mt, pr, pi)
-    outs = [shape(2, n, n, dtype=BF16), shape(tall, cols)]
-
-    def start(turn, acc):
-        args = common + (fwd_wave, lr0, li0) + (() if acc is None else (acc,))
-        aliases = {} if acc is None else {len(args) - 1: 1}
+    edge_cost = pl.CostEstimate(flops=1 << 33, bytes_accessed=1 << 20, transcendentals=0)
+    extent = shape(tall, cols)
+    edge = shape(margin, cols, dtype=BF16)
+    half = shape(2, n, n, dtype=BF16)
+
+    m, mt, pr, pi = (jnp.asarray(t) for t in (*dft_matrices(n), *propagator(n)))
+    low, high = call(edges_kernel, "edges", [edge, edge], (potential,), cost=edge_cost)
+    low = tile_shift(low, 1)
+    high = tile_shift(high, -1)
+    corners, lr0, li0, tr, ti = call(
+        first_kernel, "first",
+        [shape(4 * TICKS, LANES, dtype=jnp.int32)] + [shape(n, n)] * 2 + [extent] * 2,
+        (spots, potential, adj_wave, m, mt, pr, pi), cost=step_cost,
+    )
+    common = (corners, saved_wave, intensity, m, mt, pr, pi)
+
+    def step(tick, turn, extra, outs, aliases):
+        args = (*common, tr, ti, *extra)
         return call(
-            functools.partial(step_kernel, 0, turn, False), f"step0_{turn}",
-            [SM] + [VM] * (len(args) - 1), outs, args, aliases, step_cost,
+            functools.partial(step_kernel, tick, turn), f"step{tick}_{turn}", [half, extent, *outs], args,
+            {len(args) + i if i < 0 else i: o for i, o in aliases.items()}, step_cost,
         )
 
-    def step(tick, turn, gathered, recv, acc):
-        args = common + (recv, probe, acc)
-        return call(
-            functools.partial(step_kernel, tick, turn, gathered), f"step{tick}_{turn}",
-            [SM] + [VM] * (len(args) - 1), outs, args, {len(args) - 1: 1}, step_cost,
+    def later(tick, turn, recv, acc, outs=()):
+        return step(tick, turn, (recv, probe, acc), outs, {-1: 1})
+
+    at_tr = len(common)
+    b, acc, tr, ti = step(0, 1, (fwd_wave, lr0, li0, low, high), [extent, extent], {at_tr: 2, at_tr + 1: 3})
+    b = swap_chips(b)
+    a, acc = step(0, 0, (fwd_wave, lr0, li0, acc), (), {-1: 1})
+    a = gather_chip(a)
+    a, acc = later(1, 0, a, acc)
+    a = swap_chips(a)
+    b, acc = later(1, 1, b, acc)
+    b = gather_chip(b)
+    b, acc = later(2, 1, b, acc)
+    b = swap_chips(b)
+    a, acc = later(2, 0, a, acc)
+    a = gather_chip(a)
+    a, acc = later(3, 0, a, acc)
+    a = swap_chips(a)
+    b, acc, to_low, to_high = later(3, 1, b, acc, [edge, edge])
+    from_low = tile_shift(to_high, 1)
+    from_high = tile_shift(to_low, -1)
+    b = gather_chip(b)
+    return tuple(
+        call(
+            finish_kernel, "finish",
+            [shape(1, 1, 2, n, n), shape(1, 1, 2, n, n, dtype=BF16), shape(1, core, cols)],
+            (a, b, probe, acc, from_low, from_high),
         )
-
-    b, acc = start(1, None)
-    b = swap_chips(b)
-    a, acc = start(0, acc)
-    a = gather_chip(a)
-    a, acc = step(1, 0, True, a, acc)
-    a = swap_chips(a)
-    b, acc = step(1, 1, False, b, acc)
-    b = gather_chip(b)
-    b, acc = step(2, 1, True, b, acc)
-    b = swap_chips(b)
-    a, acc = step(2, 0, False, a, acc)
-    a = gather_chip(a)
-    a, acc = step(3, 0, True, a, acc)
-    a = swap_chips(a)
-    b, acc = step(3, 1, False, b, acc)
-    from_low = tile_shift(acc[margin + core : core + 2 * margin].astype(BF16), 1)
-    from_high = tile_shift(acc[:margin].astype(BF16), -1)
-    b = gather_chip(b)
-    wave, adj = call(
-        waves_kernel, "waves", [VM] * 3,
-        [shape(1, 1, 2, n, n), shape(1, 1, 2, n, n, dtype=BF16)], (a, b, probe),
-    )
-    (grad,) = call(fold_kernel, "fold", [VM] * 3, [shape(1, core, cols)], (acc, from_low, from_high))
-    return wave, adj, grad
+    )
 
 
 def solution(mesh):

time: 75.4 us -> 60.1 us (0.80)
  the two profiles are of different devices: /device:TPU:199 before, /device:TPU:274 now
where the time goes in v2:
time: 60.1 us; the launch traced here: 59.8 us
  starting transfers between devices  30.1 us (50%)
  Pallas kernels  13.8 us (23%)
  blocking collectives  9.33 us (16%)
  waiting for transfers between devices  4.42 us (7%)
  local copies, waits for them, and re-layouts  1.17 us (2%)
  between operations  0.94 us (2%)
    ppermute x4, starting transfers between devices, swap_chips(): return lax.ppermute(x, 'depth', route)  17.1 us
    pallas_call x11, Pallas kernels, call(): pl.pallas_call(kernel, name=name, in_specs=[VM] * len(args), out_specs=[V...  13.8 us
    ppermute x4, starting transfers between devices, tile_shift(): return lax.ppermute(x, 'tile', route)  13 us
    all_gather x4, blocking collectives, gather_chip(): return lax.all_gather(x, 'depth', axis_index_groups=groups)  9.33 us
    ppermute x4, waiting for transfers between devices, tile_shift(): return lax.ppermute(x, 'tile', route)  4.41 us
  transfers between devices with their start and end apart: 8, of which 2 were waited for; matrix products, arithmetic and copies ran while one was open for 0% of the time, Pallas kernels for 20%

profile of v2, /device:TPU:274, one launch (start us, length us, event | category | flops | bytes accessed | tf_op | source)
XLA Modules:
  0.0 59.8 jit_solution(11712794161364744435)
XLA Ops:
  0.7 1.1 %copy-done.8 = f32[1,256,384]{2,1,0:T(8,128)S(1)} copy-done((f32[1,256,384]{2,1,0:T(8,128)S(1)}, f32[1,256,384]{2,1,0:T(8,128)}, u32[]{:S(2)}) %copy-start.8) | copy-done | bytes 393240
  1.8 3.6 %collective-permute-start = (bf16[64,384]{1,0:T(8,128)(2,1)S(1)}, bf16[64,384]{1,0:T(8,128)(2,1)S(1)}, u32[]{:S(2)}, u32[]{:S(2)}) collective-permute-start(bf16[64,384]{1,0:T(8,128)(2,1)S(1)} %get-tuple-element.35), channel_id=1, source_target_pairs={{0,1},{1,2},{2,3},{3,4},{4,5},{5,6},{6,7},{7,8},{8,9},{9,10},{10,1... | collective-permute-start | bytes 147464 | tf_op jit(solution)/shard_map/ppermute | solution.py:282
  5.4 2.4 %collective-permute-start.1 = (bf16[64,384]{1,0:T(8,128)(2,1)S(1)}, bf16[64,384]{1,0:T(8,128)(2,1)S(1)}, u32[]{:S(2)}, u32[]{:S(2)}) collective-permute-start(bf16[64,384]{1,0:T(8,128)(2,1)S(1)} %get-tuple-element.36), channel_id=1, source_target_pairs={{1,0},{2,1},{3,2},{4,3},{5,4},{6,5},{7,6},{8,7},{9,8},{10,9},{11,1... | collective-permute-start | bytes 147464 | tf_op jit(solution)/shard_map/ppermute | solution.py:282
  7.9 1.7 %first.1 = (s32[16,128]{1,0:T(8,128)S(1)}, f32[256,256]{1,0:T(8,128)S(1)}, f32[256,256]{1,0:T(8,128)S(1)}, f32[392,384]{1,0:T(8,128)S(1)}, f32[392,384]{1,0:T(8,128)S(1)}) custom-call(s32[2,67]{1,0:T(2,128)S(1)} %bitcast.11, f32[1,256,384]{2,1,0:T(8,128)S(1)} %copy-done.9, bf16[1,1,2,256,256]{4,3,2,1,0:T(8,128)(2,1)S(1)} %copy-done.10, ...), custom_call_target="tpu_custom_call" | custom-call | flops 536870912 | bytes 1048576 | tf_op jit(solution)/shard_map/first/pallas_call | solution.py:249
  9.7 2.5 %collective-permute-done.1.refs_13_ = bf16[64,384]{1,0:T(8,128)(2,1)S(1)} collective-permute-done((bf16[64,384]{1,0:T(8,128)(2,1)S(1)}, bf16[64,384]{1,0:T(8,128)(2,1)S(1)}, u32[]{:S(2)}, u32[]{:S(2)}) %collective-permute-start.1) | collective-permute-done | bytes 49184 | tf_op jit(solution)/shard_map/ppermute | solution.py:282
  13.0 2.4 %collective-permute-start.3 = (bf16[2,256,256]{2,1,0:T(8,128)(2,1)S(1)}, bf16[2,256,256]{2,1,0:T(8,128)(2,1)S(1)}, u32[]{:S(2)}, u32[]{:S(2)}) collective-permute-start(bf16[2,256,256]{2,1,0:T(8,128)(2,1)S(1)} %get-tuple-element.43), channel_id=1, source_target_pairs={{0,0},{496,496},{16,32},{32,16},{48,64},{64,48},{80,96},{96,80},{1... | collective-permute-start | bytes 786440 | tf_op jit(solution)/shard_map/ppermute | solution.py:270
  15.3 1.5 %step0_0.1 = (bf16[2,256,256]{2,1,0:T(8,128)(2,1)S(1)}, f32[392,384]{1,0:T(8,128)S(1)}) custom-call(s32[16,128]{1,0:T(8,128)S(1)} %get-tuple-element.30.refs_0_, bf16[1,1,4,2,256,256]{5,4,3,2,1,0:T(8,128)(2,1)S(1)} %copy-done, bf16[1,4,256,256]{3,2,1,0:T(8,128)(2,1)S(1)} %copy-done.3, ...), custom_call_target="tpu_custom_call", output_to_operand_aliasing={{1}: (12, {})} | custom-call | flops 536870912 | bytes 1048576 | tf_op jit(solution)/shard_map/step0_0/pallas_call | solution.py:249
  16.9 2.8 %all-gather = bf16[4,256,256]{2,1,0:T(8,128)(2,1)S(1)} all-gather(bf16[2,256,256]{2,1,0:T(8,128)(2,1)S(1)} %get-tuple-element.40), channel_id=2, replica_groups={{0,16},{32,48},{64,80},{96,112},{128,144},{160,176},{192,208},{224,240}..., dimensions={0}, use_global_device_ids=true | all-gather | bytes 786432 | tf_op jit(solution)/shard_map/all_gather | solution.py:276
  19.6 1.3 %step1_0.1 = (bf16[2,256,256]{2,1,0:T(8,128)(2,1)S(1)}, f32[392,384]{1,0:T(8,128)S(1)}) custom-call(s32[16,128]{1,0:T(8,128)S(1)} %get-tuple-element.30.refs_0_, bf16[1,1,4,2,256,256]{5,4,3,2,1,0:T(8,128)(2,1)S(1)} %copy-done, bf16[1,4,256,256]{3,2,1,0:T(8,128)(2,1)S(1)} %copy-done.3, ...), custom_call_target="tpu_custom_call", output_to_operand_aliasing={{1}: (11, {})} | custom-call | flops 536870912 | bytes 1048576 | tf_op jit(solution)/shard_map/step1_0/pallas_call | solution.py:249
  21.0 5.5 %collective-permute-start.2 = (bf16[2,256,256]{2,1,0:T(8,128)(2,1)S(1)}, bf16[2,256,256]{2,1,0:T(8,128)(2,1)S(1)}, u32[]{:S(2)}, u32[]{:S(2)}) collective-permute-start(bf16[2,256,256]{2,1,0:T(8,128)(2,1)S(1)} %get-tuple-element.42), channel_id=1, source_target_pairs={{0,0},{496,496},{16,32},{32,16},{48,64},{64,48},{80,96},{96,80},{1... | collective-permute-start | bytes 786440 | tf_op jit(solution)/shard_map/ppermute | solution.py:270
  26.5 1.5 %step1_1.1 = (bf16[2,256,256]{2,1,0:T(8,128)(2,1)S(1)}, f32[392,384]{1,0:T(8,128)S(1)}) custom-call(s32[16,128]{1,0:T(8,128)S(1)} %get-tuple-element.30.refs_0_, bf16[1,1,4,2,256,256]{5,4,3,2,1,0:T(8,128)(2,1)S(1)} %copy-done, bf16[1,4,256,256]{3,2,1,0:T(8,128)(2,1)S(1)} %copy-done.3, ...), custom_call_target="tpu_custom_call", output_to_operand_aliasing={{1}: (11, {})} | custom-call | flops 536870912 | bytes 1048576 | tf_op jit(solution)/shard_map/step1_1/pallas_call | solution.py:249
  28.0 2.2 %all-gather.1 = bf16[4,256,256]{2,1,0:T(8,128)(2,1)S(1)} all-gather(bf16[2,256,256]{2,1,0:T(8,128)(2,1)S(1)} %get-tuple-element.45), channel_id=3, replica_groups={{0,16},{32,48},{64,80},{96,112},{128,144},{160,176},{192,208},{224,240}..., dimensions={0}, use_global_device_ids=true | all-gather | bytes 786432 | tf_op jit(solution)/shard_map/all_gather | solution.py:276
  30.2 1.4 %step2_1.1 = (bf16[2,256,256]{2,1,0:T(8,128)(2,1)S(1)}, f32[392,384]{1,0:T(8,128)S(1)}) custom-call(s32[16,128]{1,0:T(8,128)S(1)} %get-tuple-element.30.refs_0_, bf16[1,1,4,2,256,256]{5,4,3,2,1,0:T(8,128)(2,1)S(1)} %copy-done, bf16[1,4,256,256]{3,2,1,0:T(8,128)(2,1)S(1)} %copy-done.3, ...), custom_call_target="tpu_custom_call", output_to_operand_aliasing={{1}: (11, {})} | custom-call | flops 536870912 | bytes 1048576 | tf_op jit(solution)/shard_map/step2_1/pallas_call | solution.py:249
  31.6 3.6 %collective-permute-start.5 = (bf16[2,256,256]{2,1,0:T(8,128)(2,1)S(1)}, bf16[2,256,256]{2,1,0:T(8,128)(2,1)S(1)}, u32[]{:S(2)}, u32[]{:S(2)}) collective-permute-start(bf16[2,256,256]{2,1,0:T(8,128)(2,1)S(1)} %get-tuple-element.51), channel_id=1, source_target_pairs={{0,0},{496,496},{16,32},{32,16},{48,64},{64,48},{80,96},{96,80},{1... | collective-permute-start | bytes 786440 | tf_op jit(solution)/shard_map/ppermute | solution.py:270
  35.2 1.7 %step2_0.1 = (bf16[2,256,256]{2,1,0:T(8,128)(2,1)S(1)}, f32[392,384]{1,0:T(8,128)S(1)}) custom-call(s32[16,128]{1,0:T(8,128)S(1)} %get-tuple-element.30.refs_0_, bf16[1,1,4,2,256,256]{5,4,3,2,1,0:T(8,128)(2,1)S(1)} %copy-done, bf16[1,4,256,256]{3,2,1,0:T(8,128)(2,1)S(1)} %copy-done.3, ...), custom_call_target="tpu_custom_call", output_to_operand_aliasing={{1}: (11, {})} | custom-call | flops 536870912 | bytes 1048576 | tf_op jit(solution)/shard_map/step2_0/pallas_call | solution.py:249
  36.9 2.2 %all-gather.2 = bf16[4,256,256]{2,1,0:T(8,128)(2,1)S(1)} all-gather(bf16[2,256,256]{2,1,0:T(8,128)(2,1)S(1)} %get-tuple-element.48), channel_id=4, replica_groups={{0,16},{32,48},{64,80},{96,112},{128,144},{160,176},{192,208},{224,240}..., dimensions={0}, use_global_device_ids=true | all-gather | bytes 786432 | tf_op jit(solution)/shard_map/all_gather | solution.py:276
  39.1 1.3 %step3_0.1 = (bf16[2,256,256]{2,1,0:T(8,128)(2,1)S(1)}, f32[392,384]{1,0:T(8,128)S(1)}) custom-call(s32[16,128]{1,0:T(8,128)S(1)} %get-tuple-element.30.refs_0_, bf16[1,1,4,2,256,256]{5,4,3,2,1,0:T(8,128)(2,1)S(1)} %copy-done, bf16[1,4,256,256]{3,2,1,0:T(8,128)(2,1)S(1)} %copy-done.3, ...), custom_call_target="tpu_custom_call", output_to_operand_aliasing={{1}: (11, {})} | custom-call | flops 536870912 | bytes 1048576 | tf_op jit(solution)/shard_map/step3_0/pallas_call | solution.py:249
  40.4 5.5 %collective-permute-start.4 = (bf16[2,256,256]{2,1,0:T(8,128)(2,1)S(1)}, bf16[2,256,256]{2,1,0:T(8,128)(2,1)S(1)}, u32[]{:S(2)}, u32[]{:S(2)}) collective-permute-start(bf16[2,256,256]{2,1,0:T(8,128)(2,1)S(1)} %get-tuple-element.50), channel_id=1, source_target_pairs={{0,0},{496,496},{16,32},{32,16},{48,64},{64,48},{80,96},{96,80},{1... | collective-permute-start | bytes 786440 | tf_op jit(solution)/shard_map/ppermute | solution.py:270
  46.0 1.5 %step3_1.1 = (bf16[2,256,256]{2,1,0:T(8,128)(2,1)S(1)}, f32[392,384]{1,0:T(8,128)S(1)}, bf16[64,384]{1,0:T(8,128)(2,1)S(1)}, bf16[64,384]{1,0:T(8,128)(2,1)S(1)}) custom-call(s32[16,128]{1,0:T(8,128)S(1)} %get-tuple-element.30.refs_0_, bf16[1,1,4,2,256,256]{5,4,3,2,1,0:T(8,128)(2,1)S(1)} %copy-done, ...), custom_call_target="tpu_custom_call", output_to_operand_aliasing={{1}: (11, {})} | custom-call | flops 536870912 | bytes 1048576 | tf_op jit(solution)/shard_map/step3_1/pallas_call | solution.py:249
  47.5 5.1 %collective-permute-start.6 = (bf16[64,384]{1,0:T(8,128)(2,1)S(1)}, bf16[64,384]{1,0:T(8,128)(2,1)S(1)}, u32[]{:S(2)}, u32[]{:S(2)}) collective-permute-start(bf16[64,384]{1,0:T(8,128)(2,1)S(1)} %get-tuple-element.55), channel_id=1, source_target_pairs={{0,1},{1,2},{2,3},{3,4},{4,5},{5,6},{6,7},{7,8},{8,9},{9,10},{10,1... | collective-permute-start | bytes 147464 | tf_op jit(solution)/shard_map/ppermute | solution.py:282
  52.6 1.9 %collective-permute-start.7 = (bf16[64,384]{1,0:T(8,128)(2,1)S(1)}, bf16[64,384]{1,0:T(8,128)(2,1)S(1)}, u32[]{:S(2)}, u32[]{:S(2)}) collective-permute-start(bf16[64,384]{1,0:T(8,128)(2,1)S(1)} %get-tuple-element.56), channel_id=1, source_target_pairs={{1,0},{2,1},{3,2},{4,3},{5,4},{6,5},{7,6},{8,7},{9,8},{10,9},{11,1... | collective-permute-start | bytes 147464 | tf_op jit(solution)/shard_map/ppermute | solution.py:282
  54.6 2.2 %all-gather.3 = bf16[4,256,256]{2,1,0:T(8,128)(2,1)S(1)} all-gather(bf16[2,256,256]{2,1,0:T(8,128)(2,1)S(1)} %get-tuple-element.53), channel_id=5, replica_groups={{0,16},{32,48},{64,80},{96,112},{128,144},{160,176},{192,208},{224,240}..., dimensions={0}, use_global_device_ids=true | all-gather | bytes 786432 | tf_op jit(solution)/shard_map/all_gather | solution.py:276
  56.8 1.9 %collective-permute-done.7.from_high = bf16[64,384]{1,0:T(8,128)(2,1)S(1)} collective-permute-done((bf16[64,384]{1,0:T(8,128)(2,1)S(1)}, bf16[64,384]{1,0:T(8,128)(2,1)S(1)}, u32[]{:S(2)}, u32[]{:S(2)}) %collective-permute-start.7) | collective-permute-done | bytes 49184 | tf_op jit(solution)/shard_map/ppermute | solution.py:282
  58.6 1.1 %finish.1 = (f32[1,1,2,256,256]{4,3,2,1,0:T(8,128)}, bf16[1,1,2,256,256]{4,3,2,1,0:T(8,128)(2,1)}, f32[1,256,384]{2,1,0:T(8,128)}) custom-call(bf16[2,256,256]{2,1,0:T(8,128)(2,1)S(1)} %collective-permute-done.4.swapped, bf16[2,2,256,256]{3,2,1,0:T(8,128)(2,1)S(1)} %bitcast.10, bf16[2,256,256]{2,1,0:T(8,128)(2,1)S(1)} %copy-done.6, ...), custom_call_target="tpu_custom_call" | custom-call | tf_op jit(solution)/shard_map/finish/pallas_call | solution.py:249
  (31 shorter events, 0.9 us)
Async XLA Ops:
  0.6 7.2 %copy-start.1 = (bf16[512,512]{1,0:T(8,128)(2,1)S(1)}, bf16[512,512]{1,0:T(8,128)(2,1)}, u32[]{:S(2)}) copy-start(bf16[512,512]{1,0:T(8,128)(2,1)} %constant.9.clone.mt.refs_4_) | copy-start | bytes 1572868
  0.6 7.2 %copy-start.2 = (bf16[512,512]{1,0:T(8,128)(2,1)S(1)}, bf16[512,512]{1,0:T(8,128)(2,1)}, u32[]{:S(2)}) copy-start(bf16[512,512]{1,0:T(8,128)(2,1)} %constant.8.clone.m.refs_3_) | copy-start | bytes 1572868
  0.7 7.2 %copy-start.4 = (f32[256,256]{1,0:T(8,128)S(1)}, f32[256,256]{1,0:T(8,128)}, u32[]{:S(2)}) copy-start(f32[256,256]{1,0:T(8,128)} %constant.11.clone.pi.refs_6_) | copy-start | bytes 786436
  0.7 7.2 %copy-start.5 = (f32[256,256]{1,0:T(8,128)S(1)}, f32[256,256]{1,0:T(8,128)}, u32[]{:S(2)}) copy-start(f32[256,256]{1,0:T(8,128)} %constant.10.clone.pr.refs_5_) | copy-start | bytes 786436
  0.7 1.1 %copy-start.8 = (f32[1,256,384]{2,1,0:T(8,128)S(1)}, f32[1,256,384]{2,1,0:T(8,128)}, u32[]{:S(2)}) copy-start(f32[1,256,384]{2,1,0:T(8,128)} %pot.3) | copy-start | bytes 1179652
  1.8 6.1 %copy-start.9 = (f32[1,256,384]{2,1,0:T(8,128)S(1)}, f32[1,256,384]{2,1,0:T(8,128)}, u32[]{:S(2)}) copy-start(f32[1,256,384]{2,1,0:T(8,128)} %pot.3) | copy-start | bytes 1179652
  1.8 6.1 %copy-start.10 = (bf16[1,1,2,256,256]{4,3,2,1,0:T(8,128)(2,1)S(1)}, bf16[1,1,2,256,256]{4,3,2,1,0:T(8,128)(2,1)}, u32[]{:S(2)}) copy-start(bf16[1,1,2,256,256]{4,3,2,1,0:T(8,128)(2,1)} %adj.1) | copy-start | bytes 786436
  1.8 7.8 %collective-permute-start = (bf16[64,384]{1,0:T(8,128)(2,1)S(1)}, bf16[64,384]{1,0:T(8,128)(2,1)S(1)}, u32[]{:S(2)}, u32[]{:S(2)}) collective-permute-start(bf16[64,384]{1,0:T(8,128)(2,1)S(1)} %get-tuple-element.35), channel_id=1, source_target_pairs={{0,1},{1,2},{2,3},{3,4},{4,5},{5,6},{6,7},{7,8},{8,9},{9,10},{10,1... | collective-permute-start | bytes 147464 | tf_op jit(solution)/shard_map/ppermute | solution.py:282
  5.4 2.4 %copy-start.11 = (s32[1,67,2]{1,2,0:T(2,128)S(1)}, s32[1,67,2]{1,2,0:T(2,128)}, u32[]{:S(2)}) copy-start(s32[1,67,2]{1,2,0:T(2,128)} %param.13) | copy-start | bytes 1612
  5.4 6.8 %collective-permute-start.1 = (bf16[64,384]{1,0:T(8,128)(2,1)S(1)}, bf16[64,384]{1,0:T(8,128)(2,1)S(1)}, u32[]{:S(2)}, u32[]{:S(2)}) collective-permute-start(bf16[64,384]{1,0:T(8,128)(2,1)S(1)} %get-tuple-element.36), channel_id=1, source_target_pairs={{1,0},{2,1},{3,2},{4,3},{5,4},{6,5},{7,6},{8,7},{9,8},{10,9},{11,1... | collective-permute-start | bytes 147464 | tf_op jit(solution)/shard_map/ppermute | solution.py:282
  7.9 4.3 %copy-start = (bf16[1,1,4,2,256,256]{5,4,3,2,1,0:T(8,128)(2,1)S(1)}, bf16[1,1,4,2,256,256]{5,4,3,2,1,0:T(8,128)(2,1)}, u32[]{:S(2)}) copy-start(bf16[1,1,4,2,256,256]{5,4,3,2,1,0:T(8,128)(2,1)} %refs_1_.15) | copy-start | bytes 3145732
  7.9 4.3 %copy-start.3 = (bf16[1,4,256,256]{3,2,1,0:T(8,128)(2,1)S(1)}, bf16[1,4,256,256]{3,2,1,0:T(8,128)(2,1)}, u32[]{:S(2)}) copy-start(bf16[1,4,256,256]{3,2,1,0:T(8,128)(2,1)} %refs_2_.15) | copy-start | bytes 1572868
  7.9 4.3 %copy-start.7 = (f32[1,1,2,256,256]{4,3,2,1,0:T(8,128)S(1)}, f32[1,1,2,256,256]{4,3,2,1,0:T(8,128)}, u32[]{:S(2)}) copy-start(f32[1,1,2,256,256]{4,3,2,1,0:T(8,128)} %refs_9_.3) | copy-start | bytes 1572868
  13.0 13.6 %collective-permute-start.3 = (bf16[2,256,256]{2,1,0:T(8,128)(2,1)S(1)}, bf16[2,256,256]{2,1,0:T(8,128)(2,1)S(1)}, u32[]{:S(2)}, u32[]{:S(2)}) collective-permute-start(bf16[2,256,256]{2,1,0:T(8,128)(2,1)S(1)} %get-tuple-element.43), channel_id=1, source_target_pairs={{0,0},{496,496},{16,32},{32,16},{48,64},{64,48},{80,96},{96,80},{1... | collective-permute-start | bytes 786440 | tf_op jit(solution)/shard_map/ppermute | solution.py:270
  16.8 2.8 %copy-start.6 = (bf16[2,256,256]{2,1,0:T(8,128)(2,1)S(1)}, bf16[2,256,256]{2,1,0:T(8,128)(2,1)}, u32[]{:S(2)}) copy-start(bf16[2,256,256]{2,1,0:T(8,128)(2,1)} %probe.1) | copy-start | bytes 786436
  21.0 14.2 %collective-permute-start.2 = (bf16[2,256,256]{2,1,0:T(8,128)(2,1)S(1)}, bf16[2,256,256]{2,1,0:T(8,128)(2,1)S(1)}, u32[]{:S(2)}, u32[]{:S(2)}) collective-permute-start(bf16[2,256,256]{2,1,0:T(8,128)(2,1)S(1)} %get-tuple-element.42), channel_id=1, source_target_pairs={{0,0},{496,496},{16,32},{32,16},{48,64},{64,48},{80,96},{96,80},{1... | collective-permute-start | bytes 786440 | tf_op jit(solution)/shard_map/ppermute | solution.py:270
  31.6 14.4 %collective-permute-start.5 = (bf16[2,256,256]{2,1,0:T(8,128)(2,1)S(1)}, bf16[2,256,256]{2,1,0:T(8,128)(2,1)S(1)}, u32[]{:S(2)}, u32[]{:S(2)}) collective-permute-start(bf16[2,256,256]{2,1,0:T(8,128)(2,1)S(1)} %get-tuple-element.51), channel_id=1, source_target_pairs={{0,0},{496,496},{16,32},{32,16},{48,64},{64,48},{80,96},{96,80},{1... | collective-permute-start | bytes 786440 | tf_op jit(solution)/shard_map/ppermute | solution.py:270
  40.4 16.3 %collective-permute-start.4 = (bf16[2,256,256]{2,1,0:T(8,128)(2,1)S(1)}, bf16[2,256,256]{2,1,0:T(8,128)(2,1)S(1)}, u32[]{:S(2)}, u32[]{:S(2)}) collective-permute-start(bf16[2,256,256]{2,1,0:T(8,128)(2,1)S(1)} %get-tuple-element.50), channel_id=1, source_target_pairs={{0,0},{496,496},{16,32},{32,16},{48,64},{64,48},{80,96},{96,80},{1... | collective-permute-start | bytes 786440 | tf_op jit(solution)/shard_map/ppermute | solution.py:270
  47.5 9.3 %collective-permute-start.6 = (bf16[64,384]{1,0:T(8,128)(2,1)S(1)}, bf16[64,384]{1,0:T(8,128)(2,1)S(1)}, u32[]{:S(2)}, u32[]{:S(2)}) collective-permute-start(bf16[64,384]{1,0:T(8,128)(2,1)S(1)} %get-tuple-element.55), channel_id=1, source_target_pairs={{0,1},{1,2},{2,3},{3,4},{4,5},{5,6},{6,7},{7,8},{8,9},{9,10},{10,1... | collective-permute-start | bytes 147464 | tf_op jit(solution)/shard_map/ppermute | solution.py:282
  52.6 6.0 %collective-permute-start.7 = (bf16[64,384]{1,0:T(8,128)(2,1)S(1)}, bf16[64,384]{1,0:T(8,128)(2,1)S(1)}, u32[]{:S(2)}, u32[]{:S(2)}) collective-permute-start(bf16[64,384]{1,0:T(8,128)(2,1)S(1)} %get-tuple-element.56), channel_id=1, source_target_pairs={{1,0},{2,1},{3,2},{4,3},{5,4},{6,5},{7,6},{8,7},{9,8},{10,9},{11,1... | collective-permute-start | bytes 147464 | tf_op jit(solution)/shard_map/ppermute | solution.py:282

commit v3 on v2

v3 whole, which is shorter than its diff:
```python
import functools
import math

import jax
import jax.numpy as jnp
import numpy as np
from jax import lax
from jax.experimental import pallas as pl
from jax.experimental.pallas import tpu as pltpu
from jax.sharding import PartitionSpec as P

TICKS = 4
SIGMA = 0.8
DEFOCUS = 6.0
LANES = 128
SUB = 8
F32 = jnp.float32
BF16 = jnp.bfloat16


def halves(n):
    return np.concatenate([np.arange(0, n, 2), np.arange(1, n, 2)])


def dft_matrices(n):
    idx = np.arange(n)
    angle = ((idx[:, None] * idx[None, :]) % n).astype(np.float32) * np.float32(2.0 * math.pi / n)
    scale = np.float32(1.0 / math.sqrt(n))
    cos_t = np.cos(angle) * scale
    sin_t = np.sin(angle) * scale
    both = []
    for odd in range(2):
        c, s = cos_t[: n // 2, odd::2], sin_t[: n // 2, odd::2]
        both.append(np.block([[c, -s], [s, c]]))
    order = (halves(n)[:, None] == idx[None, :]).astype(np.float32)
    return np.stack([*both, both[0].T, both[1].T, order]).astype(BF16)


def propagator(n):
    freq = np.where(np.arange(n) < n // 2, np.arange(n), np.arange(n) - n).astype(np.float32)[halves(n)]
    square = freq[:, None] * freq[:, None] + freq[None, :] * freq[None, :]
    phase = np.float32(-math.pi * DEFOCUS) * square / np.float32(n * n)
    return np.stack([np.cos(phase), np.sin(phase)]).astype(np.float32)


def sin_cos(x):
    mid = 1.2
    y = x - mid
    z = y * y
    s = y * (1.0 + z * (-1.0 / 6 + z * (1.0 / 120 + z * (-1.0 / 5040 + z * (1.0 / 362880)))))
    c = 1.0 + z * (-0.5 + z * (1.0 / 24 + z * (-1.0 / 720 + z * (1.0 / 40320 + z * (-1.0 / 3628800)))))
    cm, sm = math.cos(mid), math.sin(mid)
    return s * cm + c * sm, c * cm - s * sm


def turned(x, back, size, axis):
    own = lax.broadcasted_iota(jnp.int32, x.shape, axis)
    return pltpu.roll(x, lax.rem(size - back, size), axis), own < size - back


def cut(ref, row, col, n):
    base = pl.multiple_of(row // SUB * SUB, SUB)
    groups = n // SUB + 1
    pieces = []
    for j in range(n // LANES + 1):
        x = ref[pl.ds(base, n + SUB), j * LANES : (j + 1) * LANES].reshape(groups, SUB, LANES)
        x, near = turned(x, row - base, SUB, 1)
        x = jnp.where(near[1:], x[:-1], x[1:]).reshape(n, LANES)
        pieces.append(turned(x, col, LANES, 1))
    return jnp.concatenate(
        [jnp.where(here[1], here[0], after[0]) for here, after in zip(pieces[:-1], pieces[1:])], axis=1
    )


def place(ref, row, col, block):
    n = block.shape[0]
    base = pl.multiple_of(row // SUB * SUB, SUB)
    groups = n // SUB
    zero = jnp.zeros((n, LANES), F32)
    pieces = [
        pltpu.roll(block[:, j * LANES : (j + 1) * LANES], lax.rem(col, LANES), 1) for j in range(n // LANES)
    ]
    far = lax.broadcasted_iota(jnp.int32, (n, LANES), 1) >= col
    gap = jnp.zeros((1, SUB, LANES), F32)
    low = lax.broadcasted_iota(jnp.int32, (groups + 1, SUB, LANES), 1) >= row - base
    for j, (before, here) in enumerate(zip([zero] + pieces, pieces + [zero])):
        x = jnp.where(far, here, before).reshape(groups, SUB, LANES)
        x = pltpu.roll(x, row - base, 1)
        x = jnp.where(low, jnp.concatenate([x, gap], 0), jnp.concatenate([gap, x], 0))
        spot = (pl.ds(base, n + SUB), slice(j * LANES, (j + 1) * LANES))
        ref[spot] = ref[spot] + x.reshape(n + SUB, LANES)


def dot(a, b):
    return jnp.dot(a, b, preferred_element_type=F32)


def beside(a, b):
    return jnp.concatenate([a.astype(BF16), b.astype(BF16)], axis=1)


def above(a, b):
    return jnp.concatenate([a.astype(BF16), b.astype(BF16)], axis=0)


def forward(xr, xi, tables):
    h = xr.shape[0] // 2
    xr, xi = xr.astype(F32), xi.astype(F32)
    even = dot(beside(xr[:, :h] + xr[:, h:], xi[:, :h] + xi[:, h:]), tables[0])
    odd = dot(beside(xr[:, :h] - xr[:, h:], xi[:, :h] - xi[:, h:]), tables[1])
    even_sum, even_gap = even[:h] + even[h:], even[:h] - even[h:]
    odd_sum, odd_gap = odd[:h] + odd[h:], odd[:h] - odd[h:]
    rows = []
    for table, e, o in ((2, even_sum, odd_sum), (3, even_gap, odd_gap)):
        rows.append(dot(tables[table], above(beside(e[:, :h], o[:, :h]), beside(e[:, h:], o[:, h:]))))
    return jnp.concatenate([r[:h] for r in rows], 0), jnp.concatenate([r[h:] for r in rows], 0)


def inverse(fr, fi, tables):
    h = fr.shape[0] // 2
    even = dot(beside(fr[:, :h], fi[:, :h]), tables[2])
    odd = dot(beside(fr[:, h:], fi[:, h:]), tables[3])
    low, high = even + odd, even - odd
    rows = []
    for table, at in ((0, slice(0, h)), (1, slice(h, 2 * h))):
        both = above(beside(low[at, :h], high[at, :h]), beside(low[at, h:], high[at, h:]))
        rows.append(dot(tables[table], both))
    even, odd = rows
    low, high = even + odd, even - odd
    return jnp.concatenate([low[:h], high[:h]], 0), jnp.concatenate([low[h:], high[h:]], 0)


def adjoint(lr, li, tables, prop):
    br, bi = forward(lr, li, tables)
    return inverse(br * prop[0] + bi * prop[1], bi * prop[0] - br * prop[1], tables)


def edges_kernel(pot, low, high):
    margin = low.shape[0]
    core = pot.shape[1]
    low[...] = pot[0, core - margin :].astype(BF16)
    high[...] = pot[0, :margin].astype(BF16)


def transmit(v, tr, ti, rows):
    s, c = sin_cos(SIGMA * v)
    tr[rows] = c
    ti[rows] = s


def window_of(section, tick, forward):
    return jnp.where(forward, tick - section + 2 * lax.axis_size("depth") - 1, tick + section)


def first_kernel(spots, pot, corners, tr, ti):
    core = pot.shape[1]
    margin = (tr.shape[0] - SUB - core) // 2
    section = lax.axis_index("depth")
    even = lax.rem(section, 2) == 0
    mate = jnp.where(even, section + 1, section - 1)
    which = lax.broadcasted_iota(jnp.int32, spots.shape, 1)
    windows = [window_of(section, 0, jnp.logical_not(even))]
    for tick in range(TICKS):
        windows += [window_of(section, tick, even), window_of(mate, tick, even)]
    windows[own(TICKS - 1)] = window_of(mate, TICKS - 1, jnp.logical_not(even))
    for i, mb in enumerate(windows):
        chosen = jnp.sum(jnp.where(which == mb, spots[...].astype(F32), 0.0), axis=1, keepdims=True)
        corners[2 * i : 2 * i + 2] = jnp.broadcast_to(chosen.astype(jnp.int32), (2, LANES))
    transmit(pot[0], tr, ti, slice(margin, margin + core))


def corner(corners, which):
    numbers = corners[...]
    return numbers[2 * which, 0], numbers[2 * which + 1, 0]


def own(tick):
    return 1 + 2 * tick


def mates(tick):
    return 2 + 2 * tick


def pack(ref, at, block):
    rows, n = block.shape[0], ref.shape[1]
    block = block.astype(BF16)
    ref[at : at + rows] = block[:, :n]
    ref[at + rows : at + rows + rows // 2, : n // 2] = block[: rows // 2, n:]
    ref[at + rows : at + rows + rows // 2, n // 2 :] = block[rows // 2 :, n:]


def unpack(rows, packed):
    n = packed.shape[1]
    return (
        (slice(0, rows), slice(0, n), packed[:rows]),
        (slice(0, rows // 2), slice(n, n + n // 2), packed[rows:, : n // 2]),
        (slice(rows // 2, rows), slice(n, n + n // 2), packed[rows:, n // 2 :]),
    )


def share_kernel(low, high, pot, saved, tr0, ti0, tr, ti, shared):
    margin = low.shape[0]
    core = pot.shape[1]
    transmit(low[...].astype(F32), tr, ti, slice(0, margin))
    transmit(high[...].astype(F32), tr, ti, slice(margin + core, 2 * margin + core))
    n = shared.shape[1]
    for tick in range(1, TICKS):
        for part in range(2):
            at = (2 * (tick - 1) + part) * n
            shared[at : at + n] = saved[0, 0, tick, part]
    whole = jnp.concatenate([low[...], pot[0].astype(BF16), high[...]], axis=0)
    pack(shared, 2 * (TICKS - 1) * n, whole)


def forward_step(xr, xi, section, tick, spot, tr, ti, intens, tables, prop, far):
    n = far.shape[1]
    wr = cut(tr, *spot, n)
    wi = cut(ti, *spot, n)
    xr, xi = xr.astype(F32), xi.astype(F32)
    br, bi = forward(wr * xr - wi * xi, wr * xi + wi * xr, tables)
    far[0] = br * prop[0] - bi * prop[1]
    far[1] = br * prop[1] + bi * prop[0]

    @pl.when(section == lax.axis_size("depth") - 1)
    def _():
        rows = dot(tables[4], intens[0, tick]).astype(BF16)
        ordered = lax.dot_general(rows, tables[4], (((1,), (1,)), ((), ())), preferred_element_type=F32)
        fr, fi = far[0], far[1]
        excess = fr * fr + fi * fi - ordered
        far[0] = excess * fr
        far[1] = excess * fi

    sr, si = inverse(far[0], far[1], tables)
    return sr.astype(BF16), si.astype(BF16)


def backward_step(lr, li, saved, spot, tr, ti, acc):
    n = lr.shape[0]
    wr = cut(tr, *spot, n)
    wi = cut(ti, *spot, n)
    br = wr * lr + wi * li
    bi = wr * li - wi * lr
    place(acc, *spot, SIGMA * (bi * saved[0].astype(F32) - br * saved[1].astype(F32)))
    return br.astype(BF16), bi.astype(BF16)


def entering(recv, probe, section):
    at_start = section == 0
    return [jnp.where(at_start, probe[part], recv[part]) for part in range(2)]


def first_step_kernel(corners, saved, intens, tables, prop, tr, ti, fwd, adj, out, acc, far):
    section = lax.axis_index("depth")
    even = lax.rem(section, 2) == 0
    spot = corner(corners, 0)
    acc[...] = jnp.zeros(acc.shape, F32)

    @pl.when(jnp.logical_not(even))
    def _():
        x = fwd[0, 0, 0], fwd[0, 0, 1]
        out[0], out[1] = forward_step(*x, section, 0, spot, tr, ti, intens, tables, prop, far)

    @pl.when(even)
    def _():
        theirs = saved[0, 0, 0, 0], saved[0, 0, 0, 1]
        x = adjoint(adj[0, 0, 0], adj[0, 0, 1], tables, prop)
        out[0], out[1] = backward_step(*x, theirs, spot, tr, ti, acc)


def last_step_kernel(corners, intens, tables, prop, mate_tr, mate_ti, shared, recv, probe, acc0, out, acc, packed, far):
    tick = TICKS - 1
    section = lax.axis_index("depth")
    even = lax.rem(section, 2) == 0
    n = far.shape[1]
    spot = corner(corners, own(tick))

    @pl.when(jnp.logical_not(even))
    def _():
        x = entering(recv, probe, section - 1)
        x = forward_step(*x, section - 1, tick, spot, mate_tr, mate_ti, intens, tables, prop, far)
        out[0], out[1] = x

    @pl.when(even)
    def _():
        x = adjoint(recv[0], recv[1], tables, prop)
        at = 2 * (tick - 1) * n
        theirs = shared[at : at + n], shared[at + n : at + 2 * n]
        out[0], out[1] = backward_step(*x, theirs, spot, mate_tr, mate_ti, acc)

    pack(packed, 0, acc[: acc.shape[0] - SUB])


def pair_kernel(tick, fresh, corners, saved, intens, tables, prop, tr, ti, shared, *refs):
    if fresh:
        fwd, adj, _, out, acc, mate_acc, mate_tr, mate_ti, far = refs
    else:
        recv, probe, mate_tr, mate_ti, _, _, out, acc, mate_acc, far = refs
    section = lax.axis_index("depth")
    even = lax.rem(section, 2) == 0
    n = far.shape[1]
    spot, mate_spot = corner(corners, own(tick)), corner(corners, mates(tick + 1))
    if fresh:
        rows = mate_tr.shape[0] - SUB
        for where_rows, where_columns, v in unpack(rows, shared[2 * (TICKS - 1) * n :]):
            s, c = sin_cos(SIGMA * v.astype(F32))
            mate_tr[where_rows, where_columns] = c
            mate_ti[where_rows, where_columns] = s
        mate_acc[...] = jnp.zeros(mate_acc.shape, F32)

    @pl.when(even)
    def _():
        x = (fwd[0, 0, 0], fwd[0, 0, 1]) if fresh else entering(recv, probe, section)
        x = forward_step(*x, section, tick, spot, tr, ti, intens, tables, prop, far)
        x = forward_step(*x, section + 1, tick + 1, mate_spot, mate_tr, mate_ti, intens, tables, prop, far)
        out[0], out[1] = x

    @pl.when(jnp.logical_not(even))
    def _():
        x = (adj[0, 0, 0], adj[0, 0, 1]) if fresh else (recv[0], recv[1])
        x = adjoint(*x, tables, prop)
        x = backward_step(*x, (saved[0, 0, tick, 0], saved[0, 0, tick, 1]), spot, tr, ti, acc)
        x = adjoint(*x, tables, prop)
        at = 2 * tick * n
        theirs = shared[at : at + n], shared[at + n : at + 2 * n]
        x = backward_step(*x, theirs, mate_spot, mate_tr, mate_ti, mate_acc)
        out[0], out[1] = x


def sum_kernel(gathered, acc0, low, high, acc):
    other = 1 - lax.rem(lax.axis_index("depth"), 2)
    rows = acc.shape[0] - SUB
    margin = low.shape[0]
    for where_rows, where_columns, part in unpack(rows, gathered[other]):
        acc[where_rows, where_columns] += part.astype(F32)
    low[...] = acc[:margin].astype(BF16)
    high[...] = acc[rows - margin : rows].astype(BF16)


def waves_kernel(swapped, stayed, probe, wave, adj):
    section = lax.axis_index("depth")
    even = lax.rem(section, 2) == 0

    @pl.when(even)
    def _():
        wave[0, 0] = jnp.where(section == 0, probe[...], swapped[...]).astype(F32)
        adj[0, 0] = stayed[...]

    @pl.when(jnp.logical_not(even))
    def _():
        wave[0, 0] = stayed[...].astype(F32)
        adj[0, 0] = swapped[...]


def fold_kernel(acc, from_low, from_high, grad):
    margin = from_low.shape[0]
    core = grad.shape[1]
    grad[0, :margin] = acc[margin : 2 * margin] + from_low[...].astype(F32)
    grad[0, margin : core - margin] = acc[2 * margin : core]
    grad[0, core - margin :] = acc[core : core + margin] + from_high[...].astype(F32)


VM = pl.BlockSpec(memory_space=pltpu.VMEM)


def call(kernel, name, outs, args, aliases=None, cost=None, scratch=()):
    return pl.pallas_call(
        kernel,
        name=name,
        in_specs=[VM] * len(args),
        out_specs=[VM] * len(outs),
        out_shape=outs,
        scratch_shapes=scratch,
        input_output_aliases=aliases or {},
        compiler_params=pltpu.CompilerParams(vmem_limit_bytes=24 << 20),
        cost_estimate=cost,
    )(*args)


def shape(*dims, dtype=F32):
    return jax.ShapeDtypeStruct(dims, dtype)


def swap_chips(x):
    last = lax.axis_size("depth") - 1
    route = [(0, 0), (last, last)]
    for i in range(1, last, 2):
        route += [(i, i + 1), (i + 1, i)]
    return lax.ppermute(x, "depth", route)


def ring(x):
    last = lax.axis_size("depth") - 1
    route = [(last - 1, last), (1, 0)]
    for i in range(0, last - 1, 2):
        route += [(i, i + 2), (i + 3, i + 1)]
    return lax.ppermute(x, "depth", route)


def cross(x):
    last = lax.axis_size("depth") - 1
    route = [(last - 1, last - 1), (1, 1)]
    for i in range(0, last - 1, 2):
        route += [(i, i + 3), (i + 3, i)]
    return lax.ppermute(x, "depth", route)


def swap_cores(x):
    return lax.ppermute(x, "depth", [(i, i ^ 1) for i in range(lax.axis_size("depth"))])


def gather_chip(x):
    count = lax.axis_size("depth")
    groups = [[i, i + 1] for i in range(0, count, 2)]
    return lax.all_gather(x, "depth", axis_index_groups=groups)


def tile_shift(x, distance):
    devices = range(lax.axis_size("tile"))
    route = [(i - distance, i) for i in devices if i - distance in devices]
    return lax.ppermute(x, "tile", route)


def on_device(potential, probe, positions, intensity, fwd_wave, adj_wave, saved_wave):
    n = probe.shape[1]
    core, cols = potential.shape[1:]
    margin = (cols - core) // 2
    tall = core + 2 * margin + SUB
    spots = positions[0].T
    step_cost = pl.CostEstimate(flops=8 * 2 * n * n * n * 2, bytes_accessed=1 << 20, transcendentals=0)
    pair_cost = pl.CostEstimate(flops=2 * 8 * 2 * n * n * n * 2, bytes_accessed=1 << 20, transcendentals=0)
    edge_cost = pl.CostEstimate(flops=1 << 33, bytes_accessed=1 << 20, transcendentals=0)
    far = [pltpu.VMEM((2, n, n), F32)]
    extent = shape(tall, cols)
    edge = shape(margin, cols, dtype=BF16)
    half = shape(2, n, n, dtype=BF16)

    tables, prop = jnp.asarray(dft_matrices(n)), jnp.asarray(propagator(n))
    low, high = call(edges_kernel, "edges", [edge, edge], (potential,), cost=edge_cost)
    low = tile_shift(low, 1)
    high = tile_shift(high, -1)
    corners, tr, ti = call(
        first_kernel, "first", [shape(4 * TICKS + 8, LANES, dtype=jnp.int32), extent, extent], (spots, potential),
        cost=step_cost,
    )
    packed = (tall - SUB) * 3 // 2
    tr, ti, shared = call(
        share_kernel, "share", [extent] * 2 + [shape(2 * (TICKS - 1) * n + packed, n, dtype=BF16)],
        (low, high, potential, saved_wave, tr, ti), {4: 0, 5: 1},
    )
    shared = swap_cores(shared)
    common = (corners, saved_wave, intensity, tables, prop, tr, ti)
    entry = (fwd_wave, adj_wave)

    b, acc = call(first_step_kernel, "step0", [half, extent], common + entry, cost=step_cost, scratch=far)
    b = swap_chips(b)
    args = (*common, shared, *entry, acc)
    a, acc, mate_acc, mate_tr, mate_ti = call(
        functools.partial(pair_kernel, 0, True), "steps01", [half] + [extent] * 4, args, {len(args) - 1: 1}, pair_cost, far
    )
    a = ring(a)

    def pair(tick, recv, acc, mate_acc):
        args = (*common, shared, recv, probe, mate_tr, mate_ti, acc, mate_acc)
        return call(
            functools.partial(pair_kernel, tick, False), f"steps{tick}{tick + 1}", [half, extent, extent], args,
            {len(args) - 2: 1, len(args) - 1: 2}, pair_cost, far,
        )

    b, acc, mate_acc = pair(1, b, acc, mate_acc)
    b = cross(b)
    a, acc, mate_acc = pair(2, a, acc, mate_acc)
    a = ring(a)
    args = (corners, intensity, tables, prop, mate_tr, mate_ti, shared, b, probe, mate_acc)
    b, mate_acc, mate_sum = call(
        last_step_kernel, "step3", [half, extent, shape(packed, n, dtype=BF16)], args, {len(args) - 1: 1}, step_cost, far
    )
    to_low, to_high, acc = call(sum_kernel, "sum", [edge, edge, extent], (gather_chip(mate_sum), acc), {1: 2})
    from_low = tile_shift(to_high, 1)
    from_high = tile_shift(to_low, -1)
    wave, adj = call(
        waves_kernel, "waves", [shape(1, 1, 2, n, n), shape(1, 1, 2, n, n, dtype=BF16)], (a, b, probe)
    )
    acc, wave, adj = lax.optimization_barrier((acc, wave, adj))
    (grad,) = call(fold_kernel, "fold", [shape(1, core, cols)], (acc, from_low, from_high))
    return wave, adj, grad


def solution(mesh):
    placed = (
        P("depth", "tile", None),
        P(),
        P("tile", None, None),
        P("tile", None, None, None),
        P("depth", "tile", None, None, None),
        P("depth", "tile", None, None, None),
        P("depth", "tile", None, None, None, None),
    )
    return jax.shard_map(
        on_device,
        mesh=mesh,
        in_specs=placed,
        out_specs=(
            P("depth", "tile", None, None, None),
            P("depth", "tile", None, None, None),
            P("depth", "tile", None),
        ),
        check_vma=False,
    )
```

time: 60.1 us -> 58.2 us (0.968)
  the two profiles are of different devices: /device:TPU:274 before, /device:TPU:210 now
where the time goes in v3:
time: 58.2 us; the launch traced here: 57.8 us
  starting transfers between devices  34.6 us (59%)
  Pallas kernels  12.2 us (21%)
  waiting for transfers between devices  6.81 us (12%)
  blocking collectives  2.23 us (4%)
  local copies, waits for them, and re-layouts  1.03 us (2%)
  between operations  0.92 us (2%)
    ppermute x4, starting transfers between devices, tile_shift(): return lax.ppermute(x, 'tile', route)  13 us
    pallas_call x11, Pallas kernels, call(): pl.pallas_call(kernel, name=name, in_specs=[VM] * len(args), out_specs=[V...  12.2 us
    ppermute x2, starting transfers between devices, ring(): return lax.ppermute(x, 'depth', route)  11.2 us
    ppermute x4, waiting for transfers between devices, tile_shift(): return lax.ppermute(x, 'tile', route)  6.79 us
    ppermute x1, starting transfers between devices, cross(): return lax.ppermute(x, 'depth', route)  5.05 us
    ppermute x1, starting transfers between devices, swap_chips(): return lax.ppermute(x, 'depth', route)  3.23 us
    all_gather x1, blocking collectives, gather_chip(): return lax.all_gather(x, 'depth', axis_index_groups=groups)  2.23 us
    ppermute x1, starting transfers between devices, swap_cores(): lax.ppermute(x, 'depth', [(i, i ^ 1) for i in range(lax.axis_size('depth'...  2.05 us
  transfers between devices with their start and end apart: 9, of which 2 were waited for; matrix products, arithmetic and copies ran while one was open for 0% of the time, Pallas kernels for 19%

profile of v3, /device:TPU:210, one launch (start us, length us, event | category | flops | bytes accessed | tf_op | source)
XLA Modules:
  0.0 57.8 jit_solution(10049939164985766885)
XLA Ops:
  0.6 1.0 %copy-done.7 = f32[1,256,384]{2,1,0:T(8,128)S(1)} copy-done((f32[1,256,384]{2,1,0:T(8,128)S(1)}, f32[1,256,384]{2,1,0:T(8,128)}, u32[]{:S(2)}) %copy-start.7) | copy-done | bytes 393240
  1.7 3.6 %collective-permute-start = (bf16[64,384]{1,0:T(8,128)(2,1)S(1)}, bf16[64,384]{1,0:T(8,128)(2,1)S(1)}, u32[]{:S(2)}, u32[]{:S(2)}) collective-permute-start(bf16[64,384]{1,0:T(8,128)(2,1)S(1)} %get-tuple-element.35), channel_id=1, source_target_pairs={{0,1},{1,2},{2,3},{3,4},{4,5},{5,6},{6,7},{7,8},{8,9},{9,10},{10,1... | collective-permute-start | bytes 147464 | tf_op jit(solution)/shard_map/ppermute | solution.py:421
  5.3 2.4 %collective-permute-start.1 = (bf16[64,384]{1,0:T(8,128)(2,1)S(1)}, bf16[64,384]{1,0:T(8,128)(2,1)S(1)}, u32[]{:S(2)}, u32[]{:S(2)}) collective-permute-start(bf16[64,384]{1,0:T(8,128)(2,1)S(1)} %get-tuple-element.36), channel_id=1, source_target_pairs={{1,0},{2,1},{3,2},{4,3},{5,4},{6,5},{7,6},{8,7},{9,8},{10,9},{11,1... | collective-permute-start | bytes 147464 | tf_op jit(solution)/shard_map/ppermute | solution.py:421
  7.7 0.7 %first.1 = (s32[24,128]{1,0:T(8,128)S(1)}, f32[392,384]{1,0:T(8,128)S(1)}, f32[392,384]{1,0:T(8,128)S(1)}) custom-call(s32[2,67]{1,0:T(2,128)S(1)} %bitcast.5, f32[1,256,384]{2,1,0:T(8,128)S(1)} %copy-done.8), custom_call_target="tpu_custom_call" | custom-call | flops 536870912 | bytes 1048576 | tf_op jit(solution)/shard_map/first/pallas_call | solution.py:367
  8.3 3.7 %collective-permute-done.1.high = bf16[64,384]{1,0:T(8,128)(2,1)S(1)} collective-permute-done((bf16[64,384]{1,0:T(8,128)(2,1)S(1)}, bf16[64,384]{1,0:T(8,128)(2,1)S(1)}, u32[]{:S(2)}, u32[]{:S(2)}) %collective-permute-start.1) | collective-permute-done | bytes 49184 | tf_op jit(solution)/shard_map/ppermute | solution.py:421
  12.1 0.0 copy-start.6
  12.1 0.3 share.1
  12.3 2.1 %collective-permute-start.2 = (bf16[2112,256]{1,0:T(8,128)(2,1)S(1)}, bf16[2112,256]{1,0:T(8,128)(2,1)S(1)}, u32[]{:S(2)}, u32[]{:S(2)}) collective-permute-start(bf16[2112,256]{1,0:T(8,128)(2,1)S(1)} %get-tuple-element.41), channel_id=1, source_target_pairs={{0,16},{16,0},{32,48},{48,32},{64,80},{80,64},{96,112},{112,96},{1... | collective-permute-start | bytes 3244040 | tf_op jit(solution)/shard_map/ppermute | solution.py:409
  14.4 1.2 %step0.1 = (bf16[2,256,256]{2,1,0:T(8,128)(2,1)S(1)}, f32[392,384]{1,0:T(8,128)S(1)}) custom-call(s32[24,128]{1,0:T(8,128)S(1)} %get-tuple-element.34.corners, bf16[1,1,4,2,256,256]{5,4,3,2,1,0:T(8,128)(2,1)S(1)} %copy-done, bf16[1,4,256,256]{3,2,1,0:T(8,128)(2,1)S(1)} %copy-done.2, bf16[5,256,256]{2,1,0:T(8,128)(2,1)S(1)} %copy-done.1, ...), custom_call_target="tpu_custom_call" | custom-call | flops 536870912 | bytes 1048576 | tf_op jit(solution)/shard_map/step0/pallas_call | solution.py:367
  15.6 3.2 %collective-permute-start.3 = (bf16[2,256,256]{2,1,0:T(8,128)(2,1)S(1)}, bf16[2,256,256]{2,1,0:T(8,128)(2,1)S(1)}, u32[]{:S(2)}, u32[]{:S(2)}) collective-permute-start(bf16[2,256,256]{2,1,0:T(8,128)(2,1)S(1)} %get-tuple-element.45), channel_id=1, source_target_pairs={{0,0},{496,496},{16,32},{32,16},{48,64},{64,48},{80,96},{96,80},{1... | collective-permute-start | bytes 786440 | tf_op jit(solution)/shard_map/ppermute | solution.py:389
  18.9 2.9 %steps01.1 = (bf16[2,256,256]{2,1,0:T(8,128)(2,1)S(1)}, f32[392,384]{1,0:T(8,128)S(1)}, f32[392,384]{1,0:T(8,128)S(1)}, f32[392,384]{1,0:T(8,128)S(1)}, f32[392,384]{1,0:T(8,128)S(1)}) custom-call(s32[24,128]{1,0:T(8,128)S(1)} %get-tuple-element.34.corners, bf16[1,1,4,2,256,256]{5,4,3,2,1,0:T(8,128)(2,1)S(1)} %copy-done, ...), custom_call_target="tpu_custom_call", output_to_operand_aliasing={{1}: (10, {})} | custom-call | flops 1073741824 | bytes 1048576 | tf_op jit(solution)/shard_map/steps01/pallas_call | solution.py:367
  21.8 4.2 %collective-permute-start.5 = (bf16[2,256,256]{2,1,0:T(8,128)(2,1)S(1)}, bf16[2,256,256]{2,1,0:T(8,128)(2,1)S(1)}, u32[]{:S(2)}, u32[]{:S(2)}) collective-permute-start(bf16[2,256,256]{2,1,0:T(8,128)(2,1)S(1)} %get-tuple-element.49), channel_id=1, source_target_pairs={{480,496},{16,0},{0,32},{48,16},{32,64},{80,48},{64,96},{112,80},{... | collective-permute-start | bytes 786440 | tf_op jit(solution)/shard_map/ppermute | solution.py:397
  26.1 2.0 %steps12.1 = (bf16[2,256,256]{2,1,0:T(8,128)(2,1)S(1)}, f32[392,384]{1,0:T(8,128)S(1)}, f32[392,384]{1,0:T(8,128)S(1)}) custom-call(s32[24,128]{1,0:T(8,128)S(1)} %get-tuple-element.34.corners, bf16[1,1,4,2,256,256]{5,4,3,2,1,0:T(8,128)(2,1)S(1)} %copy-done, bf16[1,4,256,256]{3,2,1,0:T(8,128)(2,1)S(1)} %copy-done.2, ...), custom_call_target="tpu_custom_call", output_to_operand_aliasing={{1}: (12, {}), {2}: (13, {})} | custom-call | flops 1073741824 | bytes 1048576 | tf_op jit(solution)/shard_map/steps12/pallas_call | solution.py:367
  28.1 5.0 %collective-permute-start.4 = (bf16[2,256,256]{2,1,0:T(8,128)(2,1)S(1)}, bf16[2,256,256]{2,1,0:T(8,128)(2,1)S(1)}, u32[]{:S(2)}, u32[]{:S(2)}) collective-permute-start(bf16[2,256,256]{2,1,0:T(8,128)(2,1)S(1)} %get-tuple-element.48), channel_id=1, source_target_pairs={{480,480},{16,16},{0,48},{48,0},{32,80},{80,32},{64,112},{112,64},... | collective-permute-start | bytes 786440 | tf_op jit(solution)/shard_map/ppermute | solution.py:405
  33.2 2.2 %steps23.1 = (bf16[2,256,256]{2,1,0:T(8,128)(2,1)S(1)}, f32[392,384]{1,0:T(8,128)S(1)}, f32[392,384]{1,0:T(8,128)S(1)}) custom-call(s32[24,128]{1,0:T(8,128)S(1)} %get-tuple-element.34.corners, bf16[1,1,4,2,256,256]{5,4,3,2,1,0:T(8,128)(2,1)S(1)} %copy-done, bf16[1,4,256,256]{3,2,1,0:T(8,128)(2,1)S(1)} %copy-done.2, ...), custom_call_target="tpu_custom_call", output_to_operand_aliasing={{1}: (12, {}), {2}: (13, {})} | custom-call | flops 1073741824 | bytes 1048576 | tf_op jit(solution)/shard_map/steps23/pallas_call | solution.py:367
  35.4 7.0 %collective-permute-start.6 = (bf16[2,256,256]{2,1,0:T(8,128)(2,1)S(1)}, bf16[2,256,256]{2,1,0:T(8,128)(2,1)S(1)}, u32[]{:S(2)}, u32[]{:S(2)}) collective-permute-start(bf16[2,256,256]{2,1,0:T(8,128)(2,1)S(1)} %get-tuple-element.56), channel_id=1, source_target_pairs={{480,496},{16,0},{0,32},{48,16},{32,64},{80,48},{64,96},{112,80},{... | collective-permute-start | bytes 786440 | tf_op jit(solution)/shard_map/ppermute | solution.py:397
  42.4 1.2 %step3.1 = (bf16[2,256,256]{2,1,0:T(8,128)(2,1)S(1)}, f32[392,384]{1,0:T(8,128)S(1)}, bf16[576,256]{1,0:T(8,128)(2,1)S(1)}) custom-call(s32[24,128]{1,0:T(8,128)S(1)} %get-tuple-element.34.corners, bf16[1,4,256,256]{3,2,1,0:T(8,128)(2,1)S(1)} %copy-done.2, bf16[5,256,256]{2,1,0:T(8,128)(2,1)S(1)} %copy-done.1, ...), custom_call_target="tpu_custom_call", output_to_operand_aliasing={{1}: (9, {})} | custom-call | flops 536870912 | bytes 1048576 | tf_op jit(solution)/shard_map/step3/pallas_call | solution.py:367
  43.6 2.2 %all-gather = bf16[1152,256]{1,0:T(8,128)(2,1)S(1)} all-gather(bf16[576,256]{1,0:T(8,128)(2,1)S(1)} %get-tuple-element.53), channel_id=2, replica_groups={{0,16},{32,48},{64,80},{96,112},{128,144},{160,176},{192,208},{224,240}..., dimensions={0}, use_global_device_ids=true | all-gather | bytes 884736 | tf_op jit(solution)/shard_map/all_gather | solution.py:415
  45.8 0.1 sum.1
  45.9 5.1 %collective-permute-start.7 = (bf16[64,384]{1,0:T(8,128)(2,1)S(1)}, bf16[64,384]{1,0:T(8,128)(2,1)S(1)}, u32[]{:S(2)}, u32[]{:S(2)}) collective-permute-start(bf16[64,384]{1,0:T(8,128)(2,1)S(1)} %get-tuple-element.63), channel_id=1, source_target_pairs={{0,1},{1,2},{2,3},{3,4},{4,5},{5,6},{6,7},{7,8},{8,9},{9,10},{10,1... | collective-permute-start | bytes 147464 | tf_op jit(solution)/shard_map/ppermute | solution.py:421
  51.1 1.9 %collective-permute-start.8 = (bf16[64,384]{1,0:T(8,128)(2,1)S(1)}, bf16[64,384]{1,0:T(8,128)(2,1)S(1)}, u32[]{:S(2)}, u32[]{:S(2)}) collective-permute-start(bf16[64,384]{1,0:T(8,128)(2,1)S(1)} %get-tuple-element.64), channel_id=1, source_target_pairs={{1,0},{2,1},{3,2},{4,3},{5,4},{6,5},{7,6},{8,7},{9,8},{10,9},{11,1... | collective-permute-start | bytes 147464 | tf_op jit(solution)/shard_map/ppermute | solution.py:421
  53.0 1.0 %waves.1 = (f32[1,1,2,256,256]{4,3,2,1,0:T(8,128)}, bf16[1,1,2,256,256]{4,3,2,1,0:T(8,128)(2,1)}) custom-call(bf16[2,256,256]{2,1,0:T(8,128)(2,1)S(1)} %collective-permute-done.6.swapped, bf16[2,256,256]{2,1,0:T(8,128)(2,1)S(1)} %get-tuple-element.57.stayed, bf16[2,256,256]{2,1,0:T(8,128)(2,1)S(1)} %copy-done.4), custom_call_target="tpu_custom_call" | custom-call | tf_op jit(solution)/shard_map/waves/pallas_call | solution.py:367
  53.9 3.1 %collective-permute-done.8.from_high = bf16[64,384]{1,0:T(8,128)(2,1)S(1)} collective-permute-done((bf16[64,384]{1,0:T(8,128)(2,1)S(1)}, bf16[64,384]{1,0:T(8,128)(2,1)S(1)}, u32[]{:S(2)}, u32[]{:S(2)}) %collective-permute-start.8) | collective-permute-done | bytes 49184 | tf_op jit(solution)/shard_map/ppermute | solution.py:421
  57.0 0.8 %fold.1 = f32[1,256,384]{2,1,0:T(8,128)} custom-call(f32[392,384]{1,0:T(8,128)S(1)} %get-tuple-element.62.acc, bf16[64,384]{1,0:T(8,128)(2,1)S(1)} %collective-permute-done.7.from_low, bf16[64,384]{1,0:T(8,128)(2,1)S(1)} %collective-permute-done.8.from_high), custom_call_target="tpu_custom_call" | custom-call | tf_op jit(solution)/shard_map/fold/pallas_call | solution.py:367
  (26 shorter events, 0.1 us)
Async XLA Ops:
  0.6 1.0 %copy-start.7 = (f32[1,256,384]{2,1,0:T(8,128)S(1)}, f32[1,256,384]{2,1,0:T(8,128)}, u32[]{:S(2)}) copy-start(f32[1,256,384]{2,1,0:T(8,128)} %pot.5) | copy-start | bytes 1179652
  1.6 6.0 %copy-start.8 = (f32[1,256,384]{2,1,0:T(8,128)S(1)}, f32[1,256,384]{2,1,0:T(8,128)}, u32[]{:S(2)}) copy-start(f32[1,256,384]{2,1,0:T(8,128)} %pot.5) | copy-start | bytes 1179652
  1.6 6.0 %copy-start.9 = (s32[1,67,2]{1,2,0:T(2,128)S(1)}, s32[1,67,2]{1,2,0:T(2,128)}, u32[]{:S(2)}) copy-start(s32[1,67,2]{1,2,0:T(2,128)} %param.11) | copy-start | bytes 1612
  1.6 10.4 %copy-start = (bf16[1,1,4,2,256,256]{5,4,3,2,1,0:T(8,128)(2,1)S(1)}, bf16[1,1,4,2,256,256]{5,4,3,2,1,0:T(8,128)(2,1)}, u32[]{:S(2)}) copy-start(bf16[1,1,4,2,256,256]{5,4,3,2,1,0:T(8,128)(2,1)} %saved.9) | copy-start | bytes 3145732
  1.7 6.7 %collective-permute-start = (bf16[64,384]{1,0:T(8,128)(2,1)S(1)}, bf16[64,384]{1,0:T(8,128)(2,1)S(1)}, u32[]{:S(2)}, u32[]{:S(2)}) collective-permute-start(bf16[64,384]{1,0:T(8,128)(2,1)S(1)} %get-tuple-element.35), channel_id=1, source_target_pairs={{0,1},{1,2},{2,3},{3,4},{4,5},{5,6},{6,7},{7,8},{8,9},{9,10},{10,1... | collective-permute-start | bytes 147464 | tf_op jit(solution)/shard_map/ppermute | solution.py:421
  5.3 6.8 %collective-permute-start.1 = (bf16[64,384]{1,0:T(8,128)(2,1)S(1)}, bf16[64,384]{1,0:T(8,128)(2,1)S(1)}, u32[]{:S(2)}, u32[]{:S(2)}) collective-permute-start(bf16[64,384]{1,0:T(8,128)(2,1)S(1)} %get-tuple-element.36), channel_id=1, source_target_pairs={{1,0},{2,1},{3,2},{4,3},{5,4},{6,5},{7,6},{8,7},{9,8},{10,9},{11,1... | collective-permute-start | bytes 147464 | tf_op jit(solution)/shard_map/ppermute | solution.py:421
  12.0 2.4 %copy-start.1 = (bf16[5,256,256]{2,1,0:T(8,128)(2,1)S(1)}, bf16[5,256,256]{2,1,0:T(8,128)(2,1)}, u32[]{:S(2)}) copy-start(bf16[5,256,256]{2,1,0:T(8,128)(2,1)} %constant.4.clone.tables) | copy-start | bytes 1966084
  12.0 2.4 %copy-start.2 = (bf16[1,4,256,256]{3,2,1,0:T(8,128)(2,1)S(1)}, bf16[1,4,256,256]{3,2,1,0:T(8,128)(2,1)}, u32[]{:S(2)}) copy-start(bf16[1,4,256,256]{3,2,1,0:T(8,128)(2,1)} %intens.9) | copy-start | bytes 1572868
  12.0 2.4 %copy-start.3 = (f32[2,256,256]{2,1,0:T(8,128)S(1)}, f32[2,256,256]{2,1,0:T(8,128)}, u32[]{:S(2)}) copy-start(f32[2,256,256]{2,1,0:T(8,128)} %constant.5.clone.prop) | copy-start | bytes 1572868
  12.1 2.4 %copy-start.5 = (f32[1,1,2,256,256]{4,3,2,1,0:T(8,128)S(1)}, f32[1,1,2,256,256]{4,3,2,1,0:T(8,128)}, u32[]{:S(2)}) copy-start(f32[1,1,2,256,256]{4,3,2,1,0:T(8,128)} %refs_0_.1) | copy-start | bytes 1572868
  12.1 2.4 %copy-start.6 = (bf16[1,1,2,256,256]{4,3,2,1,0:T(8,128)(2,1)S(1)}, bf16[1,1,2,256,256]{4,3,2,1,0:T(8,128)(2,1)}, u32[]{:S(2)}) copy-start(bf16[1,1,2,256,256]{4,3,2,1,0:T(8,128)(2,1)} %refs_1_.3) | copy-start | bytes 786436
  12.3 6.5 %collective-permute-start.2 = (bf16[2112,256]{1,0:T(8,128)(2,1)S(1)}, bf16[2112,256]{1,0:T(8,128)(2,1)S(1)}, u32[]{:S(2)}, u32[]{:S(2)}) collective-permute-start(bf16[2112,256]{1,0:T(8,128)(2,1)S(1)} %get-tuple-element.41), channel_id=1, source_target_pairs={{0,16},{16,0},{32,48},{48,32},{64,80},{80,64},{96,112},{112,96},{1... | collective-permute-start | bytes 3244040 | tf_op jit(solution)/shard_map/ppermute | solution.py:409
  15.6 10.4 %collective-permute-start.3 = (bf16[2,256,256]{2,1,0:T(8,128)(2,1)S(1)}, bf16[2,256,256]{2,1,0:T(8,128)(2,1)S(1)}, u32[]{:S(2)}, u32[]{:S(2)}) collective-permute-start(bf16[2,256,256]{2,1,0:T(8,128)(2,1)S(1)} %get-tuple-element.45), channel_id=1, source_target_pairs={{0,0},{496,496},{16,32},{32,16},{48,64},{64,48},{80,96},{96,80},{1... | collective-permute-start | bytes 786440 | tf_op jit(solution)/shard_map/ppermute | solution.py:389
  18.9 7.2 %copy-start.4 = (bf16[2,256,256]{2,1,0:T(8,128)(2,1)S(1)}, bf16[2,256,256]{2,1,0:T(8,128)(2,1)}, u32[]{:S(2)}) copy-start(bf16[2,256,256]{2,1,0:T(8,128)(2,1)} %probe.3) | copy-start | bytes 786436
  21.8 11.4 %collective-permute-start.5 = (bf16[2,256,256]{2,1,0:T(8,128)(2,1)S(1)}, bf16[2,256,256]{2,1,0:T(8,128)(2,1)S(1)}, u32[]{:S(2)}, u32[]{:S(2)}) collective-permute-start(bf16[2,256,256]{2,1,0:T(8,128)(2,1)S(1)} %get-tuple-element.49), channel_id=1, source_target_pairs={{480,496},{16,0},{0,32},{48,16},{32,64},{80,48},{64,96},{112,80},{... | collective-permute-start | bytes 786440 | tf_op jit(solution)/shard_map/ppermute | solution.py:397
  28.1 14.3 %collective-permute-start.4 = (bf16[2,256,256]{2,1,0:T(8,128)(2,1)S(1)}, bf16[2,256,256]{2,1,0:T(8,128)(2,1)S(1)}, u32[]{:S(2)}, u32[]{:S(2)}) collective-permute-start(bf16[2,256,256]{2,1,0:T(8,128)(2,1)S(1)} %get-tuple-element.48), channel_id=1, source_target_pairs={{480,480},{16,16},{0,48},{48,0},{32,80},{80,32},{64,112},{112,64},... | collective-permute-start | bytes 786440 | tf_op jit(solution)/shard_map/ppermute | solution.py:405
  35.4 17.6 %collective-permute-start.6 = (bf16[2,256,256]{2,1,0:T(8,128)(2,1)S(1)}, bf16[2,256,256]{2,1,0:T(8,128)(2,1)S(1)}, u32[]{:S(2)}, u32[]{:S(2)}) collective-permute-start(bf16[2,256,256]{2,1,0:T(8,128)(2,1)S(1)} %get-tuple-element.56), channel_id=1, source_target_pairs={{480,496},{16,0},{0,32},{48,16},{32,64},{80,48},{64,96},{112,80},{... | collective-permute-start | bytes 786440 | tf_op jit(solution)/shard_map/ppermute | solution.py:397
  45.9 8.0 %collective-permute-start.7 = (bf16[64,384]{1,0:T(8,128)(2,1)S(1)}, bf16[64,384]{1,0:T(8,128)(2,1)S(1)}, u32[]{:S(2)}, u32[]{:S(2)}) collective-permute-start(bf16[64,384]{1,0:T(8,128)(2,1)S(1)} %get-tuple-element.63), channel_id=1, source_target_pairs={{0,1},{1,2},{2,3},{3,4},{4,5},{5,6},{6,7},{7,8},{8,9},{9,10},{10,1... | collective-permute-start | bytes 147464 | tf_op jit(solution)/shard_map/ppermute | solution.py:421
  51.1 6.0 %collective-permute-start.8 = (bf16[64,384]{1,0:T(8,128)(2,1)S(1)}, bf16[64,384]{1,0:T(8,128)(2,1)S(1)}, u32[]{:S(2)}, u32[]{:S(2)}) collective-permute-start(bf16[64,384]{1,0:T(8,128)(2,1)S(1)} %get-tuple-element.64), channel_id=1, source_target_pairs={{1,0},{2,1},{3,2},{4,3},{5,4},{6,5},{7,6},{8,7},{9,8},{10,9},{11,1... | collective-permute-start | bytes 147464 | tf_op jit(solution)/shard_map/ppermute | solution.py:421

commit v4 on v3

--- a/solution.py
+++ b/solution.py
@@ -135,11 +135,17 @@
     return inverse(br * prop[0] + bi * prop[1], bi * prop[0] - br * prop[1], tables)
 
 
-def edges_kernel(pot, low, high):
-    margin = low.shape[0]
+def odd_tile():
+    return lax.rem(lax.axis_index("tile"), 2) == 1
+
+
+def edges_kernel(pot, inner, outer):
+    margin = inner.shape[0]
     core = pot.shape[1]
-    low[...] = pot[0, core - margin :].astype(BF16)
-    high[...] = pot[0, :margin].astype(BF16)
+    low = pot[0, :margin].astype(BF16)
+    high = pot[0, core - margin :].astype(BF16)
+    inner[...] = jnp.where(odd_tile(), high, low)
+    outer[...] = jnp.where(odd_tile(), low, high)
 
 
 def transmit(v, tr, ti, rows):
@@ -199,17 +205,19 @@
     )
 
 
-def share_kernel(low, high, pot, saved, tr0, ti0, tr, ti, shared):
-    margin = low.shape[0]
+def share_kernel(inner, outer, pot, saved, tr0, ti0, tr, ti, shared):
+    margin = inner.shape[0]
     core = pot.shape[1]
-    transmit(low[...].astype(F32), tr, ti, slice(0, margin))
-    transmit(high[...].astype(F32), tr, ti, slice(margin + core, 2 * margin + core))
+    low = jnp.where(odd_tile(), outer[...], inner[...])
+    high = jnp.where(odd_tile(), inner[...], outer[...])
+    transmit(low.astype(F32), tr, ti, slice(0, margin))
+    transmit(high.astype(F32), tr, ti, slice(margin + core, 2 * margin + core))
     n = shared.shape[1]
     for tick in range(1, TICKS):
         for part in range(2):
             at = (2 * (tick - 1) + part) * n
             shared[at : at + n] = saved[0, 0, tick, part]
-    whole = jnp.concatenate([low[...], pot[0].astype(BF16), high[...]], axis=0)
+    whole = jnp.concatenate([low, pot[0].astype(BF16), high], axis=0)
     pack(shared, 2 * (TICKS - 1) * n, whole)
 
 
@@ -327,14 +335,16 @@
         out[0], out[1] = x
 
 
-def sum_kernel(gathered, acc0, low, high, acc):
+def sum_kernel(gathered, acc0, inner, outer, acc):
     other = 1 - lax.rem(lax.axis_index("depth"), 2)
     rows = acc.shape[0] - SUB
-    margin = low.shape[0]
+    margin = inner.shape[0]
     for where_rows, where_columns, part in unpack(rows, gathered[other]):
         acc[where_rows, where_columns] += part.astype(F32)
-    low[...] = acc[:margin].astype(BF16)
-    high[...] = acc[rows - margin : rows].astype(BF16)
+    low = acc[:margin].astype(BF16)
+    high = acc[rows - margin : rows].astype(BF16)
+    inner[...] = jnp.where(odd_tile(), high, low)
+    outer[...] = jnp.where(odd_tile(), low, high)
 
 
 def waves_kernel(swapped, stayed, probe, wave, adj):
@@ -352,12 +362,14 @@
         adj[0, 0] = swapped[...]
 
 
-def fold_kernel(acc, from_low, from_high, grad):
-    margin = from_low.shape[0]
+def fold_kernel(acc, inner, outer, grad):
+    margin = inner.shape[0]
     core = grad.shape[1]
-    grad[0, :margin] = acc[margin : 2 * margin] + from_low[...].astype(F32)
+    from_low = jnp.where(odd_tile(), outer[...], inner[...])
+    from_high = jnp.where(odd_tile(), inner[...], outer[...])
+    grad[0, :margin] = acc[margin : 2 * margin] + from_low.astype(F32)
     grad[0, margin : core - margin] = acc[2 * margin : core]
-    grad[0, core - margin :] = acc[core : core + margin] + from_high[...].astype(F32)
+    grad[0, core - margin :] = acc[core : core + margin] + from_high.astype(F32)
 
 
 VM = pl.BlockSpec(memory_space=pltpu.VMEM)
@@ -415,9 +427,10 @@
     return lax.all_gather(x, "depth", axis_index_groups=groups)
 
 
-def tile_shift(x, distance):
-    devices = range(lax.axis_size("tile"))
-    route = [(i - distance, i) for i in devices if i - distance in devices]
+def swap_tiles(x, first):
+    route = []
+    for i in range(first, lax.axis_size("tile") - 1, 2):
+        route += [(i, i + 1), (i + 1, i)]
     return lax.ppermute(x, "tile", route)
 
 
@@ -436,9 +449,9 @@
     half = shape(2, n, n, dtype=BF16)
 
     tables, prop = jnp.asarray(dft_matrices(n)), jnp.asarray(propagator(n))
-    low, high = call(edges_kernel, "edges", [edge, edge], (potential,), cost=edge_cost)
-    low = tile_shift(low, 1)
-    high = tile_shift(high, -1)
+    inner, outer = call(edges_kernel, "edges", [edge, edge], (potential,), cost=edge_cost)
+    outer = swap_tiles(outer, 0)
+    inner = swap_tiles(inner, 1)
     corners, tr, ti = call(
         first_kernel, "first", [shape(4 * TICKS + 8, LANES, dtype=jnp.int32), extent, extent], (spots, potential),
         cost=step_cost,
@@ -446,7 +459,7 @@
     packed = (tall - SUB) * 3 // 2
     tr, ti, shared = call(
         share_kernel, "share", [extent] * 2 + [shape(2 * (TICKS - 1) * n + packed, n, dtype=BF16)],
-        (low, high, potential, saved_wave, tr, ti), {4: 0, 5: 1},
+        (inner, outer, potential, saved_wave, tr, ti), {4: 0, 5: 1},
     )
     shared = swap_cores(shared)
     common = (corners, saved_wave, intensity, tables, prop, tr, ti)
@@ -475,14 +488,14 @@
     b, mate_acc, mate_sum = call(
         last_step_kernel, "step3", [half, extent, shape(packed, n, dtype=BF16)], args, {len(args) - 1: 1}, step_cost, far
     )
-    to_low, to_high, acc = call(sum_kernel, "sum", [edge, edge, extent], (gather_chip(mate_sum), acc), {1: 2})
-    from_low = tile_shift(to_high, 1)
-    from_high = tile_shift(to_low, -1)
+    inner, outer, acc = call(sum_kernel, "sum", [edge, edge, extent], (gather_chip(mate_sum), acc), {1: 2})
+    outer = swap_tiles(outer, 0)
+    inner = swap_tiles(inner, 1)
     wave, adj = call(
         waves_kernel, "waves", [shape(1, 1, 2, n, n), shape(1, 1, 2, n, n, dtype=BF16)], (a, b, probe)
     )
     acc, wave, adj = lax.optimization_barrier((acc, wave, adj))
-    (grad,) = call(fold_kernel, "fold", [shape(1, core, cols)], (acc, from_low, from_high))
+    (grad,) = call(fold_kernel, "fold", [shape(1, core, cols)], (acc, inner, outer))
     return wave, adj, grad
 
 

time: 58.2 us -> 57 us (0.979)
  the two profiles are of different devices: /device:TPU:210 before, /device:TPU:198 now
where the time goes in v4:
time: 57 us; the launch traced here: 56.6 us
  starting transfers between devices  34.8 us (61%)
  Pallas kernels  12.3 us (22%)
  waiting for transfers between devices  5.4 us (9%)
  blocking collectives  2.23 us (4%)
  local copies, waits for them, and re-layouts  1.03 us (2%)
  between operations  0.92 us (2%)
    ppermute x4, starting transfers between devices, swap_tiles(): return lax.ppermute(x, 'tile', route)  13.3 us
    pallas_call x11, Pallas kernels, call(): pl.pallas_call(kernel, name=name, in_specs=[VM] * len(args), out_specs=[V...  12.3 us
    ppermute x2, starting transfers between devices, ring(): return lax.ppermute(x, 'depth', route)  10.7 us
    ppermute x1, starting transfers between devices, cross(): return lax.ppermute(x, 'depth', route)  5.63 us
    ppermute x4, waiting for transfers between devices, swap_tiles(): return lax.ppermute(x, 'tile', route)  5.39 us
    ppermute x1, starting transfers between devices, swap_chips(): return lax.ppermute(x, 'depth', route)  3.13 us
    all_gather x1, blocking collectives, gather_chip(): return lax.all_gather(x, 'depth', axis_index_groups=groups)  2.23 us
    ppermute x1, starting transfers between devices, swap_cores(): lax.ppermute(x, 'depth', [(i, i ^ 1) for i in range(lax.axis_size('depth'...  2.05 us
  transfers between devices with their start and end apart: 9, of which 3 were waited for; matrix products, arithmetic and copies ran while one was open for 0% of the time, Pallas kernels for 20%

profile of v4, /device:TPU:198, one launch (start us, length us, event | category | flops | bytes accessed | tf_op | source)
XLA Modules:
  0.0 56.6 jit_solution(652221547901894230)
XLA Ops:
  0.6 1.0 %copy-done.7 = f32[1,256,384]{2,1,0:T(8,128)S(1)} copy-done((f32[1,256,384]{2,1,0:T(8,128)S(1)}, f32[1,256,384]{2,1,0:T(8,128)}, u32[]{:S(2)}) %copy-start.7) | copy-done | bytes 393240
  1.7 5.8 %collective-permute-start = (bf16[64,384]{1,0:T(8,128)(2,1)S(1)}, bf16[64,384]{1,0:T(8,128)(2,1)S(1)}, u32[]{:S(2)}, u32[]{:S(2)}) collective-permute-start(bf16[64,384]{1,0:T(8,128)(2,1)S(1)} %get-tuple-element.35), channel_id=1, source_target_pairs={{1,2},{2,1},{3,4},{4,3},{5,6},{6,5},{7,8},{8,7},{9,10},{10,9},{11,... | collective-permute-start | bytes 147464 | tf_op jit(solution)/shard_map/ppermute | solution.py:434
  7.5 1.9 %collective-permute-start.1 = (bf16[64,384]{1,0:T(8,128)(2,1)S(1)}, bf16[64,384]{1,0:T(8,128)(2,1)S(1)}, u32[]{:S(2)}, u32[]{:S(2)}) collective-permute-start(bf16[64,384]{1,0:T(8,128)(2,1)S(1)} %get-tuple-element.36), channel_id=1, source_target_pairs={{0,1},{1,0},{2,3},{3,2},{4,5},{5,4},{6,7},{7,6},{8,9},{9,8},{10,11... | collective-permute-start | bytes 147464 | tf_op jit(solution)/shard_map/ppermute | solution.py:434
  9.4 0.7 %first.1 = (s32[24,128]{1,0:T(8,128)S(1)}, f32[392,384]{1,0:T(8,128)S(1)}, f32[392,384]{1,0:T(8,128)S(1)}) custom-call(s32[2,67]{1,0:T(2,128)S(1)} %bitcast.5, f32[1,256,384]{2,1,0:T(8,128)S(1)} %copy-done.8), custom_call_target="tpu_custom_call" | custom-call | flops 536870912 | bytes 1048576 | tf_op jit(solution)/shard_map/first/pallas_call | solution.py:379
  10.1 3.4 %collective-permute-done.1.outer = bf16[64,384]{1,0:T(8,128)(2,1)S(1)} collective-permute-done((bf16[64,384]{1,0:T(8,128)(2,1)S(1)}, bf16[64,384]{1,0:T(8,128)(2,1)S(1)}, u32[]{:S(2)}, u32[]{:S(2)}) %collective-permute-start.1) | collective-permute-done | bytes 49184 | tf_op jit(solution)/shard_map/ppermute | solution.py:434
  13.5 0.3 share.1
  13.7 2.1 %collective-permute-start.2 = (bf16[2112,256]{1,0:T(8,128)(2,1)S(1)}, bf16[2112,256]{1,0:T(8,128)(2,1)S(1)}, u32[]{:S(2)}, u32[]{:S(2)}) collective-permute-start(bf16[2112,256]{1,0:T(8,128)(2,1)S(1)} %get-tuple-element.41), channel_id=1, source_target_pairs={{0,16},{16,0},{32,48},{48,32},{64,80},{80,64},{96,112},{112,96},{1... | collective-permute-start | bytes 3244040 | tf_op jit(solution)/shard_map/ppermute | solution.py:421
  15.9 1.2 %step0.1 = (bf16[2,256,256]{2,1,0:T(8,128)(2,1)S(1)}, f32[392,384]{1,0:T(8,128)S(1)}) custom-call(s32[24,128]{1,0:T(8,128)S(1)} %get-tuple-element.34.corners, bf16[1,1,4,2,256,256]{5,4,3,2,1,0:T(8,128)(2,1)S(1)} %copy-done, bf16[1,4,256,256]{3,2,1,0:T(8,128)(2,1)S(1)} %copy-done.2, bf16[5,256,256]{2,1,0:T(8,128)(2,1)S(1)} %copy-done.1, ...), custom_call_target="tpu_custom_call" | custom-call | flops 536870912 | bytes 1048576 | tf_op jit(solution)/shard_map/step0/pallas_call | solution.py:379
  17.0 3.1 %collective-permute-start.3 = (bf16[2,256,256]{2,1,0:T(8,128)(2,1)S(1)}, bf16[2,256,256]{2,1,0:T(8,128)(2,1)S(1)}, u32[]{:S(2)}, u32[]{:S(2)}) collective-permute-start(bf16[2,256,256]{2,1,0:T(8,128)(2,1)S(1)} %get-tuple-element.45), channel_id=1, source_target_pairs={{0,0},{496,496},{16,32},{32,16},{48,64},{64,48},{80,96},{96,80},{1... | collective-permute-start | bytes 786440 | tf_op jit(solution)/shard_map/ppermute | solution.py:401
  20.2 2.9 %steps01.1 = (bf16[2,256,256]{2,1,0:T(8,128)(2,1)S(1)}, f32[392,384]{1,0:T(8,128)S(1)}, f32[392,384]{1,0:T(8,128)S(1)}, f32[392,384]{1,0:T(8,128)S(1)}, f32[392,384]{1,0:T(8,128)S(1)}) custom-call(s32[24,128]{1,0:T(8,128)S(1)} %get-tuple-element.34.corners, bf16[1,1,4,2,256,256]{5,4,3,2,1,0:T(8,128)(2,1)S(1)} %copy-done, ...), custom_call_target="tpu_custom_call", output_to_operand_aliasing={{1}: (10, {})} | custom-call | flops 1073741824 | bytes 1048576 | tf_op jit(solution)/shard_map/steps01/pallas_call | solution.py:379
  23.1 6.4 %collective-permute-start.5 = (bf16[2,256,256]{2,1,0:T(8,128)(2,1)S(1)}, bf16[2,256,256]{2,1,0:T(8,128)(2,1)S(1)}, u32[]{:S(2)}, u32[]{:S(2)}) collective-permute-start(bf16[2,256,256]{2,1,0:T(8,128)(2,1)S(1)} %get-tuple-element.49), channel_id=1, source_target_pairs={{480,496},{16,0},{0,32},{48,16},{32,64},{80,48},{64,96},{112,80},{... | collective-permute-start | bytes 786440 | tf_op jit(solution)/shard_map/ppermute | solution.py:409
  29.6 2.1 %steps12.1 = (bf16[2,256,256]{2,1,0:T(8,128)(2,1)S(1)}, f32[392,384]{1,0:T(8,128)S(1)}, f32[392,384]{1,0:T(8,128)S(1)}) custom-call(s32[24,128]{1,0:T(8,128)S(1)} %get-tuple-element.34.corners, bf16[1,1,4,2,256,256]{5,4,3,2,1,0:T(8,128)(2,1)S(1)} %copy-done, bf16[1,4,256,256]{3,2,1,0:T(8,128)(2,1)S(1)} %copy-done.2, ...), custom_call_target="tpu_custom_call", output_to_operand_aliasing={{1}: (12, {}), {2}: (13, {})} | custom-call | flops 1073741824 | bytes 1048576 | tf_op jit(solution)/shard_map/steps12/pallas_call | solution.py:379
  31.6 5.6 %collective-permute-start.4 = (bf16[2,256,256]{2,1,0:T(8,128)(2,1)S(1)}, bf16[2,256,256]{2,1,0:T(8,128)(2,1)S(1)}, u32[]{:S(2)}, u32[]{:S(2)}) collective-permute-start(bf16[2,256,256]{2,1,0:T(8,128)(2,1)S(1)} %get-tuple-element.48), channel_id=1, source_target_pairs={{480,480},{16,16},{0,48},{48,0},{32,80},{80,32},{64,112},{112,64},... | collective-permute-start | bytes 786440 | tf_op jit(solution)/shard_map/ppermute | solution.py:417
  37.3 2.2 %steps23.1 = (bf16[2,256,256]{2,1,0:T(8,128)(2,1)S(1)}, f32[392,384]{1,0:T(8,128)S(1)}, f32[392,384]{1,0:T(8,128)S(1)}) custom-call(s32[24,128]{1,0:T(8,128)S(1)} %get-tuple-element.34.corners, bf16[1,1,4,2,256,256]{5,4,3,2,1,0:T(8,128)(2,1)S(1)} %copy-done, bf16[1,4,256,256]{3,2,1,0:T(8,128)(2,1)S(1)} %copy-done.2, ...), custom_call_target="tpu_custom_call", output_to_operand_aliasing={{1}: (12, {}), {2}: (13, {})} | custom-call | flops 1073741824 | bytes 1048576 | tf_op jit(solution)/shard_map/steps23/pallas_call | solution.py:379
  39.5 4.3 %collective-permute-start.6 = (bf16[2,256,256]{2,1,0:T(8,128)(2,1)S(1)}, bf16[2,256,256]{2,1,0:T(8,128)(2,1)S(1)}, u32[]{:S(2)}, u32[]{:S(2)}) collective-permute-start(bf16[2,256,256]{2,1,0:T(8,128)(2,1)S(1)} %get-tuple-element.56), channel_id=1, source_target_pairs={{480,496},{16,0},{0,32},{48,16},{32,64},{80,48},{64,96},{112,80},{... | collective-permute-start | bytes 786440 | tf_op jit(solution)/shard_map/ppermute | solution.py:409
  43.8 1.2 %step3.1 = (bf16[2,256,256]{2,1,0:T(8,128)(2,1)S(1)}, f32[392,384]{1,0:T(8,128)S(1)}, bf16[576,256]{1,0:T(8,128)(2,1)S(1)}) custom-call(s32[24,128]{1,0:T(8,128)S(1)} %get-tuple-element.34.corners, bf16[1,4,256,256]{3,2,1,0:T(8,128)(2,1)S(1)} %copy-done.2, bf16[5,256,256]{2,1,0:T(8,128)(2,1)S(1)} %copy-done.1, ...), custom_call_target="tpu_custom_call", output_to_operand_aliasing={{1}: (9, {})} | custom-call | flops 536870912 | bytes 1048576 | tf_op jit(solution)/shard_map/step3/pallas_call | solution.py:379
  44.9 2.2 %all-gather = bf16[1152,256]{1,0:T(8,128)(2,1)S(1)} all-gather(bf16[576,256]{1,0:T(8,128)(2,1)S(1)} %get-tuple-element.53), channel_id=2, replica_groups={{0,16},{32,48},{64,80},{96,112},{128,144},{160,176},{192,208},{224,240}..., dimensions={0}, use_global_device_ids=true | all-gather | bytes 884736 | tf_op jit(solution)/shard_map/all_gather | solution.py:427
  47.2 0.1 sum.1
  47.3 2.6 %collective-permute-start.7 = (bf16[64,384]{1,0:T(8,128)(2,1)S(1)}, bf16[64,384]{1,0:T(8,128)(2,1)S(1)}, u32[]{:S(2)}, u32[]{:S(2)}) collective-permute-start(bf16[64,384]{1,0:T(8,128)(2,1)S(1)} %get-tuple-element.63), channel_id=1, source_target_pairs={{1,2},{2,1},{3,4},{4,3},{5,6},{6,5},{7,8},{8,7},{9,10},{10,9},{11,... | collective-permute-start | bytes 147464 | tf_op jit(solution)/shard_map/ppermute | solution.py:434
  49.8 3.0 %collective-permute-start.8 = (bf16[64,384]{1,0:T(8,128)(2,1)S(1)}, bf16[64,384]{1,0:T(8,128)(2,1)S(1)}, u32[]{:S(2)}, u32[]{:S(2)}) collective-permute-start(bf16[64,384]{1,0:T(8,128)(2,1)S(1)} %get-tuple-element.64), channel_id=1, source_target_pairs={{0,1},{1,0},{2,3},{3,2},{4,5},{5,4},{6,7},{7,6},{8,9},{9,8},{10,11... | collective-permute-start | bytes 147464 | tf_op jit(solution)/shard_map/ppermute | solution.py:434
  52.9 1.0 %waves.1 = (f32[1,1,2,256,256]{4,3,2,1,0:T(8,128)}, bf16[1,1,2,256,256]{4,3,2,1,0:T(8,128)(2,1)}) custom-call(bf16[2,256,256]{2,1,0:T(8,128)(2,1)S(1)} %collective-permute-done.6.swapped, bf16[2,256,256]{2,1,0:T(8,128)(2,1)S(1)} %get-tuple-element.57.stayed, bf16[2,256,256]{2,1,0:T(8,128)(2,1)S(1)} %copy-done.4), custom_call_target="tpu_custom_call" | custom-call | tf_op jit(solution)/shard_map/waves/pallas_call | solution.py:379
  53.8 1.5 %collective-permute-done.7.inner = bf16[64,384]{1,0:T(8,128)(2,1)S(1)} collective-permute-done((bf16[64,384]{1,0:T(8,128)(2,1)S(1)}, bf16[64,384]{1,0:T(8,128)(2,1)S(1)}, u32[]{:S(2)}, u32[]{:S(2)}) %collective-permute-start.7) | collective-permute-done | bytes 49184 | tf_op jit(solution)/shard_map/ppermute | solution.py:434
  55.3 0.5 collective-permute-done.8.outer
  55.8 0.8 %fold.1 = f32[1,256,384]{2,1,0:T(8,128)} custom-call(f32[392,384]{1,0:T(8,128)S(1)} %get-tuple-element.62.acc, bf16[64,384]{1,0:T(8,128)(2,1)S(1)} %collective-permute-done.7.inner, bf16[64,384]{1,0:T(8,128)(2,1)S(1)} %collective-permute-done.8.outer), custom_call_target="tpu_custom_call" | custom-call | tf_op jit(solution)/shard_map/fold/pallas_call | solution.py:379
  (26 shorter events, 0.1 us)
Async XLA Ops:
  0.6 1.0 %copy-start.7 = (f32[1,256,384]{2,1,0:T(8,128)S(1)}, f32[1,256,384]{2,1,0:T(8,128)}, u32[]{:S(2)}) copy-start(f32[1,256,384]{2,1,0:T(8,128)} %pot.5) | copy-start | bytes 1179652
  1.6 7.8 %copy-start.8 = (f32[1,256,384]{2,1,0:T(8,128)S(1)}, f32[1,256,384]{2,1,0:T(8,128)}, u32[]{:S(2)}) copy-start(f32[1,256,384]{2,1,0:T(8,128)} %pot.5) | copy-start | bytes 1179652
  1.6 7.8 %copy-start.9 = (s32[1,67,2]{1,2,0:T(2,128)S(1)}, s32[1,67,2]{1,2,0:T(2,128)}, u32[]{:S(2)}) copy-start(s32[1,67,2]{1,2,0:T(2,128)} %param.11) | copy-start | bytes 1612
  1.7 11.8 %copy-start = (bf16[1,1,4,2,256,256]{5,4,3,2,1,0:T(8,128)(2,1)S(1)}, bf16[1,1,4,2,256,256]{5,4,3,2,1,0:T(8,128)(2,1)}, u32[]{:S(2)}) copy-start(bf16[1,1,4,2,256,256]{5,4,3,2,1,0:T(8,128)(2,1)} %saved.9) | copy-start | bytes 3145732
  1.7 8.4 %collective-permute-start = (bf16[64,384]{1,0:T(8,128)(2,1)S(1)}, bf16[64,384]{1,0:T(8,128)(2,1)S(1)}, u32[]{:S(2)}, u32[]{:S(2)}) collective-permute-start(bf16[64,384]{1,0:T(8,128)(2,1)S(1)} %get-tuple-element.35), channel_id=1, source_target_pairs={{1,2},{2,1},{3,4},{4,3},{5,6},{6,5},{7,8},{8,7},{9,10},{10,9},{11,... | collective-permute-start | bytes 147464 | tf_op jit(solution)/shard_map/ppermute | solution.py:434
  7.5 6.0 %collective-permute-start.1 = (bf16[64,384]{1,0:T(8,128)(2,1)S(1)}, bf16[64,384]{1,0:T(8,128)(2,1)S(1)}, u32[]{:S(2)}, u32[]{:S(2)}) collective-permute-start(bf16[64,384]{1,0:T(8,128)(2,1)S(1)} %get-tuple-element.36), channel_id=1, source_target_pairs={{0,1},{1,0},{2,3},{3,2},{4,5},{5,4},{6,7},{7,6},{8,9},{9,8},{10,11... | collective-permute-start | bytes 147464 | tf_op jit(solution)/shard_map/ppermute | solution.py:434
  13.4 2.4 %copy-start.1 = (bf16[5,256,256]{2,1,0:T(8,128)(2,1)S(1)}, bf16[5,256,256]{2,1,0:T(8,128)(2,1)}, u32[]{:S(2)}) copy-start(bf16[5,256,256]{2,1,0:T(8,128)(2,1)} %constant.4.clone.tables) | copy-start | bytes 1966084
  13.4 2.4 %copy-start.2 = (bf16[1,4,256,256]{3,2,1,0:T(8,128)(2,1)S(1)}, bf16[1,4,256,256]{3,2,1,0:T(8,128)(2,1)}, u32[]{:S(2)}) copy-start(bf16[1,4,256,256]{3,2,1,0:T(8,128)(2,1)} %intens.9) | copy-start | bytes 1572868
  13.4 2.4 %copy-start.3 = (f32[2,256,256]{2,1,0:T(8,128)S(1)}, f32[2,256,256]{2,1,0:T(8,128)}, u32[]{:S(2)}) copy-start(f32[2,256,256]{2,1,0:T(8,128)} %constant.5.clone.prop) | copy-start | bytes 1572868
  13.4 2.4 %copy-start.5 = (f32[1,1,2,256,256]{4,3,2,1,0:T(8,128)S(1)}, f32[1,1,2,256,256]{4,3,2,1,0:T(8,128)}, u32[]{:S(2)}) copy-start(f32[1,1,2,256,256]{4,3,2,1,0:T(8,128)} %refs_0_.1) | copy-start | bytes 1572868
  13.5 2.4 %copy-start.6 = (bf16[1,1,2,256,256]{4,3,2,1,0:T(8,128)(2,1)S(1)}, bf16[1,1,2,256,256]{4,3,2,1,0:T(8,128)(2,1)}, u32[]{:S(2)}) copy-start(bf16[1,1,2,256,256]{4,3,2,1,0:T(8,128)(2,1)} %refs_1_.3) | copy-start | bytes 786436
  13.7 6.4 %collective-permute-start.2 = (bf16[2112,256]{1,0:T(8,128)(2,1)S(1)}, bf16[2112,256]{1,0:T(8,128)(2,1)S(1)}, u32[]{:S(2)}, u32[]{:S(2)}) collective-permute-start(bf16[2112,256]{1,0:T(8,128)(2,1)S(1)} %get-tuple-element.41), channel_id=1, source_target_pairs={{0,16},{16,0},{32,48},{48,32},{64,80},{80,64},{96,112},{112,96},{1... | collective-permute-start | bytes 3244040 | tf_op jit(solution)/shard_map/ppermute | solution.py:421
  17.0 12.5 %collective-permute-start.3 = (bf16[2,256,256]{2,1,0:T(8,128)(2,1)S(1)}, bf16[2,256,256]{2,1,0:T(8,128)(2,1)S(1)}, u32[]{:S(2)}, u32[]{:S(2)}) collective-permute-start(bf16[2,256,256]{2,1,0:T(8,128)(2,1)S(1)} %get-tuple-element.45), channel_id=1, source_target_pairs={{0,0},{496,496},{16,32},{32,16},{48,64},{64,48},{80,96},{96,80},{1... | collective-permute-start | bytes 786440 | tf_op jit(solution)/shard_map/ppermute | solution.py:401
  20.2 9.4 %copy-start.4 = (bf16[2,256,256]{2,1,0:T(8,128)(2,1)S(1)}, bf16[2,256,256]{2,1,0:T(8,128)(2,1)}, u32[]{:S(2)}) copy-start(bf16[2,256,256]{2,1,0:T(8,128)(2,1)} %probe.3) | copy-start | bytes 786436
  23.1 14.2 %collective-permute-start.5 = (bf16[2,256,256]{2,1,0:T(8,128)(2,1)S(1)}, bf16[2,256,256]{2,1,0:T(8,128)(2,1)S(1)}, u32[]{:S(2)}, u32[]{:S(2)}) collective-permute-start(bf16[2,256,256]{2,1,0:T(8,128)(2,1)S(1)} %get-tuple-element.49), channel_id=1, source_target_pairs={{480,496},{16,0},{0,32},{48,16},{32,64},{80,48},{64,96},{112,80},{... | collective-permute-start | bytes 786440 | tf_op jit(solution)/shard_map/ppermute | solution.py:409
  31.6 12.1 %collective-permute-start.4 = (bf16[2,256,256]{2,1,0:T(8,128)(2,1)S(1)}, bf16[2,256,256]{2,1,0:T(8,128)(2,1)S(1)}, u32[]{:S(2)}, u32[]{:S(2)}) collective-permute-start(bf16[2,256,256]{2,1,0:T(8,128)(2,1)S(1)} %get-tuple-element.48), channel_id=1, source_target_pairs={{480,480},{16,16},{0,48},{48,0},{32,80},{80,32},{64,112},{112,64},... | collective-permute-start | bytes 786440 | tf_op jit(solution)/shard_map/ppermute | solution.py:417
  39.5 13.3 %collective-permute-start.6 = (bf16[2,256,256]{2,1,0:T(8,128)(2,1)S(1)}, bf16[2,256,256]{2,1,0:T(8,128)(2,1)S(1)}, u32[]{:S(2)}, u32[]{:S(2)}) collective-permute-start(bf16[2,256,256]{2,1,0:T(8,128)(2,1)S(1)} %get-tuple-element.56), channel_id=1, source_target_pairs={{480,496},{16,0},{0,32},{48,16},{32,64},{80,48},{64,96},{112,80},{... | collective-permute-start | bytes 786440 | tf_op jit(solution)/shard_map/ppermute | solution.py:409
  47.3 8.1 %collective-permute-start.7 = (bf16[64,384]{1,0:T(8,128)(2,1)S(1)}, bf16[64,384]{1,0:T(8,128)(2,1)S(1)}, u32[]{:S(2)}, u32[]{:S(2)}) collective-permute-start(bf16[64,384]{1,0:T(8,128)(2,1)S(1)} %get-tuple-element.63), channel_id=1, source_target_pairs={{1,2},{2,1},{3,4},{4,3},{5,6},{6,5},{7,8},{8,7},{9,10},{10,9},{11,... | collective-permute-start | bytes 147464 | tf_op jit(solution)/shard_map/ppermute | solution.py:434
  49.8 6.0 %collective-permute-start.8 = (bf16[64,384]{1,0:T(8,128)(2,1)S(1)}, bf16[64,384]{1,0:T(8,128)(2,1)S(1)}, u32[]{:S(2)}, u32[]{:S(2)}) collective-permute-start(bf16[64,384]{1,0:T(8,128)(2,1)S(1)} %get-tuple-element.64), channel_id=1, source_target_pairs={{0,1},{1,0},{2,3},{3,2},{4,5},{5,4},{6,7},{7,6},{8,9},{9,8},{10,11... | collective-permute-start | bytes 147464 | tf_op jit(solution)/shard_map/ppermute | solution.py:434

commit v5 on v4

--- a/solution.py
+++ b/solution.py
@@ -205,9 +205,10 @@
     )
 
 
-def share_kernel(inner, outer, pot, saved, tr0, ti0, tr, ti, shared):
+def share_kernel(inner, outer, saved, tr0, ti0, tr, ti, shared):
     margin = inner.shape[0]
-    core = pot.shape[1]
+    rows = tr.shape[0] - SUB
+    core = rows - 2 * margin
     low = jnp.where(odd_tile(), outer[...], inner[...])
     high = jnp.where(odd_tile(), inner[...], outer[...])
     transmit(low.astype(F32), tr, ti, slice(0, margin))
@@ -217,8 +218,9 @@
         for part in range(2):
             at = (2 * (tick - 1) + part) * n
             shared[at : at + n] = saved[0, 0, tick, part]
-    whole = jnp.concatenate([low, pot[0].astype(BF16), high], axis=0)
-    pack(shared, 2 * (TICKS - 1) * n, whole)
+    at = 2 * (TICKS - 1) * n
+    pack(shared, at, tr[:rows])
+    pack(shared, at + rows * 3 // 2, ti[:rows])
 
 
 def forward_step(xr, xi, section, tick, spot, tr, ti, intens, tables, prop, far):
@@ -310,10 +312,11 @@
     spot, mate_spot = corner(corners, own(tick)), corner(corners, mates(tick + 1))
     if fresh:
         rows = mate_tr.shape[0] - SUB
-        for where_rows, where_columns, v in unpack(rows, shared[2 * (TICKS - 1) * n :]):
-            s, c = sin_cos(SIGMA * v.astype(F32))
-            mate_tr[where_rows, where_columns] = c
-            mate_ti[where_rows, where_columns] = s
+        at = 2 * (TICKS - 1) * n
+        for target in (mate_tr, mate_ti):
+            for where_rows, where_columns, t in unpack(rows, shared[at : at + rows * 3 // 2]):
+                target[where_rows, where_columns] = t.astype(F32)
+            at += rows * 3 // 2
         mate_acc[...] = jnp.zeros(mate_acc.shape, F32)
 
     @pl.when(even)
@@ -458,8 +461,8 @@
     )
     packed = (tall - SUB) * 3 // 2
     tr, ti, shared = call(
-        share_kernel, "share", [extent] * 2 + [shape(2 * (TICKS - 1) * n + packed, n, dtype=BF16)],
-        (inner, outer, potential, saved_wave, tr, ti), {4: 0, 5: 1},
+        share_kernel, "share", [extent] * 2 + [shape(2 * (TICKS - 1) * n + 2 * packed, n, dtype=BF16)],
+        (inner, outer, saved_wave, tr, ti), {3: 0, 4: 1},
     )
     shared = swap_cores(shared)
     common = (corners, saved_wave, intensity, tables, prop, tr, ti)

time: 57 us -> 56.8 us (level)
  the two profiles are of different devices: /device:TPU:198 before, /device:TPU:202 now
where the time goes in v5:
time: 56.8 us; the launch traced here: 56.4 us
  starting transfers between devices  36.1 us (64%)
  Pallas kernels  11.6 us (20%)
  waiting for transfers between devices  4.57 us (8%)
  blocking collectives  2.23 us (4%)
  local copies, waits for them, and re-layouts  1.04 us (2%)
  between operations  0.93 us (2%)
    ppermute x4, starting transfers between devices, swap_tiles(): return lax.ppermute(x, 'tile', route)  14.4 us
    pallas_call x11, Pallas kernels, call(): pl.pallas_call(kernel, name=name, in_specs=[VM] * len(args), out_specs=[V...  11.6 us
    ppermute x2, starting transfers between devices, ring(): return lax.ppermute(x, 'depth', route)  10.7 us
    ppermute x1, starting transfers between devices, cross(): return lax.ppermute(x, 'depth', route)  5.57 us
    ppermute x4, waiting for transfers between devices, swap_tiles(): return lax.ppermute(x, 'tile', route)  4.01 us
    ppermute x1, starting transfers between devices, swap_chips(): return lax.ppermute(x, 'depth', route)  3.54 us
    all_gather x1, blocking collectives, gather_chip(): return lax.all_gather(x, 'depth', axis_index_groups=groups)  2.23 us
    ppermute x1, starting transfers between devices, swap_cores(): lax.ppermute(x, 'depth', [(i, i ^ 1) for i in range(lax.axis_size('depth'...  1.92 us
  transfers between devices with their start and end apart: 9, of which 3 were waited for; matrix products, arithmetic and copies ran while one was open for 0% of the time, Pallas kernels for 18%

profile of v5, /device:TPU:202, one launch (start us, length us, event | category | flops | bytes accessed | tf_op | source)
XLA Modules:
  0.0 56.4 jit_solution(13042342058963920300)
XLA Ops:
  0.6 1.0 %copy-done.7 = f32[1,256,384]{2,1,0:T(8,128)S(1)} copy-done((f32[1,256,384]{2,1,0:T(8,128)S(1)}, f32[1,256,384]{2,1,0:T(8,128)}, u32[]{:S(2)}) %copy-start.7) | copy-done | bytes 393240
  1.7 3.6 %collective-permute-start = (bf16[64,384]{1,0:T(8,128)(2,1)S(1)}, bf16[64,384]{1,0:T(8,128)(2,1)S(1)}, u32[]{:S(2)}, u32[]{:S(2)}) collective-permute-start(bf16[64,384]{1,0:T(8,128)(2,1)S(1)} %get-tuple-element.35), channel_id=1, source_target_pairs={{1,2},{2,1},{3,4},{4,3},{5,6},{6,5},{7,8},{8,7},{9,10},{10,9},{11,... | collective-permute-start | bytes 147464 | tf_op jit(solution)/shard_map/ppermute | solution.py:437
  5.3 4.2 %collective-permute-start.1 = (bf16[64,384]{1,0:T(8,128)(2,1)S(1)}, bf16[64,384]{1,0:T(8,128)(2,1)S(1)}, u32[]{:S(2)}, u32[]{:S(2)}) collective-permute-start(bf16[64,384]{1,0:T(8,128)(2,1)S(1)} %get-tuple-element.36), channel_id=1, source_target_pairs={{0,1},{1,0},{2,3},{3,2},{4,5},{5,4},{6,7},{7,6},{8,9},{9,8},{10,11... | collective-permute-start | bytes 147464 | tf_op jit(solution)/shard_map/ppermute | solution.py:437
  9.6 0.7 %first.1 = (s32[24,128]{1,0:T(8,128)S(1)}, f32[392,384]{1,0:T(8,128)S(1)}, f32[392,384]{1,0:T(8,128)S(1)}) custom-call(s32[2,67]{1,0:T(2,128)S(1)} %bitcast.5, f32[1,256,384]{2,1,0:T(8,128)S(1)} %copy-done.8), custom_call_target="tpu_custom_call" | custom-call | flops 536870912 | bytes 1048576 | tf_op jit(solution)/shard_map/first/pallas_call | solution.py:382
  10.3 1.3 %collective-permute-done.1.outer = bf16[64,384]{1,0:T(8,128)(2,1)S(1)} collective-permute-done((bf16[64,384]{1,0:T(8,128)(2,1)S(1)}, bf16[64,384]{1,0:T(8,128)(2,1)S(1)}, u32[]{:S(2)}, u32[]{:S(2)}) %collective-permute-start.1) | collective-permute-done | bytes 49184 | tf_op jit(solution)/shard_map/ppermute | solution.py:437
  11.6 0.3 share.1
  11.9 1.9 %collective-permute-start.2 = (bf16[2688,256]{1,0:T(8,128)(2,1)S(1)}, bf16[2688,256]{1,0:T(8,128)(2,1)S(1)}, u32[]{:S(2)}, u32[]{:S(2)}) collective-permute-start(bf16[2688,256]{1,0:T(8,128)(2,1)S(1)} %get-tuple-element.41), channel_id=1, source_target_pairs={{0,16},{16,0},{32,48},{48,32},{64,80},{80,64},{96,112},{112,96},{1... | collective-permute-start | bytes 4128776 | tf_op jit(solution)/shard_map/ppermute | solution.py:424
  13.9 1.2 %step0.1 = (bf16[2,256,256]{2,1,0:T(8,128)(2,1)S(1)}, f32[392,384]{1,0:T(8,128)S(1)}) custom-call(s32[24,128]{1,0:T(8,128)S(1)} %get-tuple-element.34.corners, bf16[1,1,4,2,256,256]{5,4,3,2,1,0:T(8,128)(2,1)S(1)} %copy-done, bf16[1,4,256,256]{3,2,1,0:T(8,128)(2,1)S(1)} %copy-done.2, bf16[5,256,256]{2,1,0:T(8,128)(2,1)S(1)} %copy-done.1, ...), custom_call_target="tpu_custom_call" | custom-call | flops 536870912 | bytes 1048576 | tf_op jit(solution)/shard_map/step0/pallas_call | solution.py:382
  15.1 3.5 %collective-permute-start.3 = (bf16[2,256,256]{2,1,0:T(8,128)(2,1)S(1)}, bf16[2,256,256]{2,1,0:T(8,128)(2,1)S(1)}, u32[]{:S(2)}, u32[]{:S(2)}) collective-permute-start(bf16[2,256,256]{2,1,0:T(8,128)(2,1)S(1)} %get-tuple-element.45), channel_id=1, source_target_pairs={{0,0},{496,496},{16,32},{32,16},{48,64},{64,48},{80,96},{96,80},{1... | collective-permute-start | bytes 786440 | tf_op jit(solution)/shard_map/ppermute | solution.py:404
  18.6 2.1 %steps01.1 = (bf16[2,256,256]{2,1,0:T(8,128)(2,1)S(1)}, f32[392,384]{1,0:T(8,128)S(1)}, f32[392,384]{1,0:T(8,128)S(1)}, f32[392,384]{1,0:T(8,128)S(1)}, f32[392,384]{1,0:T(8,128)S(1)}) custom-call(s32[24,128]{1,0:T(8,128)S(1)} %get-tuple-element.34.corners, bf16[1,1,4,2,256,256]{5,4,3,2,1,0:T(8,128)(2,1)S(1)} %copy-done, ...), custom_call_target="tpu_custom_call", output_to_operand_aliasing={{1}: (10, {})} | custom-call | flops 1073741824 | bytes 1048576 | tf_op jit(solution)/shard_map/steps01/pallas_call | solution.py:382
  20.8 3.9 %collective-permute-start.5 = (bf16[2,256,256]{2,1,0:T(8,128)(2,1)S(1)}, bf16[2,256,256]{2,1,0:T(8,128)(2,1)S(1)}, u32[]{:S(2)}, u32[]{:S(2)}) collective-permute-start(bf16[2,256,256]{2,1,0:T(8,128)(2,1)S(1)} %get-tuple-element.49), channel_id=1, source_target_pairs={{480,496},{16,0},{0,32},{48,16},{32,64},{80,48},{64,96},{112,80},{... | collective-permute-start | bytes 786440 | tf_op jit(solution)/shard_map/ppermute | solution.py:412
  24.7 0.5 collective-permute-done.3.refs_0_
  25.3 2.0 %steps12.1 = (bf16[2,256,256]{2,1,0:T(8,128)(2,1)S(1)}, f32[392,384]{1,0:T(8,128)S(1)}, f32[392,384]{1,0:T(8,128)S(1)}) custom-call(s32[24,128]{1,0:T(8,128)S(1)} %get-tuple-element.34.corners, bf16[1,1,4,2,256,256]{5,4,3,2,1,0:T(8,128)(2,1)S(1)} %copy-done, bf16[1,4,256,256]{3,2,1,0:T(8,128)(2,1)S(1)} %copy-done.2, ...), custom_call_target="tpu_custom_call", output_to_operand_aliasing={{1}: (12, {}), {2}: (13, {})} | custom-call | flops 1073741824 | bytes 1048576 | tf_op jit(solution)/shard_map/steps12/pallas_call | solution.py:382
  27.3 5.6 %collective-permute-start.4 = (bf16[2,256,256]{2,1,0:T(8,128)(2,1)S(1)}, bf16[2,256,256]{2,1,0:T(8,128)(2,1)S(1)}, u32[]{:S(2)}, u32[]{:S(2)}) collective-permute-start(bf16[2,256,256]{2,1,0:T(8,128)(2,1)S(1)} %get-tuple-element.48), channel_id=1, source_target_pairs={{480,480},{16,16},{0,48},{48,0},{32,80},{80,32},{64,112},{112,64},... | collective-permute-start | bytes 786440 | tf_op jit(solution)/shard_map/ppermute | solution.py:420
  32.9 2.2 %steps23.1 = (bf16[2,256,256]{2,1,0:T(8,128)(2,1)S(1)}, f32[392,384]{1,0:T(8,128)S(1)}, f32[392,384]{1,0:T(8,128)S(1)}) custom-call(s32[24,128]{1,0:T(8,128)S(1)} %get-tuple-element.34.corners, bf16[1,1,4,2,256,256]{5,4,3,2,1,0:T(8,128)(2,1)S(1)} %copy-done, bf16[1,4,256,256]{3,2,1,0:T(8,128)(2,1)S(1)} %copy-done.2, ...), custom_call_target="tpu_custom_call", output_to_operand_aliasing={{1}: (12, {}), {2}: (13, {})} | custom-call | flops 1073741824 | bytes 1048576 | tf_op jit(solution)/shard_map/steps23/pallas_call | solution.py:382
  35.1 6.8 %collective-permute-start.6 = (bf16[2,256,256]{2,1,0:T(8,128)(2,1)S(1)}, bf16[2,256,256]{2,1,0:T(8,128)(2,1)S(1)}, u32[]{:S(2)}, u32[]{:S(2)}) collective-permute-start(bf16[2,256,256]{2,1,0:T(8,128)(2,1)S(1)} %get-tuple-element.56), channel_id=1, source_target_pairs={{480,496},{16,0},{0,32},{48,16},{32,64},{80,48},{64,96},{112,80},{... | collective-permute-start | bytes 786440 | tf_op jit(solution)/shard_map/ppermute | solution.py:412
  41.9 1.2 %step3.1 = (bf16[2,256,256]{2,1,0:T(8,128)(2,1)S(1)}, f32[392,384]{1,0:T(8,128)S(1)}, bf16[576,256]{1,0:T(8,128)(2,1)S(1)}) custom-call(s32[24,128]{1,0:T(8,128)S(1)} %get-tuple-element.34.corners, bf16[1,4,256,256]{3,2,1,0:T(8,128)(2,1)S(1)} %copy-done.2, bf16[5,256,256]{2,1,0:T(8,128)(2,1)S(1)} %copy-done.1, ...), custom_call_target="tpu_custom_call", output_to_operand_aliasing={{1}: (9, {})} | custom-call | flops 536870912 | bytes 1048576 | tf_op jit(solution)/shard_map/step3/pallas_call | solution.py:382
  43.1 2.2 %all-gather = bf16[1152,256]{1,0:T(8,128)(2,1)S(1)} all-gather(bf16[576,256]{1,0:T(8,128)(2,1)S(1)} %get-tuple-element.53), channel_id=2, replica_groups={{0,16},{32,48},{64,80},{96,112},{128,144},{160,176},{192,208},{224,240}..., dimensions={0}, use_global_device_ids=true | all-gather | bytes 884736 | tf_op jit(solution)/shard_map/all_gather | solution.py:430
  45.3 0.1 sum.1
  45.4 4.2 %collective-permute-start.7 = (bf16[64,384]{1,0:T(8,128)(2,1)S(1)}, bf16[64,384]{1,0:T(8,128)(2,1)S(1)}, u32[]{:S(2)}, u32[]{:S(2)}) collective-permute-start(bf16[64,384]{1,0:T(8,128)(2,1)S(1)} %get-tuple-element.63), channel_id=1, source_target_pairs={{1,2},{2,1},{3,4},{4,3},{5,6},{6,5},{7,8},{8,7},{9,10},{10,9},{11,... | collective-permute-start | bytes 147464 | tf_op jit(solution)/shard_map/ppermute | solution.py:437
  49.6 2.3 %collective-permute-start.8 = (bf16[64,384]{1,0:T(8,128)(2,1)S(1)}, bf16[64,384]{1,0:T(8,128)(2,1)S(1)}, u32[]{:S(2)}, u32[]{:S(2)}) collective-permute-start(bf16[64,384]{1,0:T(8,128)(2,1)S(1)} %get-tuple-element.64), channel_id=1, source_target_pairs={{0,1},{1,0},{2,3},{3,2},{4,5},{5,4},{6,7},{7,6},{8,9},{9,8},{10,11... | collective-permute-start | bytes 147464 | tf_op jit(solution)/shard_map/ppermute | solution.py:437
  51.9 1.0 %waves.1 = (f32[1,1,2,256,256]{4,3,2,1,0:T(8,128)}, bf16[1,1,2,256,256]{4,3,2,1,0:T(8,128)(2,1)}) custom-call(bf16[2,256,256]{2,1,0:T(8,128)(2,1)S(1)} %collective-permute-done.6.swapped, bf16[2,256,256]{2,1,0:T(8,128)(2,1)S(1)} %get-tuple-element.57.stayed, bf16[2,256,256]{2,1,0:T(8,128)(2,1)S(1)} %copy-done.4), custom_call_target="tpu_custom_call" | custom-call | tf_op jit(solution)/shard_map/waves/pallas_call | solution.py:382
  52.9 2.7 %collective-permute-done.8.outer = bf16[64,384]{1,0:T(8,128)(2,1)S(1)} collective-permute-done((bf16[64,384]{1,0:T(8,128)(2,1)S(1)}, bf16[64,384]{1,0:T(8,128)(2,1)S(1)}, u32[]{:S(2)}, u32[]{:S(2)}) %collective-permute-start.8) | collective-permute-done | bytes 49184 | tf_op jit(solution)/shard_map/ppermute | solution.py:437
  55.6 0.8 %fold.1 = f32[1,256,384]{2,1,0:T(8,128)} custom-call(f32[392,384]{1,0:T(8,128)S(1)} %get-tuple-element.62.acc, bf16[64,384]{1,0:T(8,128)(2,1)S(1)} %collective-permute-done.7.inner, bf16[64,384]{1,0:T(8,128)(2,1)S(1)} %collective-permute-done.8.outer), custom_call_target="tpu_custom_call" | custom-call | tf_op jit(solution)/shard_map/fold/pallas_call | solution.py:382
  (26 shorter events, 0.1 us)
Async XLA Ops:
  0.6 1.0 %copy-start.7 = (f32[1,256,384]{2,1,0:T(8,128)S(1)}, f32[1,256,384]{2,1,0:T(8,128)}, u32[]{:S(2)}) copy-start(f32[1,256,384]{2,1,0:T(8,128)} %pot.3) | copy-start | bytes 1179652
  1.6 7.9 %copy-start.8 = (f32[1,256,384]{2,1,0:T(8,128)S(1)}, f32[1,256,384]{2,1,0:T(8,128)}, u32[]{:S(2)}) copy-start(f32[1,256,384]{2,1,0:T(8,128)} %pot.3) | copy-start | bytes 1179652
  1.6 7.9 %copy-start.9 = (s32[1,67,2]{1,2,0:T(2,128)S(1)}, s32[1,67,2]{1,2,0:T(2,128)}, u32[]{:S(2)}) copy-start(s32[1,67,2]{1,2,0:T(2,128)} %param.11) | copy-start | bytes 1612
  1.7 9.9 %copy-start = (bf16[1,1,4,2,256,256]{5,4,3,2,1,0:T(8,128)(2,1)S(1)}, bf16[1,1,4,2,256,256]{5,4,3,2,1,0:T(8,128)(2,1)}, u32[]{:S(2)}) copy-start(bf16[1,1,4,2,256,256]{5,4,3,2,1,0:T(8,128)(2,1)} %saved.9) | copy-start | bytes 3145732
  1.7 8.6 %collective-permute-start = (bf16[64,384]{1,0:T(8,128)(2,1)S(1)}, bf16[64,384]{1,0:T(8,128)(2,1)S(1)}, u32[]{:S(2)}, u32[]{:S(2)}) collective-permute-start(bf16[64,384]{1,0:T(8,128)(2,1)S(1)} %get-tuple-element.35), channel_id=1, source_target_pairs={{1,2},{2,1},{3,4},{4,3},{5,6},{6,5},{7,8},{8,7},{9,10},{10,9},{11,... | collective-permute-start | bytes 147464 | tf_op jit(solution)/shard_map/ppermute | solution.py:437
  5.3 6.3 %collective-permute-start.1 = (bf16[64,384]{1,0:T(8,128)(2,1)S(1)}, bf16[64,384]{1,0:T(8,128)(2,1)S(1)}, u32[]{:S(2)}, u32[]{:S(2)}) collective-permute-start(bf16[64,384]{1,0:T(8,128)(2,1)S(1)} %get-tuple-element.36), channel_id=1, source_target_pairs={{0,1},{1,0},{2,3},{3,2},{4,5},{5,4},{6,7},{7,6},{8,9},{9,8},{10,11... | collective-permute-start | bytes 147464 | tf_op jit(solution)/shard_map/ppermute | solution.py:437
  9.5 4.3 %copy-start.6 = (bf16[1,1,2,256,256]{4,3,2,1,0:T(8,128)(2,1)S(1)}, bf16[1,1,2,256,256]{4,3,2,1,0:T(8,128)(2,1)}, u32[]{:S(2)}) copy-start(bf16[1,1,2,256,256]{4,3,2,1,0:T(8,128)(2,1)} %refs_1_.3) | copy-start | bytes 786436
  10.2 3.6 %copy-start.1 = (bf16[5,256,256]{2,1,0:T(8,128)(2,1)S(1)}, bf16[5,256,256]{2,1,0:T(8,128)(2,1)}, u32[]{:S(2)}) copy-start(bf16[5,256,256]{2,1,0:T(8,128)(2,1)} %constant.4.clone.tables) | copy-start | bytes 1966084
  10.2 3.6 %copy-start.2 = (bf16[1,4,256,256]{3,2,1,0:T(8,128)(2,1)S(1)}, bf16[1,4,256,256]{3,2,1,0:T(8,128)(2,1)}, u32[]{:S(2)}) copy-start(bf16[1,4,256,256]{3,2,1,0:T(8,128)(2,1)} %intens.9) | copy-start | bytes 1572868
  10.2 3.6 %copy-start.3 = (f32[2,256,256]{2,1,0:T(8,128)S(1)}, f32[2,256,256]{2,1,0:T(8,128)}, u32[]{:S(2)}) copy-start(f32[2,256,256]{2,1,0:T(8,128)} %constant.5.clone.prop) | copy-start | bytes 1572868
  10.3 3.6 %copy-start.5 = (f32[1,1,2,256,256]{4,3,2,1,0:T(8,128)S(1)}, f32[1,1,2,256,256]{4,3,2,1,0:T(8,128)}, u32[]{:S(2)}) copy-start(f32[1,1,2,256,256]{4,3,2,1,0:T(8,128)} %refs_0_.1) | copy-start | bytes 1572868
  11.9 6.7 %collective-permute-start.2 = (bf16[2688,256]{1,0:T(8,128)(2,1)S(1)}, bf16[2688,256]{1,0:T(8,128)(2,1)S(1)}, u32[]{:S(2)}, u32[]{:S(2)}) collective-permute-start(bf16[2688,256]{1,0:T(8,128)(2,1)S(1)} %get-tuple-element.41), channel_id=1, source_target_pairs={{0,16},{16,0},{32,48},{48,32},{64,80},{80,64},{96,112},{112,96},{1... | collective-permute-start | bytes 4128776 | tf_op jit(solution)/shard_map/ppermute | solution.py:424
  15.1 10.2 %collective-permute-start.3 = (bf16[2,256,256]{2,1,0:T(8,128)(2,1)S(1)}, bf16[2,256,256]{2,1,0:T(8,128)(2,1)S(1)}, u32[]{:S(2)}, u32[]{:S(2)}) collective-permute-start(bf16[2,256,256]{2,1,0:T(8,128)(2,1)S(1)} %get-tuple-element.45), channel_id=1, source_target_pairs={{0,0},{496,496},{16,32},{32,16},{48,64},{64,48},{80,96},{96,80},{1... | collective-permute-start | bytes 786440 | tf_op jit(solution)/shard_map/ppermute | solution.py:404
  18.6 6.6 %copy-start.4 = (bf16[2,256,256]{2,1,0:T(8,128)(2,1)S(1)}, bf16[2,256,256]{2,1,0:T(8,128)(2,1)}, u32[]{:S(2)}) copy-start(bf16[2,256,256]{2,1,0:T(8,128)(2,1)} %probe.3) | copy-start | bytes 786436
  20.8 12.1 %collective-permute-start.5 = (bf16[2,256,256]{2,1,0:T(8,128)(2,1)S(1)}, bf16[2,256,256]{2,1,0:T(8,128)(2,1)S(1)}, u32[]{:S(2)}, u32[]{:S(2)}) collective-permute-start(bf16[2,256,256]{2,1,0:T(8,128)(2,1)S(1)} %get-tuple-element.49), channel_id=1, source_target_pairs={{480,496},{16,0},{0,32},{48,16},{32,64},{80,48},{64,96},{112,80},{... | collective-permute-start | bytes 786440 | tf_op jit(solution)/shard_map/ppermute | solution.py:412
  27.3 14.6 %collective-permute-start.4 = (bf16[2,256,256]{2,1,0:T(8,128)(2,1)S(1)}, bf16[2,256,256]{2,1,0:T(8,128)(2,1)S(1)}, u32[]{:S(2)}, u32[]{:S(2)}) collective-permute-start(bf16[2,256,256]{2,1,0:T(8,128)(2,1)S(1)} %get-tuple-element.48), channel_id=1, source_target_pairs={{480,480},{16,16},{0,48},{48,0},{32,80},{80,32},{64,112},{112,64},... | collective-permute-start | bytes 786440 | tf_op jit(solution)/shard_map/ppermute | solution.py:420
  35.1 16.8 %collective-permute-start.6 = (bf16[2,256,256]{2,1,0:T(8,128)(2,1)S(1)}, bf16[2,256,256]{2,1,0:T(8,128)(2,1)S(1)}, u32[]{:S(2)}, u32[]{:S(2)}) collective-permute-start(bf16[2,256,256]{2,1,0:T(8,128)(2,1)S(1)} %get-tuple-element.56), channel_id=1, source_target_pairs={{480,496},{16,0},{0,32},{48,16},{32,64},{80,48},{64,96},{112,80},{... | collective-permute-start | bytes 786440 | tf_op jit(solution)/shard_map/ppermute | solution.py:412
  45.4 7.5 %collective-permute-start.7 = (bf16[64,384]{1,0:T(8,128)(2,1)S(1)}, bf16[64,384]{1,0:T(8,128)(2,1)S(1)}, u32[]{:S(2)}, u32[]{:S(2)}) collective-permute-start(bf16[64,384]{1,0:T(8,128)(2,1)S(1)} %get-tuple-element.63), channel_id=1, source_target_pairs={{1,2},{2,1},{3,4},{4,3},{5,6},{6,5},{7,8},{8,7},{9,10},{10,9},{11,... | collective-permute-start | bytes 147464 | tf_op jit(solution)/shard_map/ppermute | solution.py:437
  49.6 6.0 %collective-permute-start.8 = (bf16[64,384]{1,0:T(8,128)(2,1)S(1)}, bf16[64,384]{1,0:T(8,128)(2,1)S(1)}, u32[]{:S(2)}, u32[]{:S(2)}) collective-permute-start(bf16[64,384]{1,0:T(8,128)(2,1)S(1)} %get-tuple-element.64), channel_id=1, source_target_pairs={{0,1},{1,0},{2,3},{3,2},{4,5},{5,4},{6,7},{7,6},{8,9},{9,8},{10,11... | collective-permute-start | bytes 147464 | tf_op jit(solution)/shard_map/ppermute | solution.py:437
